TPU v7x, 32 devices: a whole 2x2x4 slice. The times are simulated.
32 devices in a mesh: river: 4 (over x, core), hours: 8 (over z, y).
Axes of the slice: x: 2, y: 2, z: 4, core: 2. Of those that a mesh axis runs over, the one named last changes fastest.
Arguments:
- release: float32 [40, 128, 512], P('river', 'hours'), may hold values from 0 to 1
- storage_dual: float32 [40, 128, 512], P('river', 'hours'), may hold values from -3 to 3
- demand_dual: float32 [128, 512], P('hours'), may hold values from -1 to 0
- cost: float32 [40, 128, 512], P('river', 'hours'), may hold values from -1.8 to 1.8
- inflow: float32 [40, 128, 512], P('river', 'hours'), may hold values from 0 to 1.2
- demand: float32 [128, 512], P('hours'), may hold values from 2.2135944 to 4.110961
- storage_start: float32 [40], P('river'), may hold values from -0.5 to 0.5
- storage_low: float32 [40], P('river'), may hold values from -2 to -0.5
- storage_high: float32 [40], P('river'), may hold values from 0.5 to 2
- release_cap: float32 [40], P('river'), may hold values from 0.5 to 1.5
- efficiency: float32 [40], P('river'), may hold values from 0.5 to 1.5
- downstream: int32 [40], P('river'), may hold values from -1 to 39, as said below
- travel_delay: int32 [40], P('river'), may hold values from 1 to 6
Outputs:
- release_new: float32 [40, 128, 512], P('river', 'hours')
- storage_dual_new: float32 [40, 128, 512], P('river', 'hours')
- demand_dual_new: float32 [128, 512], P('hours')
- storage_excess: float32 [40, 128, 512], P('river', 'hours')
Inputs may be any that keep to these rules, and one draw needn't show every extreme that they name: Each reservoir's downstream index is -1 or lies 1 to 10 positions after its own index.
All inputs are finite; a program needn't handle non-finite values.
Results may differ from a plain program's by a relative error of at most 0.00013.
Values sent between devices are 32-bit elements; how exact they have to be, the bound alone decides.
No kernel may reach another device: no remote copies, remote signals or barrier semaphores. Data moves between devices by JAX's collectives and lax.ppermute only.
A program may use at most 64 MiB of HBM per device.

v0:
```python
import math

import jax
import jax.numpy as jnp
from jax import lax
from jax.sharding import PartitionSpec as P

DMAX = 6


primal_step = 1.0
dual_step = 0.1


def passed_along(block, axis, distance):
    devices = range(lax.axis_size(axis))
    route = [(i - distance, i) for i in devices if i - distance in devices]
    return lax.ppermute(block, axis, route)


def prefix(part, axis, combine, identity, reverse):
    count = lax.axis_size(axis)
    place = lax.axis_index(axis)
    ahead = count - 1 - place if reverse else place
    gathered = lax.all_gather(part, axis)
    state = jnp.zeros_like(part) + jnp.asarray(identity, part.dtype)

    def one(turn, state):
        source = count - 1 - turn if reverse else turn
        return combine(state, lax.dynamic_index_in_dim(gathered, source, 0, False))

    return lax.fori_loop(0, ahead, one, state)


def add_pair(earlier_part, later_part):
    return earlier_part + later_part


def hold_back(field, travel_delay, earlier_rim):
    length = field.shape[1]
    extended = jnp.concatenate([earlier_rim, field], 1)
    result = jnp.zeros_like(field)
    for lag_hours in range(1, DMAX + 1):
        window = extended[:, DMAX - lag_hours : DMAX - lag_hours + length]
        result = result + jnp.where((travel_delay == lag_hours)[:, None, None], window, 0.0)
    return result


def bring_forward(field, travel_delay, later_rim):
    length = field.shape[1]
    extended = jnp.concatenate([field, later_rim], 1)
    result = jnp.zeros_like(field)
    for lag_hours in range(1, DMAX + 1):
        window = extended[:, lag_hours : lag_hours + length]
        result = result + jnp.where((travel_delay == lag_hours)[:, None, None], window, 0.0)
    return result


def route_down(matrix, field):
    return jnp.einsum("ij,jtw->itw", matrix, field, precision=lax.Precision.HIGHEST)


def route_up(matrix, field):
    return jnp.einsum("ij,itw->jtw", matrix, field, precision=lax.Precision.HIGHEST)


def iterate(fields, statics, scales, prefix_sum, suffix_sum, from_earlier, from_later):
    release, storage_dual, demand_dual, cost, inflow, demand = fields
    (
        storage_start,
        storage_low,
        storage_high,
        release_cap,
        efficiency,
        travel_delay,
        to_own,
        to_next,
    ) = statics
    scale_time, scale_sum = scales
    suffix = suffix_sum(storage_dual)
    beyond = passed_along(suffix, "river", -1)
    at_sink = route_up(to_own, suffix) + route_up(to_next, beyond)
    later_duals = bring_forward(at_sink, travel_delay, from_later(at_sink[:, :DMAX]))
    gradient = (
        cost
        + scale_time * (later_duals - suffix)
        + scale_sum * efficiency[:, None, None] * demand_dual[None]
    )
    release_new = jnp.clip(release - primal_step * gradient, 0.0, release_cap[:, None, None])
    extrapolated = 2.0 * release_new - release
    length = extrapolated.shape[1]
    delayed = hold_back(extrapolated, travel_delay, from_earlier(extrapolated[:, length - DMAX :]))
    incoming = passed_along(route_down(to_next, delayed), "river", 1)
    routed = route_down(to_own, delayed) + incoming
    storage = storage_start[:, None, None] + scale_time * prefix_sum(inflow + routed - extrapolated)
    lower_bound = storage_low[:, None, None]
    upper_bound = storage_high[:, None, None]
    storage_dual_new = (
        storage_dual
        + dual_step * storage
        - dual_step * jnp.clip(storage_dual / dual_step + storage, lower_bound, upper_bound)
    )
    storage_excess = storage - jnp.clip(storage, lower_bound, upper_bound)
    partial_power = jnp.sum(scale_sum * efficiency[:, None, None] * extrapolated, 0)
    supplied = lax.psum(partial_power, "river")
    demand_dual_new = jnp.minimum(demand_dual + dual_step * (supplied - demand), 0.0)
    return (release_new, storage_dual_new, demand_dual_new, storage_excess)


def suffix_local(field):
    return jnp.flip(jnp.cumsum(jnp.flip(field, 1), 1), 1)


def shards(
    release,
    storage_dual,
    demand_dual,
    cost,
    inflow,
    demand,
    storage_start,
    storage_low,
    storage_high,
    release_cap,
    efficiency,
    downstream,
    travel_delay,
):
    res_dev = release.shape[0]
    scale_time = 1.0 / (release.shape[1] * lax.axis_size("hours"))
    scale_sum = 1.0 / math.sqrt(res_dev * lax.axis_size("river"))
    base_index = lax.axis_index("river") * res_dev
    target = downstream - base_index
    indices = jnp.arange(res_dev, dtype=jnp.int32)
    to_own = (target[None, :] == indices[:, None]).astype(jnp.float32)
    to_next = (target[None, :] == indices[:, None] + res_dev).astype(jnp.float32)
    statics = (
        storage_start,
        storage_low,
        storage_high,
        release_cap,
        efficiency,
        travel_delay,
        to_own,
        to_next,
    )
    scales = (scale_time, scale_sum)

    def prefix_blocks(field):
        local_sum = jnp.cumsum(field, 1)
        totals = local_sum[:, -1]
        offset = prefix(totals, "hours", add_pair, jnp.zeros_like(totals), False)
        return local_sum + offset[:, None]

    def suffix_blocks(field):
        local_sum = suffix_local(field)
        totals = local_sum[:, 0]
        offset = prefix(totals, "hours", add_pair, jnp.zeros_like(totals), True)
        return local_sum + offset[:, None]

    def earlier_block(part):
        return passed_along(part, "hours", 1)

    def later_block(part):
        return passed_along(part, "hours", -1)

    fields = (release, storage_dual, demand_dual, cost, inflow, demand)
    return iterate(
        fields, statics, scales, prefix_blocks, suffix_blocks, earlier_block, later_block
    )


def solution(mesh):
    return jax.shard_map(
        shards,
        mesh=mesh,
        in_specs=(
            P("river", "hours", None),
            P("river", "hours", None),
            P("hours", None),
            P("river", "hours", None),
            P("river", "hours", None),
            P("hours", None),
            P("river"),
            P("river"),
            P("river"),
            P("river"),
            P("river"),
            P("river"),
            P("river"),
        ),
        out_specs=(
            P("river", "hours", None),
            P("river", "hours", None),
            P("hours", None),
            P("river", "hours", None),
        ),
        check_vma=False,
    )
```

profile of v0, /device:TPU:0, one launch (start us, length us, event | category | flops | bytes accessed | tf_op | source)
XLA Modules:
  0.0 116.3 jit_solution(13543634953635832184)
XLA Ops:
  0.6 1.8 %rev.7 = f32[10,16,512]{2,1,0:T(8,128)S(1)} reverse(f32[10,16,512]{2,1,0:T(8,128)} %param.18), dimensions={1} | reverse | bytes 655360 | tf_op jit(solution)/shard_map/jit(_flip)/rev | solution.py:111
  2.9 32.4 %all-gather = f32[80,1,512]{2,1,0:T(1,128)S(1)} all-gather(f32[10,1,512]{2,1,0:T(1,128)S(1)} %copy.42), channel_id=2, replica_groups=mesh['river'=4,'hours'=8] {'hours'}, dimensions={0}, use_global_device_ids=true | all-gather | bytes 184320 | tf_op jit(solution)/shard_map/all_gather | solution.py:25
  36.0 1.3 %collective-permute-start = (f32[10,16,512]{2,0,1:T(8,128)S(1)}, f32[10,16,512]{2,0,1:T(8,128)S(1)}, u32[]{:S(2)}, u32[]{:S(2)}) collective-permute-start(f32[10,16,512]{2,0,1:T(8,128)S(1)} %reverse_add_fusion), channel_id=1, source_target_pairs={{8,0},{16,8},{24,16},{9,1},{17,9},{25,17},{10,2},{18,10},{26,18},{... | collective-permute-start | bytes 983048 | tf_op jit(solution)/shard_map/ppermute | solution.py:18
  37.4 0.6 copy-done.7
  38.0 0.6 copy-done.8
  38.7 0.4 fusion.49
  39.1 0.7 collective-permute-done
  39.8 0.5 convolution_add_fusion.1
  40.4 1.4 %collective-permute-start.1 = (f32[10,6,512]{2,0,1:T(8,128)S(1)}, f32[10,6,512]{2,0,1:T(8,128)S(1)}, u32[]{:S(2)}, u32[]{:S(2)}) collective-permute-start(f32[10,6,512]{2,0,1:T(8,128)S(1)} %slice.66), channel_id=1, source_target_pairs={{1,0},{2,1},{3,2},{4,3},{5,4},{6,5},{7,6},{9,8},{10,9},{11,10},{12... | collective-permute-start | bytes 368648 | tf_op jit(solution)/shard_map/ppermute | solution.py:18
  41.9 6.2 %collective-permute-done.1 = f32[10,6,512]{2,0,1:T(8,128)S(1)} collective-permute-done((f32[10,6,512]{2,0,1:T(8,128)S(1)}, f32[10,6,512]{2,0,1:T(8,128)S(1)}, u32[]{:S(2)}, u32[]{:S(2)}) %collective-permute-start.1) | collective-permute-done | bytes 122912 | tf_op jit(solution)/shard_map/ppermute | solution.py:18
  48.1 0.6 copy-done.6
  48.8 0.8 multiply_reduce_fusion
  49.5 4.3 %collective-permute-start.2 = (f32[10,6,512]{2,0,1:T(8,128)S(1)}, f32[10,6,512]{2,0,1:T(8,128)S(1)}, u32[]{:S(2)}, u32[]{:S(2)}) collective-permute-start(f32[10,6,512]{2,0,1:T(8,128)S(1)} %slice.77), channel_id=1, source_target_pairs={{0,1},{1,2},{2,3},{3,4},{4,5},{5,6},{6,7},{8,9},{9,10},{10,11},{11... | collective-permute-start | bytes 368648 | tf_op jit(solution)/shard_map/ppermute | solution.py:18
  53.9 3.2 %collective-permute-done.2 = f32[10,6,512]{2,0,1:T(8,128)S(1)} collective-permute-done((f32[10,6,512]{2,0,1:T(8,128)S(1)}, f32[10,6,512]{2,0,1:T(8,128)S(1)}, u32[]{:S(2)}, u32[]{:S(2)}) %collective-permute-start.2) | collective-permute-done | bytes 122912 | tf_op jit(solution)/shard_map/ppermute | solution.py:18
  57.7 6.5 %collective-permute-start.3 = (f32[10,16,512]{2,0,1:T(8,128)S(1)}, f32[10,16,512]{2,0,1:T(8,128)S(1)}, u32[]{:S(2)}, u32[]{:S(2)}) collective-permute-start(f32[10,16,512]{2,0,1:T(8,128)S(1)} %fusion.51), channel_id=1, source_target_pairs={{0,8},{8,16},{16,24},{1,9},{9,17},{17,25},{2,10},{10,18},{18,26},{... | collective-permute-start | bytes 983048 | tf_op jit(solution)/shard_map/ppermute | solution.py:18
  64.3 0.9 copy.52
  65.2 13.0 %psum.7 = f32[16,512]{1,0:T(8,128)S(1)} all-reduce(f32[16,512]{1,0:T(8,128)S(1)} %get-tuple-element.113), channel_id=1, replica_groups=mesh['river'=4,'hours'=8] {'river'}, use_global_device_ids=true, to_apply=%region_7.8 | all-reduce | flops 8192 | bytes 65536 | tf_op jit(solution)/shard_map/psum | solution.py:105
  78.2 0.6 add_minimum_fusion
  78.8 0.5 fusion.1
  79.3 2.7 %fusion.63 = f32[10,16,512]{2,0,1:T(8,128)S(1)} fusion(f32[10,16,512]{2,0,1:T(8,128)S(1)} %fusion.1), kind=kOutput, calls=%fused_computation.105 | output fusion | flops 1228800 | bytes 655360 | tf_op jit(solution)/shard_map/jit(cumsum)/reduce_window_sum | solution.py:150
  82.1 30.6 %all-gather.1 = f32[80,1,512]{2,1,0:T(1,128)S(1)} all-gather(f32[10,1,512]{2,1,0:T(1,128)S(1)} %copy.49), channel_id=3, replica_groups=mesh['river'=4,'hours'=8] {'hours'}, dimensions={0}, use_global_device_ids=true | all-gather | bytes 184320 | tf_op jit(solution)/shard_map/all_gather | solution.py:25
  113.2 0.9 copy-done
  114.4 0.9 copy.53
  115.3 0.9 copy.54
  (52 shorter events, 2.8 us)
Async XLA Ops:
  36.0 3.8 %collective-permute-start = (f32[10,16,512]{2,0,1:T(8,128)S(1)}, f32[10,16,512]{2,0,1:T(8,128)S(1)}, u32[]{:S(2)}, u32[]{:S(2)}) collective-permute-start(f32[10,16,512]{2,0,1:T(8,128)S(1)} %reverse_add_fusion), channel_id=1, source_target_pairs={{8,0},{16,8},{24,16},{9,1},{17,9},{25,17},{10,2},{18,10},{26,18},{... | collective-permute-start | bytes 983048 | tf_op jit(solution)/shard_map/ppermute | solution.py:18
  37.3 0.7 copy-start.7
  38.0 0.7 copy-start.8
  39.8 8.3 %copy-start.3 = (f32[10,16,512]{2,1,0:T(8,128)S(1)}, f32[10,16,512]{2,1,0:T(8,128)}, u32[]{:S(2)}) copy-start(f32[10,16,512]{2,1,0:T(8,128)} %param.20) | copy-start | bytes 983044
  40.3 1.5 %copy-start.12 = (f32[10]{0:T(128)S(1)}, f32[10]{0:T(128)}, u32[]{:S(2)}) copy-start(f32[10]{0:T(128)} %param.27) | copy-start | bytes 124
  40.4 7.7 %copy-start.2 = (f32[10,16,512]{2,1,0:T(8,128)S(1)}, f32[10,16,512]{2,1,0:T(8,128)}, u32[]{:S(2)}) copy-start(f32[10,16,512]{2,1,0:T(8,128)} %param.17) | copy-start | bytes 983044
  40.4 7.7 %copy-start.4 = (f32[16,512]{1,0:T(8,128)S(1)}, f32[16,512]{1,0:T(8,128)}, u32[]{:S(2)}) copy-start(f32[16,512]{1,0:T(8,128)} %param.19) | copy-start | bytes 98308
  40.4 7.7 %collective-permute-start.1 = (f32[10,6,512]{2,0,1:T(8,128)S(1)}, f32[10,6,512]{2,0,1:T(8,128)S(1)}, u32[]{:S(2)}, u32[]{:S(2)}) collective-permute-start(f32[10,6,512]{2,0,1:T(8,128)S(1)} %slice.66), channel_id=1, source_target_pairs={{1,0},{2,1},{3,2},{4,3},{5,4},{6,5},{7,6},{9,8},{10,9},{11,10},{12... | collective-permute-start | bytes 368648 | tf_op jit(solution)/shard_map/ppermute | solution.py:18
  48.1 0.7 copy-start.6
  49.5 7.5 %collective-permute-start.2 = (f32[10,6,512]{2,0,1:T(8,128)S(1)}, f32[10,6,512]{2,0,1:T(8,128)S(1)}, u32[]{:S(2)}, u32[]{:S(2)}) collective-permute-start(f32[10,6,512]{2,0,1:T(8,128)S(1)} %slice.77), channel_id=1, source_target_pairs={{0,1},{1,2},{2,3},{3,4},{4,5},{5,6},{6,7},{8,9},{9,10},{10,11},{11... | collective-permute-start | bytes 368648 | tf_op jit(solution)/shard_map/ppermute | solution.py:18
  57.7 21.1 %collective-permute-start.3 = (f32[10,16,512]{2,0,1:T(8,128)S(1)}, f32[10,16,512]{2,0,1:T(8,128)S(1)}, u32[]{:S(2)}, u32[]{:S(2)}) collective-permute-start(f32[10,16,512]{2,0,1:T(8,128)S(1)} %fusion.51), channel_id=1, source_target_pairs={{0,8},{8,16},{16,24},{1,9},{9,17},{17,25},{2,10},{10,18},{18,26},{... | collective-permute-start | bytes 983048 | tf_op jit(solution)/shard_map/ppermute | solution.py:18
  64.2 14.6 %copy-start.1 = (f32[10,16,512]{2,1,0:T(8,128)S(1)}, f32[10,16,512]{2,1,0:T(8,128)}, u32[]{:S(2)}) copy-start(f32[10,16,512]{2,1,0:T(8,128)} %param.21) | copy-start | bytes 983044
  65.2 13.0 %copy-start.5 = (f32[16,512]{1,0:T(8,128)S(1)}, f32[16,512]{1,0:T(8,128)}, u32[]{:S(2)}) copy-start(f32[16,512]{1,0:T(8,128)} %param.22) | copy-start | bytes 98308
  113.1 1.0 copy-start
  113.1 0.9 copy-start.9
  113.1 0.9 copy-start.10
  113.2 0.9 copy-start.11
where the time goes:
time: 117 us; the launch traced here: 116 us
  blocking collectives  75.9 us (65%)
  starting transfers between devices  13.6 us (12%)
  waiting for transfers between devices  10.2 us (9%)
  local copies, waits for them, and re-layouts  7.6 us (6%)
  other arithmetic  6.01 us (5%)
  matrix products  1.84 us (2%)
    all_gather x2, blocking collectives, prefix(): gathered = lax.all_gather(part, axis)  62.9 us
    ppermute x4, starting transfers between devices, passed_along(): return lax.ppermute(block, axis, route)  13.6 us
    psum x1, blocking collectives, iterate(): supplied = lax.psum(partial_power, 'river')  13 us
    ppermute x4, waiting for transfers between devices, passed_along(): return lax.ppermute(block, axis, route)  10.2 us
    unnamed x29, local copies, waits for them, and re-layouts  5.62 us
    another operation x1, other arithmetic, prefix_blocks(): local_sum = jnp.cumsum(field, 1)  2.71 us
  transfers between devices with their start and end apart: 4, of which 3 were waited for; matrix products, arithmetic and copies ran while one was open for 2% of the time, Pallas kernels for 0%

commit v1 on v0

v1 whole, which is shorter than its diff:
```python
import functools
import math

import jax
import jax.numpy as jnp
from jax import lax
from jax.experimental import pallas as pl
from jax.experimental.pallas import tpu as pltpu
from jax.sharding import PartitionSpec as P

DMAX = 6
RIM = 8

primal_step = 1.0
dual_step = 0.1


def scan_rows(block, reverse):
    rows, lanes = block.shape
    place = lax.broadcasted_iota(jnp.int32, (8, lanes), 0)
    tiles = [block[k : k + 8] for k in range(0, rows, 8)]
    order = range(len(tiles) - 1, -1, -1) if reverse else range(len(tiles))
    carry = None
    for k in order:
        tile = tiles[k]
        for step in (1, 2, 4):
            moved = pltpu.roll(tile, 8 - step if reverse else step, 0)
            keep = place < 8 - step if reverse else place >= step
            tile = tile + jnp.where(keep, moved, 0.0)
        if carry is not None:
            tile = tile + carry
        tiles[k] = tile
        carry = tile[0:1] if reverse else tile[7:8]
    return jnp.concatenate(tiles, 0), carry


def sink_of(down_ref, j, count):
    down = down_ref[j]
    base = lax.axis_index("river") * count
    return jnp.where(down < 0, 2 * count, down - base)


def turned(tiles, amount):
    return [pltpu.roll(tile, amount, 0) for tile in tiles]


def totals_kernel(sd_ref, total_ref):
    for i in range(sd_ref.shape[0]):
        total_ref[i : i + 1] = jnp.sum(sd_ref[i], 0, keepdims=True)


def ahead_kernel(scale_time, scale_sum, down_ref, delay_ref, eff_ref, sd_ref, next_ref, rel_ref, cost_ref, dual_ref, q_ref, w_ref, sums_ref):
    count, hours, lanes = sd_ref.shape
    for i in range(2 * count):
        ref, k = (sd_ref, i) if i < count else (next_ref, i - count)
        sums_ref[i] = scan_rows(ref[k], True)[0]
    sums_ref[2 * count] = jnp.zeros((hours, lanes), jnp.float32)
    dual = dual_ref[...]
    place = lax.broadcasted_iota(jnp.int32, (RIM, lanes), 0)
    for j in range(count):
        lag = delay_ref[j]
        sink = sums_ref[sink_of(down_ref, j, count)]
        inside = place < RIM - lag
        tiles = turned([sink[k : k + RIM] for k in range(0, hours, RIM)], RIM - lag)
        w_ref[j] = jnp.where(inside, 0.0, tiles[0] - sink[0:1])
        tiles.append(jnp.zeros((RIM, lanes), jnp.float32))
        later = jnp.concatenate([jnp.where(inside, tiles[k], tiles[k + 1]) for k in range(hours // RIM)], 0)
        gradient = cost_ref[j] + scale_time * (later - sums_ref[j]) + scale_sum * eff_ref[j] * dual
        q_ref[j] = rel_ref[j] - primal_step * gradient


def release_kernel(scale_time, scale_sum, down_ref, delay_ref, eff_ref, cap_ref, q_ref, w_ref, own_ref, next_ref, rel_ref, inflow_ref, new_ref, own_out, next_out, tot_own, tot_next, power_ref, acc, tot):
    count, hours, lanes = q_ref.shape
    for i in range(count):
        tot[i] = own_ref[i : i + 1]
        tot[count + i] = next_ref[i : i + 1]
    tot[2 * count] = jnp.zeros((1, lanes), jnp.float32)
    lags = [delay_ref[j] for j in range(count)]
    sinks = [sink_of(down_ref, j, count) for j in range(count)]
    shifts = [tot[sinks[j]] - tot[j] for j in range(count)]
    acc[...] = jnp.zeros_like(acc)
    tot[...] = jnp.zeros_like(tot)
    power = jnp.zeros((hours, lanes), jnp.float32)
    place = lax.broadcasted_iota(jnp.int32, (RIM, lanes), 0)
    zeros = jnp.zeros((RIM, lanes), jnp.float32)
    for j in range(count):
        later = jnp.concatenate([jnp.zeros((hours - RIM, lanes), jnp.float32), w_ref[j]], 0) + shifts[j]
        release = rel_ref[j]
        new = jnp.clip(q_ref[j] - (primal_step * scale_time) * later, 0.0, cap_ref[j])
        new_ref[j] = new
        extra = 2.0 * new - release
        power = power + (scale_sum * eff_ref[j]) * extra
        sums, total = scan_rows(extra, False)
        arrived = place >= lags[j]
        tiles = [zeros] + turned([sums[k : k + RIM] for k in range(0, hours, RIM)], lags[j])
        window = [jnp.where(arrived, tiles[k + 1], tiles[k]) for k in range(hours // RIM)]
        window.append(jnp.where(arrived, 0.0, tiles[-1] - total))
        acc[sinks[j]] = acc[sinks[j]] + jnp.concatenate(window, 0)
        tot[sinks[j]] = tot[sinks[j]] + total
        local, change = scan_rows(inflow_ref[j] - extra, False)
        acc[j, 0:hours] = acc[j, 0:hours] + local
        tot[j] = tot[j] + change
    own_out[...] = acc[0:count]
    next_out[...] = acc[count : 2 * count]
    for i in range(count):
        tot_own[i : i + 1] = tot[i]
        tot_next[i : i + 1] = tot[count + i]
    power_ref[...] = power


def storage_kernel(scale_time, start_ref, low_ref, high_ref, mine_ref, came_ref, rim_ref, off_ref, sd_ref, power_ref, dual_ref, demand_ref, sd_out, excess_out, dual_out):
    count, hours, lanes = sd_ref.shape
    for i in range(count):
        change = mine_ref[i, 0:hours] + came_ref[i, 0:hours] + off_ref[i : i + 1]
        rim = jnp.concatenate([rim_ref[i], jnp.zeros((hours - RIM, lanes), jnp.float32)], 0)
        storage = start_ref[i] + scale_time * (change + rim)
        low, high = low_ref[i], high_ref[i]
        dual = sd_ref[i]
        sd_out[i] = dual + dual_step * storage - dual_step * jnp.clip(dual / dual_step + storage, low, high)
        excess_out[i] = storage - jnp.clip(storage, low, high)
    dual_out[...] = jnp.minimum(dual_ref[...] + dual_step * (power_ref[...] - demand_ref[...]), 0.0)


def passed_along(block, axis, distance):
    devices = range(lax.axis_size(axis))
    route = [(i - distance, i) for i in devices if i - distance in devices]
    return lax.ppermute(block, axis, route)


def swapped(block, axis, bit):
    return lax.ppermute(block, axis, [(i, i ^ bit) for i in range(lax.axis_size(axis))])


def offsets(total, axis, reverse):
    count, place = lax.axis_size(axis), lax.axis_index(axis)
    result = jnp.zeros_like(total)
    bit = 1
    while bit < count:
        other = swapped(total, axis, bit)
        low = (place & bit) == 0
        result = result + jnp.where(low if reverse else ~low, other, 0.0)
        total = total + other
        bit *= 2
    return result


def all_summed(part, axis):
    count = lax.axis_size(axis)
    bit = 1
    while bit < count:
        part = part + swapped(part, axis, bit)
        bit *= 2
    return part


SMEM = pl.BlockSpec(memory_space=pltpu.SMEM)
VMEM = pl.BlockSpec(memory_space=pltpu.VMEM)


def call(body, smem, vmem, shapes, scratch):
    return pl.pallas_call(
        body,
        out_shape=[jax.ShapeDtypeStruct(s, jnp.float32) for s in shapes],
        in_specs=[SMEM] * len(smem) + [VMEM] * len(vmem),
        out_specs=[VMEM] * len(shapes),
        scratch_shapes=[pltpu.VMEM(s, jnp.float32) for s in scratch],
        compiler_params=pltpu.CompilerParams(vmem_limit_bytes=32 * 1024 * 1024),
    )(*smem, *vmem)


def shards(
    release,
    storage_dual,
    demand_dual,
    cost,
    inflow,
    demand,
    storage_start,
    storage_low,
    storage_high,
    release_cap,
    efficiency,
    downstream,
    travel_delay,
):
    count, hours, lanes = release.shape
    scale_time = 1.0 / (hours * lax.axis_size("hours"))
    scale_sum = 1.0 / math.sqrt(count * lax.axis_size("river"))
    slab, flat, rim = (count, hours, lanes), (count, lanes), (count, RIM, lanes)
    wide = (count, hours + RIM, lanes)

    sd_next = passed_along(storage_dual, "river", -1)
    (total,) = call(totals_kernel, (), (storage_dual,), [flat], [])
    off_own = offsets(total, "hours", True)
    off_next = passed_along(off_own, "river", -1)
    q, w = call(
        functools.partial(ahead_kernel, scale_time, scale_sum),
        (downstream, travel_delay, efficiency),
        (storage_dual, sd_next, release, cost, demand_dual),
        [slab, rim],
        [(2 * count + 1, hours, lanes)],
    )
    w = passed_along(w, "hours", -1)
    release_new, mine, theirs, tot_own, tot_next, power = call(
        functools.partial(release_kernel, scale_time, scale_sum),
        (downstream, travel_delay, efficiency, release_cap),
        (q, w, off_own, off_next, release, inflow),
        [slab, wide, wide, flat, flat, (hours, lanes)],
        [(2 * count + 1, hours + RIM, lanes), (2 * count + 1, 1, lanes)],
    )
    came = passed_along(theirs, "river", 1)
    tot_came = passed_along(tot_next, "river", 1)
    off = offsets(tot_own + tot_came, "hours", False)
    edge = passed_along(mine[:, hours:] + came[:, hours:], "hours", 1)
    supplied = all_summed(power, "river")
    storage_dual_new, storage_excess, demand_dual_new = call(
        functools.partial(storage_kernel, scale_time),
        (storage_start, storage_low, storage_high),
        (mine, came, edge, off, storage_dual, supplied, demand_dual, demand),
        [slab, slab, (hours, lanes)],
        [],
    )
    return (release_new, storage_dual_new, demand_dual_new, storage_excess)


def solution(mesh):
    field, flat, row = P("river", "hours", None), P("hours", None), P("river")
    return jax.shard_map(
        shards,
        mesh=mesh,
        in_specs=(field, field, flat, field, field, flat) + (row,) * 7,
        out_specs=(field, field, flat, field),
        check_vma=False,
    )
```

time: 117 us -> 56.4 us (0.48)
  the two profiles are of different devices: /device:TPU:0 before, /device:TPU:18 now
where the time goes in v1:
time: 56.4 us; the launch traced here: 55.9 us
  waiting for transfers between devices  24.3 us (43%)
  starting transfers between devices  22.9 us (41%)
  Pallas kernels  4.17 us (7%)
  local copies, waits for them, and re-layouts  3.63 us (6%)
  between operations  0.86 us (2%)
    ppermute x6, starting transfers between devices, passed_along(): return lax.ppermute(block, axis, route)  17.4 us
    ppermute x6, waiting for transfers between devices, passed_along(): return lax.ppermute(block, axis, route)  12.2 us
    ppermute x8, waiting for transfers between devices, swapped(): lax.ppermute(block, axis, [(i, i ^ bit) for i in range(lax.axis_size(axis...  12.1 us
    ppermute x8, starting transfers between devices, swapped(): lax.ppermute(block, axis, [(i, i ^ bit) for i in range(lax.axis_size(axis...  5.49 us
    pallas_call x4, Pallas kernels, call(): pl.pallas_call(body, out_shape=[jax.ShapeDtypeStruct(s, jnp.float32) for...  4.17 us
    unnamed x28, local copies, waits for them, and re-layouts  3.63 us
  transfers between devices with their start and end apart: 14, of which 7 were waited for; matrix products, arithmetic and copies ran while one was open for 0% of the time, Pallas kernels for 2%

profile of v1, /device:TPU:18, one launch (start us, length us, event | category | flops | bytes accessed | tf_op | source)
XLA Modules:
  0.0 55.9 jit_solution(14145761631263250739)
XLA Ops:
  0.6 1.9 %collective-permute-start = (f32[10,16,512]{2,1,0:T(8,128)}, f32[10,16,512]{2,1,0:T(8,128)S(1)}, u32[]{:S(2)}, u32[]{:S(2)}) collective-permute-start(f32[10,16,512]{2,1,0:T(8,128)} %sd_ref.5), channel_id=1, source_target_pairs={{8,0},{16,8},{24,16},{9,1},{17,9},{25,17},{10,2},{18,10},{26,18},{... | collective-permute-start | bytes 983048 | tf_op jit(solution)/shard_map/ppermute | solution.py:127
  2.6 1.0 %copy-done = f32[10,16,512]{2,1,0:T(8,128)S(1)} copy-done((f32[10,16,512]{2,1,0:T(8,128)S(1)}, f32[10,16,512]{2,1,0:T(8,128)}, u32[]{:S(2)}) %copy-start) | copy-done | bytes 327704
  3.6 1.6 %collective-permute-start.2 = (f32[10,512]{1,0:T(8,128)S(1)}, f32[10,512]{1,0:T(8,128)S(1)}, u32[]{:S(2)}, u32[]{:S(2)}) collective-permute-start(f32[10,512]{1,0:T(8,128)S(1)} %shard_map.157), channel_id=1, source_target_pairs={{0,1},{1,0},{2,3},{3,2},{4,5},{5,4},{6,7},{7,6},{8,9},{9,8},{10,11... | collective-permute-start | bytes 61448 | tf_op jit(solution)/shard_map/ppermute | solution.py:131
  5.2 2.4 %collective-permute-done.2 = f32[10,512]{1,0:T(8,128)S(1)} collective-permute-done((f32[10,512]{1,0:T(8,128)S(1)}, f32[10,512]{1,0:T(8,128)S(1)}, u32[]{:S(2)}, u32[]{:S(2)}) %collective-permute-start.2) | collective-permute-done | bytes 20512 | tf_op jit(solution)/shard_map/ppermute | solution.py:131
  7.6 1.6 %collective-permute-start.3 = (f32[10,512]{1,0:T(8,128)S(1)}, f32[10,512]{1,0:T(8,128)S(1)}, u32[]{:S(2)}, u32[]{:S(2)}) collective-permute-start(f32[10,512]{1,0:T(8,128)S(1)} %add.36), channel_id=1, source_target_pairs={{0,2},{1,3},{2,0},{3,1},{4,6},{5,7},{6,4},{7,5},{8,10},{9,11},{10,... | collective-permute-start | bytes 61448 | tf_op jit(solution)/shard_map/ppermute | solution.py:131
  9.2 2.3 %collective-permute-done.3 = f32[10,512]{1,0:T(8,128)S(1)} collective-permute-done((f32[10,512]{1,0:T(8,128)S(1)}, f32[10,512]{1,0:T(8,128)S(1)}, u32[]{:S(2)}, u32[]{:S(2)}) %collective-permute-start.3) | collective-permute-done | bytes 20512 | tf_op jit(solution)/shard_map/ppermute | solution.py:131
  11.5 0.4 collective-permute-start.4
  12.6 1.0 %copy-done.2 = f32[10,16,512]{2,1,0:T(8,128)S(1)} copy-done((f32[10,16,512]{2,1,0:T(8,128)S(1)}, f32[10,16,512]{2,1,0:T(8,128)}, u32[]{:S(2)}) %copy-start.2) | copy-done | bytes 327704
  13.6 1.0 %copy-done.3 = f32[10,16,512]{2,1,0:T(8,128)S(1)} copy-done((f32[10,16,512]{2,1,0:T(8,128)S(1)}, f32[10,16,512]{2,1,0:T(8,128)}, u32[]{:S(2)}) %copy-start.3) | copy-done | bytes 327704
  14.6 0.9 %shard_map.156 = (f32[10,16,512]{2,1,0:T(8,128)S(1)}, f32[10,8,512]{2,1,0:T(8,128)S(1)}) custom-call(s32[10]{0:T(128)S(1)} %copy-done.7, s32[10]{0:T(128)S(1)} %copy-done.8, f32[10]{0:T(128)S(1)} %copy-done.9, f32[10,16,512]{2,1,0:T(8,128)S(1)} %copy-done.1, f32[10,16,512]{2,1,0:T(8,128)S(1)} %collective-permute-done.next_ref, f32[10,16,512]{2,1,0:T(8,128)S(1)} %copy-done.2, ...), custom_call_target="tpu_custom_call" | custom-call | tf_op jit(solution)/shard_map/pallas_call | solution.py:161
  15.4 5.6 %collective-permute-start.1 = (f32[10,8,512]{2,1,0:T(8,128)S(1)}, f32[10,8,512]{2,1,0:T(8,128)S(1)}, u32[]{:S(2)}, u32[]{:S(2)}) collective-permute-start(f32[10,8,512]{2,1,0:T(8,128)S(1)} %get-tuple-element.16), channel_id=1, source_target_pairs={{1,0},{2,1},{3,2},{4,3},{5,4},{6,5},{7,6},{9,8},{10,9},{11,10},{12... | collective-permute-start | bytes 491528 | tf_op jit(solution)/shard_map/ppermute | solution.py:127
  21.1 1.9 %collective-permute-start.5 = (f32[10,512]{1,0:T(8,128)S(1)}, f32[10,512]{1,0:T(8,128)S(1)}, u32[]{:S(2)}, u32[]{:S(2)}) collective-permute-start(f32[10,512]{1,0:T(8,128)S(1)} %select_add_fusion.1.own_ref), channel_id=1, source_target_pairs={{8,0},{16,8},{24,16},{9,1},{17,9},{25,17},{10,2},{18,10},{26,18},{... | collective-permute-start | bytes 61448 | tf_op jit(solution)/shard_map/ppermute | solution.py:127
  23.0 1.6 %collective-permute-done.5.next_ref = f32[10,512]{1,0:T(8,128)S(1)} collective-permute-done((f32[10,512]{1,0:T(8,128)S(1)}, f32[10,512]{1,0:T(8,128)S(1)}, u32[]{:S(2)}, u32[]{:S(2)}) %collective-permute-start.5) | collective-permute-done | bytes 20512 | tf_op jit(solution)/shard_map/ppermute | solution.py:127
  24.6 1.8 %shard_map.158 = (f32[10,16,512]{2,1,0:T(8,128)}, f32[10,24,512]{2,1,0:T(8,128)S(1)}, f32[10,24,512]{2,1,0:T(8,128)S(1)}, f32[10,512]{1,0:T(8,128)S(1)}, f32[10,512]{1,0:T(8,128)S(1)}, /*index=5*/f32[16,512]{1,0:T(8,128)S(1)}) custom-call(s32[10]{0:T(128)S(1)} %copy-done.7, s32[10]{0:T(128)S(1)} %copy-done.8, f32[10]{0:T(128)S(1)} %copy-done.9, ...), custom_call_target="tpu_custom_call" | custom-call | tf_op jit(solution)/shard_map/pallas_call | solution.py:161
  26.3 1.9 %collective-permute-start.6 = (f32[10,24,512]{2,1,0:T(8,128)S(1)}, f32[10,24,512]{2,1,0:T(8,128)S(1)}, u32[]{:S(2)}, u32[]{:S(2)}) collective-permute-start(f32[10,24,512]{2,1,0:T(8,128)S(1)} %get-tuple-element.19), channel_id=1, source_target_pairs={{0,8},{8,16},{16,24},{1,9},{9,17},{17,25},{2,10},{10,18},{18,26},{... | collective-permute-start | bytes 1474568 | tf_op jit(solution)/shard_map/ppermute | solution.py:127
  28.3 2.4 %collective-permute-start.8 = (f32[10,512]{1,0:T(8,128)S(1)}, f32[10,512]{1,0:T(8,128)S(1)}, u32[]{:S(2)}, u32[]{:S(2)}) collective-permute-start(f32[10,512]{1,0:T(8,128)S(1)} %get-tuple-element.21), channel_id=1, source_target_pairs={{0,8},{8,16},{16,24},{1,9},{9,17},{17,25},{2,10},{10,18},{18,26},{... | collective-permute-start | bytes 61448 | tf_op jit(solution)/shard_map/ppermute | solution.py:127
  30.7 6.1 %collective-permute-done.8 = f32[10,512]{1,0:T(8,128)S(1)} collective-permute-done((f32[10,512]{1,0:T(8,128)S(1)}, f32[10,512]{1,0:T(8,128)S(1)}, u32[]{:S(2)}, u32[]{:S(2)}) %collective-permute-start.8) | collective-permute-done | bytes 20512 | tf_op jit(solution)/shard_map/ppermute | solution.py:127
  36.8 0.5 collective-permute-start.9
  37.4 3.3 %collective-permute-done.9 = f32[10,512]{1,0:T(8,128)S(1)} collective-permute-done((f32[10,512]{1,0:T(8,128)S(1)}, f32[10,512]{1,0:T(8,128)S(1)}, u32[]{:S(2)}, u32[]{:S(2)}) %collective-permute-start.9) | collective-permute-done | bytes 20512 | tf_op jit(solution)/shard_map/ppermute | solution.py:131
  40.8 4.0 %collective-permute-done.10 = f32[10,512]{1,0:T(8,128)S(1)} collective-permute-done((f32[10,512]{1,0:T(8,128)S(1)}, f32[10,512]{1,0:T(8,128)S(1)}, u32[]{:S(2)}, u32[]{:S(2)}) %collective-permute-start.10) | collective-permute-done | bytes 20512 | tf_op jit(solution)/shard_map/ppermute | solution.py:131
  44.8 1.3 %collective-permute-start.11 = (f32[10,512]{1,0:T(8,128)S(1)}, f32[10,512]{1,0:T(8,128)S(1)}, u32[]{:S(2)}, u32[]{:S(2)}) collective-permute-start(f32[10,512]{1,0:T(8,128)S(1)} %add.44), channel_id=1, source_target_pairs={{0,4},{1,5},{2,6},{3,7},{4,0},{5,1},{6,2},{7,3},{8,12},{9,13},{10,... | collective-permute-start | bytes 61448 | tf_op jit(solution)/shard_map/ppermute | solution.py:131
  46.2 3.7 %collective-permute-start.7 = (f32[10,8,512]{2,1,0:T(8,128)S(1)}, f32[10,8,512]{2,1,0:T(8,128)S(1)}, u32[]{:S(2)}, u32[]{:S(2)}) collective-permute-start(f32[10,8,512]{2,1,0:T(8,128)S(1)} %slice_add_fusion), channel_id=1, source_target_pairs={{0,1},{1,2},{2,3},{3,4},{4,5},{5,6},{6,7},{8,9},{9,10},{10,11},{11... | collective-permute-start | bytes 491528 | tf_op jit(solution)/shard_map/ppermute | solution.py:127
  49.9 4.5 %collective-permute-done.7.rim_ref = f32[10,8,512]{2,1,0:T(8,128)S(1)} collective-permute-done((f32[10,8,512]{2,1,0:T(8,128)S(1)}, f32[10,8,512]{2,1,0:T(8,128)S(1)}, u32[]{:S(2)}, u32[]{:S(2)}) %collective-permute-start.7) | collective-permute-done | bytes 163872 | tf_op jit(solution)/shard_map/ppermute | solution.py:127
  54.4 1.5 %shard_map.159 = (f32[10,16,512]{2,1,0:T(8,128)}, f32[10,16,512]{2,1,0:T(8,128)}, f32[16,512]{1,0:T(8,128)}) custom-call(f32[10]{0:T(128)S(1)} %copy-done.10, f32[10]{0:T(128)S(1)} %copy-done.11, f32[10]{0:T(128)S(1)} %copy-done.12, f32[10,24,512]{2,1,0:T(8,128)S(1)} %get-tuple-element.18.mine_ref, f32[10,24,512]{2,1,0:T(8,128)S(1)} %collective-permute-done.6.came_ref, ...), custom_call_target="tpu_custom_call" | custom-call | tf_op jit(solution)/shard_map/pallas_call | solution.py:161
  (46 shorter events, 1.0 us)
Async XLA Ops:
  0.6 11.3 %collective-permute-start = (f32[10,16,512]{2,1,0:T(8,128)}, f32[10,16,512]{2,1,0:T(8,128)S(1)}, u32[]{:S(2)}, u32[]{:S(2)}) collective-permute-start(f32[10,16,512]{2,1,0:T(8,128)} %sd_ref.5), channel_id=1, source_target_pairs={{8,0},{16,8},{24,16},{9,1},{17,9},{25,17},{10,2},{18,10},{26,18},{... | collective-permute-start | bytes 983048 | tf_op jit(solution)/shard_map/ppermute | solution.py:127
  2.6 1.0 %copy-start = (f32[10,16,512]{2,1,0:T(8,128)S(1)}, f32[10,16,512]{2,1,0:T(8,128)}, u32[]{:S(2)}) copy-start(f32[10,16,512]{2,1,0:T(8,128)} %sd_ref.5) | copy-start | bytes 983044
  3.5 8.4 %copy-start.1 = (f32[10,16,512]{2,1,0:T(8,128)S(1)}, f32[10,16,512]{2,1,0:T(8,128)}, u32[]{:S(2)}) copy-start(f32[10,16,512]{2,1,0:T(8,128)} %sd_ref.5) | copy-start | bytes 983044
  3.6 4.0 %collective-permute-start.2 = (f32[10,512]{1,0:T(8,128)S(1)}, f32[10,512]{1,0:T(8,128)S(1)}, u32[]{:S(2)}, u32[]{:S(2)}) collective-permute-start(f32[10,512]{1,0:T(8,128)S(1)} %shard_map.157), channel_id=1, source_target_pairs={{0,1},{1,0},{2,3},{3,2},{4,5},{5,4},{6,7},{7,6},{8,9},{9,8},{10,11... | collective-permute-start | bytes 61448 | tf_op jit(solution)/shard_map/ppermute | solution.py:131
  7.6 3.9 %collective-permute-start.3 = (f32[10,512]{1,0:T(8,128)S(1)}, f32[10,512]{1,0:T(8,128)S(1)}, u32[]{:S(2)}, u32[]{:S(2)}) collective-permute-start(f32[10,512]{1,0:T(8,128)S(1)} %add.36), channel_id=1, source_target_pairs={{0,2},{1,3},{2,0},{3,1},{4,6},{5,7},{6,4},{7,5},{8,10},{9,11},{10,... | collective-permute-start | bytes 61448 | tf_op jit(solution)/shard_map/ppermute | solution.py:131
  11.5 9.5 %collective-permute-start.4 = (f32[10,512]{1,0:T(8,128)S(1)}, f32[10,512]{1,0:T(8,128)S(1)}, u32[]{:S(2)}, u32[]{:S(2)}) collective-permute-start(f32[10,512]{1,0:T(8,128)S(1)} %add.38), channel_id=1, source_target_pairs={{0,4},{1,5},{2,6},{3,7},{4,0},{5,1},{6,2},{7,3},{8,12},{9,13},{10,... | collective-permute-start | bytes 61448 | tf_op jit(solution)/shard_map/ppermute | solution.py:131
  12.6 1.0 %copy-start.2 = (f32[10,16,512]{2,1,0:T(8,128)S(1)}, f32[10,16,512]{2,1,0:T(8,128)}, u32[]{:S(2)}) copy-start(f32[10,16,512]{2,1,0:T(8,128)} %rel_ref.3) | copy-start | bytes 983044
  13.6 1.0 %copy-start.3 = (f32[10,16,512]{2,1,0:T(8,128)S(1)}, f32[10,16,512]{2,1,0:T(8,128)}, u32[]{:S(2)}) copy-start(f32[10,16,512]{2,1,0:T(8,128)} %cost_ref.1) | copy-start | bytes 983044
  14.6 10.0 %copy-start.4 = (f32[10,16,512]{2,1,0:T(8,128)S(1)}, f32[10,16,512]{2,1,0:T(8,128)}, u32[]{:S(2)}) copy-start(f32[10,16,512]{2,1,0:T(8,128)} %inflow_ref.1) | copy-start | bytes 983044
  15.4 9.1 %collective-permute-start.1 = (f32[10,8,512]{2,1,0:T(8,128)S(1)}, f32[10,8,512]{2,1,0:T(8,128)S(1)}, u32[]{:S(2)}, u32[]{:S(2)}) collective-permute-start(f32[10,8,512]{2,1,0:T(8,128)S(1)} %get-tuple-element.16), channel_id=1, source_target_pairs={{1,0},{2,1},{3,2},{4,3},{5,4},{6,5},{7,6},{9,8},{10,9},{11,10},{12... | collective-permute-start | bytes 491528 | tf_op jit(solution)/shard_map/ppermute | solution.py:127
  21.0 3.5 %copy-start.13 = (f32[10]{0:T(128)S(1)}, f32[10]{0:T(128)}, u32[]{:S(2)}) copy-start(f32[10]{0:T(128)} %cap_ref.1) | copy-start | bytes 124
  21.1 3.5 %collective-permute-start.5 = (f32[10,512]{1,0:T(8,128)S(1)}, f32[10,512]{1,0:T(8,128)S(1)}, u32[]{:S(2)}, u32[]{:S(2)}) collective-permute-start(f32[10,512]{1,0:T(8,128)S(1)} %select_add_fusion.1.own_ref), channel_id=1, source_target_pairs={{8,0},{16,8},{24,16},{9,1},{17,9},{25,17},{10,2},{18,10},{26,18},{... | collective-permute-start | bytes 61448 | tf_op jit(solution)/shard_map/ppermute | solution.py:127
  26.3 19.8 %collective-permute-start.6 = (f32[10,24,512]{2,1,0:T(8,128)S(1)}, f32[10,24,512]{2,1,0:T(8,128)S(1)}, u32[]{:S(2)}, u32[]{:S(2)}) collective-permute-start(f32[10,24,512]{2,1,0:T(8,128)S(1)} %get-tuple-element.19), channel_id=1, source_target_pairs={{0,8},{8,16},{16,24},{1,9},{9,17},{17,25},{2,10},{10,18},{18,26},{... | collective-permute-start | bytes 1474568 | tf_op jit(solution)/shard_map/ppermute | solution.py:127
  28.2 9.1 %collective-permute-start.12 = (f32[16,512]{1,0:T(8,128)S(1)}, f32[16,512]{1,0:T(8,128)S(1)}, u32[]{:S(2)}, u32[]{:S(2)}) collective-permute-start(f32[16,512]{1,0:T(8,128)S(1)} %get-tuple-element.22), channel_id=1, source_target_pairs={{0,8},{8,0},{16,24},{24,16},{1,9},{9,1},{17,25},{25,17},{2,10},{10... | collective-permute-start | bytes 98312 | tf_op jit(solution)/shard_map/ppermute | solution.py:131
  28.3 8.5 %collective-permute-start.8 = (f32[10,512]{1,0:T(8,128)S(1)}, f32[10,512]{1,0:T(8,128)S(1)}, u32[]{:S(2)}, u32[]{:S(2)}) collective-permute-start(f32[10,512]{1,0:T(8,128)S(1)} %get-tuple-element.21), channel_id=1, source_target_pairs={{0,8},{8,16},{16,24},{1,9},{9,17},{17,25},{2,10},{10,18},{18,26},{... | collective-permute-start | bytes 61448 | tf_op jit(solution)/shard_map/ppermute | solution.py:127
  36.8 3.9 %collective-permute-start.9 = (f32[10,512]{1,0:T(8,128)S(1)}, f32[10,512]{1,0:T(8,128)S(1)}, u32[]{:S(2)}, u32[]{:S(2)}) collective-permute-start(f32[10,512]{1,0:T(8,128)S(1)} %add.41), channel_id=1, source_target_pairs={{0,1},{1,0},{2,3},{3,2},{4,5},{5,4},{6,7},{7,6},{8,9},{9,8},{10,11... | collective-permute-start | bytes 61448 | tf_op jit(solution)/shard_map/ppermute | solution.py:131
  37.3 8.7 %collective-permute-start.13 = (f32[16,512]{1,0:T(8,128)S(1)}, f32[16,512]{1,0:T(8,128)S(1)}, u32[]{:S(2)}, u32[]{:S(2)}) collective-permute-start(f32[16,512]{1,0:T(8,128)S(1)} %add.46), channel_id=1, source_target_pairs={{0,16},{8,24},{16,0},{24,8},{1,17},{9,25},{17,1},{25,9},{2,18},{10... | collective-permute-start | bytes 98312 | tf_op jit(solution)/shard_map/ppermute | solution.py:131
  40.8 4.0 %collective-permute-start.10 = (f32[10,512]{1,0:T(8,128)S(1)}, f32[10,512]{1,0:T(8,128)S(1)}, u32[]{:S(2)}, u32[]{:S(2)}) collective-permute-start(f32[10,512]{1,0:T(8,128)S(1)} %add.42), channel_id=1, source_target_pairs={{0,2},{1,3},{2,0},{3,1},{4,6},{5,7},{6,4},{7,5},{8,10},{9,11},{10,... | collective-permute-start | bytes 61448 | tf_op jit(solution)/shard_map/ppermute | solution.py:131
  44.8 5.1 %collective-permute-start.11 = (f32[10,512]{1,0:T(8,128)S(1)}, f32[10,512]{1,0:T(8,128)S(1)}, u32[]{:S(2)}, u32[]{:S(2)}) collective-permute-start(f32[10,512]{1,0:T(8,128)S(1)} %add.44), channel_id=1, source_target_pairs={{0,4},{1,5},{2,6},{3,7},{4,0},{5,1},{6,2},{7,3},{8,12},{9,13},{10,... | collective-permute-start | bytes 61448 | tf_op jit(solution)/shard_map/ppermute | solution.py:131
  46.1 8.3 %copy-start.6 = (f32[16,512]{1,0:T(8,128)S(1)}, f32[16,512]{1,0:T(8,128)}, u32[]{:S(2)}) copy-start(f32[16,512]{1,0:T(8,128)} %demand_ref.1) | copy-start | bytes 98308
  46.1 8.3 %copy-start.10 = (f32[10]{0:T(128)S(1)}, f32[10]{0:T(128)}, u32[]{:S(2)}) copy-start(f32[10]{0:T(128)} %start_ref.1) | copy-start | bytes 124
  46.2 8.3 %copy-start.11 = (f32[10]{0:T(128)S(1)}, f32[10]{0:T(128)}, u32[]{:S(2)}) copy-start(f32[10]{0:T(128)} %low_ref.1) | copy-start | bytes 124
  46.2 8.3 %copy-start.12 = (f32[10]{0:T(128)S(1)}, f32[10]{0:T(128)}, u32[]{:S(2)}) copy-start(f32[10]{0:T(128)} %high_ref.1) | copy-start | bytes 124
  46.2 8.2 %collective-permute-start.7 = (f32[10,8,512]{2,1,0:T(8,128)S(1)}, f32[10,8,512]{2,1,0:T(8,128)S(1)}, u32[]{:S(2)}, u32[]{:S(2)}) collective-permute-start(f32[10,8,512]{2,1,0:T(8,128)S(1)} %slice_add_fusion), channel_id=1, source_target_pairs={{0,1},{1,2},{2,3},{3,4},{4,5},{5,6},{6,7},{8,9},{9,10},{10,11},{11... | collective-permute-start | bytes 491528 | tf_op jit(solution)/shard_map/ppermute | solution.py:127
  (4 other events, 2.8 us)

commit v2 on v1

v2 whole, which is shorter than its diff:
```python
import functools
import math

import jax
import jax.numpy as jnp
from jax import lax
from jax.experimental import pallas as pl
from jax.experimental.pallas import tpu as pltpu
from jax.sharding import PartitionSpec as P

DMAX = 6
RIM = 8

primal_step = 1.0
dual_step = 0.1


def scan_rows(block, reverse):
    rows, lanes = block.shape
    place = lax.broadcasted_iota(jnp.int32, (8, lanes), 0)
    tiles = [block[k : k + 8] for k in range(0, rows, 8)]
    order = range(len(tiles) - 1, -1, -1) if reverse else range(len(tiles))
    carry = None
    for k in order:
        tile = tiles[k]
        for step in (1, 2, 4):
            moved = pltpu.roll(tile, 8 - step if reverse else step, 0)
            keep = place < 8 - step if reverse else place >= step
            tile = tile + jnp.where(keep, moved, 0.0)
        if carry is not None:
            tile = tile + carry
        tiles[k] = tile
        carry = tile[0:1] if reverse else tile[7:8]
    return jnp.concatenate(tiles, 0), carry


def sink_of(down_ref, j, count):
    down = down_ref[j]
    base = lax.axis_index("river") * count
    return jnp.where(down < 0, 2 * count, down - base)


def turned(tiles, amount):
    return [pltpu.roll(tile, amount, 0) for tile in tiles]


def totals_kernel(sd_ref, total_ref):
    for i in range(sd_ref.shape[0]):
        total_ref[i : i + 1] = jnp.sum(sd_ref[i], 0, keepdims=True)


def price_kernel(scale_sum, eff_hbm, cap_hbm, start_hbm, low_hbm, high_hbm, rel_ref, cost_ref, dual_ref, base_ref, rows_ref, scalars, sems):
    count, hours, lanes = base_ref.shape
    small = (eff_hbm, cap_hbm, start_hbm, low_hbm, high_hbm)
    copies = [pltpu.make_async_copy(ref, scalars.at[k], sems.at[k]) for k, ref in enumerate(small)]
    for copy in copies:
        copy.start()
    for copy in copies:
        copy.wait()
    dual = dual_ref[...]
    for j in range(count):
        for k in range(5):
            at = k * count + j
            rows_ref[at : at + 1] = jnp.full((1, lanes), scalars[k, j], jnp.float32)
        base_ref[j] = rel_ref[j] - primal_step * (cost_ref[j] + (scale_sum * scalars[0, j]) * dual)


def stock_kernel(inflow_ref, stock_ref):
    for j in range(inflow_ref.shape[0]):
        stock_ref[j] = scan_rows(inflow_ref[j], False)[0]


def copy_kernel(in_ref, out_ref):
    out_ref[...] = in_ref[...]


def route_kernel(down_ref, delay_ref, sd_ref, next_ref, lead_ref, w_ref, sums_ref):
    count, hours, lanes = sd_ref.shape
    for i in range(2 * count):
        ref, k = (sd_ref, i) if i < count else (next_ref, i - count)
        sums_ref[i] = scan_rows(ref[k], True)[0]
    sums_ref[2 * count] = jnp.zeros((hours, lanes), jnp.float32)
    place = lax.broadcasted_iota(jnp.int32, (RIM, lanes), 0)
    for j in range(count):
        lag = delay_ref[j]
        sink = sums_ref[sink_of(down_ref, j, count)]
        inside = place < RIM - lag
        tiles = turned([sink[k : k + RIM] for k in range(0, hours, RIM)], RIM - lag)
        w_ref[j] = jnp.where(inside, 0.0, tiles[0] - sink[0:1])
        tiles.append(jnp.zeros((RIM, lanes), jnp.float32))
        later = jnp.concatenate([jnp.where(inside, tiles[k], tiles[k + 1]) for k in range(hours // RIM)], 0)
        lead_ref[j] = later - sums_ref[j]


def release_kernel(scale_time, scale_sum, down_ref, delay_ref, rows_ref, base_ref, lead_ref, w_ref, own_ref, next_ref, rel_ref, stock_ref, new_hbm, mine_ref, theirs_ref, tots_ref, power_ref, tot, new_ref, sems):
    count, hours, lanes = base_ref.shape
    for i in range(count):
        tot[i] = own_ref[i : i + 1]
        tot[count + i] = next_ref[i : i + 1]
    tot[2 * count] = jnp.zeros((1, lanes), jnp.float32)
    lags = [delay_ref[j] for j in range(count)]
    sinks = [sink_of(down_ref, j, count) for j in range(count)]
    shifts = [tot[sinks[j]] - tot[j] for j in range(count)]
    tot[...] = jnp.zeros_like(tot)
    mine_ref[...] = jnp.zeros_like(mine_ref)
    theirs_ref[...] = jnp.zeros_like(theirs_ref)
    power = jnp.zeros((hours, lanes), jnp.float32)
    place = lax.broadcasted_iota(jnp.int32, (RIM, lanes), 0)
    zeros = jnp.zeros((RIM, lanes), jnp.float32)
    more = lax.axis_index("hours") < lax.axis_size("hours") - 1
    copies = [pltpu.make_async_copy(new_ref.at[j], new_hbm.at[j], sems.at[j]) for j in range(count)]
    for j in range(count):
        rim = jnp.where(more, w_ref[j], 0.0)
        later = lead_ref[j] + (jnp.concatenate([jnp.zeros((hours - RIM, lanes), jnp.float32), rim], 0) + shifts[j])
        release = rel_ref[j]
        new = jnp.clip(base_ref[j] - (primal_step * scale_time) * later, 0.0, rows_ref[count + j : count + j + 1])
        new_ref[j] = new
        copies[j].start()
        extra = 2.0 * new - release
        power = power + (scale_sum * rows_ref[j : j + 1]) * extra
        sums, total = scan_rows(extra, False)
        arrived = place >= lags[j]
        tiles = [zeros] + turned([sums[k : k + RIM] for k in range(0, hours, RIM)], lags[j])
        window = [jnp.where(arrived, tiles[k + 1], tiles[k]) for k in range(hours // RIM)]
        window.append(jnp.where(arrived, 0.0, tiles[-1] - total))
        window = jnp.concatenate(window, 0)

        @pl.when(sinks[j] < count)
        def _():
            mine_ref[sinks[j]] = mine_ref[sinks[j]] + window

        @pl.when((sinks[j] >= count) & (sinks[j] < 2 * count))
        def _():
            theirs_ref[sinks[j] - count] = theirs_ref[sinks[j] - count] + window

        tot[sinks[j]] = tot[sinks[j]] + total
        local = stock_ref[j] - sums
        mine_ref[j, 0:hours] = mine_ref[j, 0:hours] + local
        tot[j] = tot[j] + local[hours - 1 : hours]
    for i in range(2 * count):
        tots_ref[i : i + 1] = tot[i]
    power_ref[...] = power
    for copy in copies:
        copy.wait()


def storage_kernel(scale_time, rows_ref, mine_ref, came_ref, rim_ref, off_ref, offcame_ref, sd_ref, power_ref, dual_ref, demand_ref, sd_hbm, excess_hbm, dual_out, sd_out, excess_out, sems):
    count, hours, lanes = sd_ref.shape
    earlier = lax.axis_index("hours") > 0
    copies = [[pltpu.make_async_copy(src.at[i], dst.at[i], sems.at[k, i]) for i in range(count)] for k, (src, dst) in enumerate(((sd_out, sd_hbm), (excess_out, excess_hbm)))]
    for i in range(count):
        row = [rows_ref[k * count + i : k * count + i + 1] for k in range(5)]
        change = mine_ref[i, 0:hours] + came_ref[i, 0:hours] + (off_ref[i : i + 1] + offcame_ref[i : i + 1])
        rim = jnp.concatenate([jnp.where(earlier, rim_ref[i], 0.0), jnp.zeros((hours - RIM, lanes), jnp.float32)], 0)
        storage = row[2] + scale_time * (change + rim)
        low, high = row[3], row[4]
        dual = sd_ref[i]
        sd_out[i] = dual + dual_step * storage - dual_step * jnp.clip(dual / dual_step + storage, low, high)
        copies[0][i].start()
        excess_out[i] = storage - jnp.clip(storage, low, high)
        copies[1][i].start()
    dual_out[...] = jnp.minimum(dual_ref[...] + dual_step * (power_ref[...] - demand_ref[...]), 0.0)
    for i in range(count):
        for k in range(2):
            copies[k][i].wait()


def passed_along(block, axis, distance):
    count = lax.axis_size(axis)
    return lax.ppermute(block, axis, [(i, (i + distance) % count) for i in range(count)])


def swapped(block, axis, bit):
    return lax.ppermute(block, axis, [(i, i ^ bit) for i in range(lax.axis_size(axis))])


def offsets(total, axis, reverse, beside):
    count, place = lax.axis_size(axis), lax.axis_index(axis)
    result = jnp.zeros_like(total)
    for step in range((count - 1).bit_length()):
        bit = 1 << step
        other = swapped(total, axis, bit)
        if step < len(beside) and beside[step]:
            other, *_ = lax.optimization_barrier((other, *beside[step]))
        low = (place & bit) == 0
        result = result + jnp.where(low if reverse else ~low, other, 0.0)
        total = total + other
    return result


def all_summed(part, axis):
    count, first = lax.axis_size(axis), None
    for step in range((count - 1).bit_length()):
        part = part + swapped(part, axis, 1 << step)
        first = part if first is None else first
    return part, first


SMEM = pl.BlockSpec(memory_space=pltpu.SMEM)
VMEM = pl.BlockSpec(memory_space=pltpu.VMEM)
HBM = pl.BlockSpec(memory_space=pltpu.HBM)


def call(body, ins, outs, scratch):
    return pl.pallas_call(
        body,
        out_shape=[jax.ShapeDtypeStruct(shape, jnp.float32) for _, shape in outs],
        in_specs=[spec for spec, _ in ins],
        out_specs=[spec for spec, _ in outs],
        scratch_shapes=[pltpu.VMEM(entry, jnp.float32) if isinstance(entry, tuple) else entry for entry in scratch],
        compiler_params=pltpu.CompilerParams(vmem_limit_bytes=32 * 1024 * 1024),
    )(*(array for _, array in ins))


def shards(
    release,
    storage_dual,
    demand_dual,
    cost,
    inflow,
    demand,
    storage_start,
    storage_low,
    storage_high,
    release_cap,
    efficiency,
    downstream,
    travel_delay,
):
    count, hours, lanes = release.shape
    scale_time = 1.0 / (hours * lax.axis_size("hours"))
    scale_sum = 1.0 / math.sqrt(count * lax.axis_size("river"))
    slab, flat, rim = (count, hours, lanes), (count, lanes), (count, RIM, lanes)
    wide = (count, hours + RIM, lanes)
    dma = pltpu.SemaphoreType.DMA

    (total,) = call(totals_kernel, [(VMEM, storage_dual)], [(VMEM, flat)], [])
    sd = storage_dual
    (sd_sent,) = call(copy_kernel, [(VMEM, lax.optimization_barrier((storage_dual, total))[0])], [(VMEM, slab)], [])
    sd_next = passed_along(sd_sent, "river", -1)
    base, rows = call(
        functools.partial(price_kernel, scale_sum),
        [(HBM, a) for a in (efficiency, release_cap, storage_start, storage_low, storage_high)] + [(VMEM, a) for a in (release, cost, demand_dual)],
        [(VMEM, slab), (VMEM, (5 * count, lanes))],
        [pltpu.SMEM((5, count), jnp.float32), dma((5,))],
    )
    (stock,) = call(stock_kernel, [(VMEM, inflow)], [(VMEM, slab)], [])
    lead, w = call(
        route_kernel,
        [(SMEM, downstream), (SMEM, travel_delay), (VMEM, sd), (VMEM, sd_next)],
        [(VMEM, slab), (VMEM, rim)],
        [(2 * count + 1, hours, lanes)],
    )
    off_own = offsets(total, "hours", True, [(base, rows), (lead, w), (stock,)])
    off_next = passed_along(off_own, "river", -1)
    w = passed_along(w, "hours", -1)
    release_new, mine, theirs, tots, power = call(
        functools.partial(release_kernel, scale_time, scale_sum),
        [(SMEM, downstream), (SMEM, travel_delay)] + [(VMEM, a) for a in (rows, base, lead, w, off_own, off_next, release, stock)],
        [(HBM, slab), (VMEM, wide), (VMEM, wide), (VMEM, (2 * count, lanes)), (VMEM, (hours, lanes))],
        [(2 * count + 1, 1, lanes), slab, dma((count,))],
    )
    came = passed_along(theirs, "river", 1)
    late = mine[:, hours:] + came[:, hours:]
    supplied, first = all_summed(power, "river")
    edge = passed_along(late, "hours", 1)
    off = offsets(tots, "hours", False, [(first,), (late,)])
    off_came = passed_along(off[count:], "river", 1)
    storage_dual_new, storage_excess, demand_dual_new = call(
        functools.partial(storage_kernel, scale_time),
        [(VMEM, a) for a in (rows, mine, came, edge, off[:count], off_came, sd, supplied, demand_dual, demand)],
        [(HBM, slab), (HBM, slab), (VMEM, (hours, lanes))],
        [slab, slab, dma((2, count))],
    )
    return (release_new, storage_dual_new, demand_dual_new, storage_excess)


def solution(mesh):
    field, flat, row = P("river", "hours", None), P("hours", None), P("river")
    return jax.shard_map(
        shards,
        mesh=mesh,
        in_specs=(field, field, flat, field, field, flat) + (row,) * 7,
        out_specs=(field, field, flat, field),
        check_vma=False,
    )
```

time: 56.4 us -> 44.4 us (0.79)
  the two profiles are of different devices: /device:TPU:18 before, /device:TPU:0 now
where the time goes in v2:
time: 44.4 us; the launch traced here: 44.3 us
  starting transfers between devices  19.6 us (44%)
  waiting for transfers between devices  17.7 us (40%)
  Pallas kernels  5.02 us (11%)
  local copies, waits for them, and re-layouts  1.04 us (2%)
  between operations  0.85 us (2%)
    ppermute x8, starting transfers between devices, swapped(): lax.ppermute(block, axis, [(i, i ^ bit) for i in range(lax.axis_size(axis...  13.7 us
    ppermute x6, waiting for transfers between devices, passed_along(): lax.ppermute(block, axis, [(i, (i + distance) % count) for i in range(cou...  9.57 us
    ppermute x8, waiting for transfers between devices, swapped(): lax.ppermute(block, axis, [(i, i ^ bit) for i in range(lax.axis_size(axis...  8.1 us
    ppermute x6, starting transfers between devices, passed_along(): lax.ppermute(block, axis, [(i, (i + distance) % count) for i in range(cou...  5.94 us
    pallas_call x7, Pallas kernels, call(): pl.pallas_call(body, out_shape=[jax.ShapeDtypeStruct(shape, jnp.float32)...  5.02 us
    unnamed x28, local copies, waits for them, and re-layouts  1.03 us
  transfers between devices with their start and end apart: 14, of which 12 were waited for; matrix products, arithmetic and copies ran while one was open for 0% of the time, Pallas kernels for 4%

profile of v2, /device:TPU:0, one launch (start us, length us, event | category | flops | bytes accessed | tf_op | source)
XLA Modules:
  0.0 44.3 jit_solution(12780924680790577615)
XLA Ops:
  0.6 1.0 %copy-done = f32[10,16,512]{2,1,0:T(8,128)S(1)} copy-done((f32[10,16,512]{2,1,0:T(8,128)S(1)}, f32[10,16,512]{2,1,0:T(8,128)}, u32[]{:S(2)}) %copy-start) | copy-done | bytes 327704
  1.8 2.4 %collective-permute-start = (f32[10,16,512]{2,1,0:T(8,128)S(1)}, f32[10,16,512]{2,1,0:T(8,128)S(1)}, u32[]{:S(2)}, u32[]{:S(2)}) collective-permute-start(f32[10,16,512]{2,1,0:T(8,128)S(1)} %shard_map.158), channel_id=1, source_target_pairs={{0,24},{8,0},{16,8},{24,16},{1,25},{9,1},{17,9},{25,17},{2,26},{10... | collective-permute-start | bytes 983048 | tf_op jit(solution)/shard_map/ppermute | solution.py:170
  4.2 1.5 %collective-permute-start.2 = (f32[10,512]{1,0:T(8,128)S(1)}, f32[10,512]{1,0:T(8,128)S(1)}, u32[]{:S(2)}, u32[]{:S(2)}) collective-permute-start(f32[10,512]{1,0:T(8,128)S(1)} %shard_map.157), channel_id=1, source_target_pairs={{0,1},{1,0},{2,3},{3,2},{4,5},{5,4},{6,7},{7,6},{8,9},{9,8},{10,11... | collective-permute-start | bytes 61448 | tf_op jit(solution)/shard_map/ppermute | solution.py:174
  6.5 1.7 %collective-permute-done.2 = f32[10,512]{1,0:T(8,128)S(1)} collective-permute-done((f32[10,512]{1,0:T(8,128)S(1)}, f32[10,512]{1,0:T(8,128)S(1)}, u32[]{:S(2)}, u32[]{:S(2)}) %collective-permute-start.2) | collective-permute-done | bytes 20512 | tf_op jit(solution)/shard_map/ppermute | solution.py:174
  8.1 1.6 %collective-permute-start.3 = (f32[10,512]{1,0:T(8,128)S(1)}, f32[10,512]{1,0:T(8,128)S(1)}, u32[]{:S(2)}, u32[]{:S(2)}) collective-permute-start(f32[10,512]{1,0:T(8,128)S(1)} %add.33), channel_id=1, source_target_pairs={{0,2},{1,3},{2,0},{3,1},{4,6},{5,7},{6,4},{7,5},{8,10},{9,11},{10,... | collective-permute-start | bytes 61448 | tf_op jit(solution)/shard_map/ppermute | solution.py:174
  10.6 1.5 %collective-permute-done.3 = f32[10,512]{1,0:T(8,128)S(1)} collective-permute-done((f32[10,512]{1,0:T(8,128)S(1)}, f32[10,512]{1,0:T(8,128)S(1)}, u32[]{:S(2)}, u32[]{:S(2)}) %collective-permute-start.3) | collective-permute-done | bytes 20512 | tf_op jit(solution)/shard_map/ppermute | solution.py:174
  12.1 2.6 %collective-permute-start.4 = (f32[10,512]{1,0:T(8,128)S(1)}, f32[10,512]{1,0:T(8,128)S(1)}, u32[]{:S(2)}, u32[]{:S(2)}) collective-permute-start(f32[10,512]{1,0:T(8,128)S(1)} %add.35), channel_id=1, source_target_pairs={{0,4},{1,5},{2,6},{3,7},{4,0},{5,1},{6,2},{7,3},{8,12},{9,13},{10,... | collective-permute-start | bytes 61448 | tf_op jit(solution)/shard_map/ppermute | solution.py:174
  14.8 2.4 %collective-permute-start.1 = (f32[10,8,512]{2,1,0:T(8,128)S(1)}, f32[10,8,512]{2,1,0:T(8,128)S(1)}, u32[]{:S(2)}, u32[]{:S(2)}) collective-permute-start(f32[10,8,512]{2,1,0:T(8,128)S(1)} %get-tuple-element.26), channel_id=1, source_target_pairs={{0,7},{1,0},{2,1},{3,2},{4,3},{5,4},{6,5},{7,6},{8,15},{9,8},{10,9... | collective-permute-start | bytes 491528 | tf_op jit(solution)/shard_map/ppermute | solution.py:170
  17.3 1.6 %collective-permute-done.5.next_ref = f32[10,512]{1,0:T(8,128)S(1)} collective-permute-done((f32[10,512]{1,0:T(8,128)S(1)}, f32[10,512]{1,0:T(8,128)S(1)}, u32[]{:S(2)}, u32[]{:S(2)}) %collective-permute-start.5) | collective-permute-done | bytes 20512 | tf_op jit(solution)/shard_map/ppermute | solution.py:170
  18.9 1.3 %collective-permute-done.1.w_ref = f32[10,8,512]{2,1,0:T(8,128)S(1)} collective-permute-done((f32[10,8,512]{2,1,0:T(8,128)S(1)}, f32[10,8,512]{2,1,0:T(8,128)S(1)}, u32[]{:S(2)}, u32[]{:S(2)}) %collective-permute-start.1) | collective-permute-done | bytes 163872 | tf_op jit(solution)/shard_map/ppermute | solution.py:170
  20.2 1.7 %shard_map.161 = (f32[10,16,512]{2,1,0:T(8,128)}, f32[10,24,512]{2,1,0:T(8,128)S(1)}, f32[10,24,512]{2,1,0:T(8,128)S(1)}, f32[20,512]{1,0:T(8,128)S(1)}, f32[16,512]{1,0:T(8,128)S(1)}) custom-call(s32[10]{0:T(128)S(1)} %copy-done.7, s32[10]{0:T(128)S(1)} %copy-done.8, f32[50,512]{1,0:T(8,128)S(1)} %get-tuple-element.22.rows_ref, ...), custom_call_target="tpu_custom_call" | custom-call | tf_op jit(solution)/shard_map/pallas_call | solution.py:205
  22.0 2.5 %collective-permute-start.8 = (f32[20,512]{1,0:T(8,128)S(1)}, f32[20,512]{1,0:T(8,128)S(1)}, u32[]{:S(2)}, u32[]{:S(2)}) collective-permute-start(f32[20,512]{1,0:T(8,128)S(1)} %get-tuple-element.33), channel_id=1, source_target_pairs={{0,1},{1,0},{2,3},{3,2},{4,5},{5,4},{6,7},{7,6},{8,9},{9,8},{10,11... | collective-permute-start | bytes 122888 | tf_op jit(solution)/shard_map/ppermute | solution.py:174
  24.9 0.9 %collective-permute-done.9 = f32[16,512]{1,0:T(8,128)S(1)} collective-permute-done((f32[16,512]{1,0:T(8,128)S(1)}, f32[16,512]{1,0:T(8,128)S(1)}, u32[]{:S(2)}, u32[]{:S(2)}) %collective-permute-start.9) | collective-permute-done | bytes 32800 | tf_op jit(solution)/shard_map/ppermute | solution.py:174
  25.7 1.3 %collective-permute-done.8 = f32[20,512]{1,0:T(8,128)S(1)} collective-permute-done((f32[20,512]{1,0:T(8,128)S(1)}, f32[20,512]{1,0:T(8,128)S(1)}, u32[]{:S(2)}, u32[]{:S(2)}) %collective-permute-start.8) | collective-permute-done | bytes 40992 | tf_op jit(solution)/shard_map/ppermute | solution.py:174
  27.1 1.6 %collective-permute-start.10 = (f32[20,512]{1,0:T(8,128)S(1)}, f32[20,512]{1,0:T(8,128)S(1)}, u32[]{:S(2)}, u32[]{:S(2)}) collective-permute-start(f32[20,512]{1,0:T(8,128)S(1)} %add.39), channel_id=1, source_target_pairs={{0,2},{1,3},{2,0},{3,1},{4,6},{5,7},{6,4},{7,5},{8,10},{9,11},{10,... | collective-permute-start | bytes 122888 | tf_op jit(solution)/shard_map/ppermute | solution.py:174
  28.7 1.5 %collective-permute-done.6.came_ref = f32[10,24,512]{2,1,0:T(8,128)S(1)} collective-permute-done((f32[10,24,512]{2,1,0:T(8,128)S(1)}, f32[10,24,512]{2,1,0:T(8,128)S(1)}, u32[]{:S(2)}, u32[]{:S(2)}) %collective-permute-start.6) | collective-permute-done | bytes 491552 | tf_op jit(solution)/shard_map/ppermute | solution.py:170
  30.3 1.0 %collective-permute-done.10 = f32[20,512]{1,0:T(8,128)S(1)} collective-permute-done((f32[20,512]{1,0:T(8,128)S(1)}, f32[20,512]{1,0:T(8,128)S(1)}, u32[]{:S(2)}, u32[]{:S(2)}) %collective-permute-start.10) | collective-permute-done | bytes 40992 | tf_op jit(solution)/shard_map/ppermute | solution.py:174
  31.2 2.4 %collective-permute-start.11 = (f32[20,512]{1,0:T(8,128)S(1)}, f32[20,512]{1,0:T(8,128)S(1)}, u32[]{:S(2)}, u32[]{:S(2)}) collective-permute-start(f32[20,512]{1,0:T(8,128)S(1)} %add.41), channel_id=1, source_target_pairs={{0,4},{1,5},{2,6},{3,7},{4,0},{5,1},{6,2},{7,3},{8,12},{9,13},{10,... | collective-permute-start | bytes 122888 | tf_op jit(solution)/shard_map/ppermute | solution.py:174
  33.6 1.0 %collective-permute-start.13 = (f32[16,512]{1,0:T(8,128)S(1)}, f32[16,512]{1,0:T(8,128)S(1)}, u32[]{:S(2)}, u32[]{:S(2)}) collective-permute-start(f32[16,512]{1,0:T(8,128)S(1)} %add.38), channel_id=1, source_target_pairs={{0,16},{8,24},{16,0},{24,8},{1,17},{9,25},{17,1},{25,9},{2,18},{10... | collective-permute-start | bytes 98312 | tf_op jit(solution)/shard_map/ppermute | solution.py:174
  34.6 1.0 %collective-permute-start.7 = (f32[10,8,512]{2,1,0:T(8,128)S(1)}, f32[10,8,512]{2,1,0:T(8,128)S(1)}, u32[]{:S(2)}, u32[]{:S(2)}) collective-permute-start(f32[10,8,512]{2,1,0:T(8,128)S(1)} %slice_add_fusion), channel_id=1, source_target_pairs={{0,1},{1,2},{2,3},{3,4},{4,5},{5,6},{6,7},{7,0},{8,9},{9,10},{10,1... | collective-permute-start | bytes 491528 | tf_op jit(solution)/shard_map/ppermute | solution.py:170
  36.4 1.1 %collective-permute-done.13 = f32[16,512]{1,0:T(8,128)S(1)} collective-permute-done((f32[16,512]{1,0:T(8,128)S(1)}, f32[16,512]{1,0:T(8,128)S(1)}, u32[]{:S(2)}, u32[]{:S(2)}) %collective-permute-start.13) | collective-permute-done | bytes 32800 | tf_op jit(solution)/shard_map/ppermute | solution.py:174
  37.5 2.2 %collective-permute-done.12.offcame_ref = f32[10,512]{1,0:T(8,128)S(1)} collective-permute-done((f32[10,512]{1,0:T(8,128)S(1)}, f32[10,512]{1,0:T(8,128)S(1)}, u32[]{:S(2)}, u32[]{:S(2)}) %collective-permute-start.12) | collective-permute-done | bytes 20512 | tf_op jit(solution)/shard_map/ppermute | solution.py:170
  39.7 2.9 %collective-permute-done.7.rim_ref = f32[10,8,512]{2,1,0:T(8,128)S(1)} collective-permute-done((f32[10,8,512]{2,1,0:T(8,128)S(1)}, f32[10,8,512]{2,1,0:T(8,128)S(1)}, u32[]{:S(2)}, u32[]{:S(2)}) %collective-permute-start.7) | collective-permute-done | bytes 163872 | tf_op jit(solution)/shard_map/ppermute | solution.py:170
  42.7 1.6 %shard_map.162 = (f32[10,16,512]{2,1,0:T(8,128)}, f32[10,16,512]{2,1,0:T(8,128)}, f32[16,512]{1,0:T(8,128)}) custom-call(f32[50,512]{1,0:T(8,128)S(1)} %get-tuple-element.22.rows_ref, f32[10,24,512]{2,1,0:T(8,128)S(1)} %get-tuple-element.31.mine_ref, f32[10,24,512]{2,1,0:T(8,128)S(1)} %collective-permute-done.6.came_ref, ...), custom_call_target="tpu_custom_call" | custom-call | tf_op jit(solution)/shard_map/pallas_call | solution.py:205
  (49 shorter events, 3.1 us)
Async XLA Ops:
  1.6 4.1 %copy-start.5 = (f32[16,512]{1,0:T(8,128)S(1)}, f32[16,512]{1,0:T(8,128)}, u32[]{:S(2)}) copy-start(f32[16,512]{1,0:T(8,128)} %dual_ref.3) | copy-start | bytes 98308
  1.6 4.1 %copy-start.9 = (f32[10]{0:T(128)S(1)}, f32[10]{0:T(128)}, u32[]{:S(2)}) copy-start(f32[10]{0:T(128)} %eff_hbm.1) | copy-start | bytes 124
  1.6 4.1 %copy-start.10 = (f32[10]{0:T(128)S(1)}, f32[10]{0:T(128)}, u32[]{:S(2)}) copy-start(f32[10]{0:T(128)} %cap_hbm.1) | copy-start | bytes 124
  1.6 4.1 %copy-start.11 = (f32[10]{0:T(128)S(1)}, f32[10]{0:T(128)}, u32[]{:S(2)}) copy-start(f32[10]{0:T(128)} %start_hbm.1) | copy-start | bytes 124
  1.6 4.1 %copy-start.12 = (f32[10]{0:T(128)S(1)}, f32[10]{0:T(128)}, u32[]{:S(2)}) copy-start(f32[10]{0:T(128)} %low_hbm.1) | copy-start | bytes 124
  1.6 4.1 %copy-start.13 = (f32[10]{0:T(128)S(1)}, f32[10]{0:T(128)}, u32[]{:S(2)}) copy-start(f32[10]{0:T(128)} %high_hbm.1) | copy-start | bytes 124
  1.7 4.1 %copy-start.2 = (f32[10,16,512]{2,1,0:T(8,128)S(1)}, f32[10,16,512]{2,1,0:T(8,128)}, u32[]{:S(2)}) copy-start(f32[10,16,512]{2,1,0:T(8,128)} %rel_ref.3) | copy-start | bytes 983044
  1.8 8.0 %copy-start.1 = (f32[10,16,512]{2,1,0:T(8,128)S(1)}, f32[10,16,512]{2,1,0:T(8,128)}, u32[]{:S(2)}) copy-start(f32[10,16,512]{2,1,0:T(8,128)} %sd_ref.5) | copy-start | bytes 983044
  1.8 8.0 %collective-permute-start = (f32[10,16,512]{2,1,0:T(8,128)S(1)}, f32[10,16,512]{2,1,0:T(8,128)S(1)}, u32[]{:S(2)}, u32[]{:S(2)}) collective-permute-start(f32[10,16,512]{2,1,0:T(8,128)S(1)} %shard_map.158), channel_id=1, source_target_pairs={{0,24},{8,0},{16,8},{24,16},{1,25},{9,1},{17,9},{25,17},{2,26},{10... | collective-permute-start | bytes 983048 | tf_op jit(solution)/shard_map/ppermute | solution.py:170
  4.2 3.9 %collective-permute-start.2 = (f32[10,512]{1,0:T(8,128)S(1)}, f32[10,512]{1,0:T(8,128)S(1)}, u32[]{:S(2)}, u32[]{:S(2)}) collective-permute-start(f32[10,512]{1,0:T(8,128)S(1)} %shard_map.157), channel_id=1, source_target_pairs={{0,1},{1,0},{2,3},{3,2},{4,5},{5,4},{6,7},{7,6},{8,9},{9,8},{10,11... | collective-permute-start | bytes 61448 | tf_op jit(solution)/shard_map/ppermute | solution.py:174
  8.1 6.6 %copy-start.4 = (f32[10,16,512]{2,1,0:T(8,128)S(1)}, f32[10,16,512]{2,1,0:T(8,128)}, u32[]{:S(2)}) copy-start(f32[10,16,512]{2,1,0:T(8,128)} %inflow_ref.1) | copy-start | bytes 983044
  8.1 4.0 %collective-permute-start.3 = (f32[10,512]{1,0:T(8,128)S(1)}, f32[10,512]{1,0:T(8,128)S(1)}, u32[]{:S(2)}, u32[]{:S(2)}) collective-permute-start(f32[10,512]{1,0:T(8,128)S(1)} %add.33), channel_id=1, source_target_pairs={{0,2},{1,3},{2,0},{3,1},{4,6},{5,7},{6,4},{7,5},{8,10},{9,11},{10,... | collective-permute-start | bytes 61448 | tf_op jit(solution)/shard_map/ppermute | solution.py:174
  12.1 5.1 %collective-permute-start.4 = (f32[10,512]{1,0:T(8,128)S(1)}, f32[10,512]{1,0:T(8,128)S(1)}, u32[]{:S(2)}, u32[]{:S(2)}) collective-permute-start(f32[10,512]{1,0:T(8,128)S(1)} %add.35), channel_id=1, source_target_pairs={{0,4},{1,5},{2,6},{3,7},{4,0},{5,1},{6,2},{7,3},{8,12},{9,13},{10,... | collective-permute-start | bytes 61448 | tf_op jit(solution)/shard_map/ppermute | solution.py:174
  14.8 5.4 %collective-permute-start.1 = (f32[10,8,512]{2,1,0:T(8,128)S(1)}, f32[10,8,512]{2,1,0:T(8,128)S(1)}, u32[]{:S(2)}, u32[]{:S(2)}) collective-permute-start(f32[10,8,512]{2,1,0:T(8,128)S(1)} %get-tuple-element.26), channel_id=1, source_target_pairs={{0,7},{1,0},{2,1},{3,2},{4,3},{5,4},{6,5},{7,6},{8,15},{9,8},{10,9... | collective-permute-start | bytes 491528 | tf_op jit(solution)/shard_map/ppermute | solution.py:170
  17.2 1.7 %collective-permute-start.5 = (f32[10,512]{1,0:T(8,128)S(1)}, f32[10,512]{1,0:T(8,128)S(1)}, u32[]{:S(2)}, u32[]{:S(2)}) collective-permute-start(f32[10,512]{1,0:T(8,128)S(1)} %select_add_fusion.1.own_ref), channel_id=1, source_target_pairs={{0,24},{8,0},{16,8},{24,16},{1,25},{9,1},{17,9},{25,17},{2,26},{10... | collective-permute-start | bytes 61448 | tf_op jit(solution)/shard_map/ppermute | solution.py:170
  21.9 8.3 %collective-permute-start.6 = (f32[10,24,512]{2,1,0:T(8,128)S(1)}, f32[10,24,512]{2,1,0:T(8,128)S(1)}, u32[]{:S(2)}, u32[]{:S(2)}) collective-permute-start(f32[10,24,512]{2,1,0:T(8,128)S(1)} %get-tuple-element.32), channel_id=1, source_target_pairs={{0,8},{8,16},{16,24},{24,0},{1,9},{9,17},{17,25},{25,1},{2,10},{10... | collective-permute-start | bytes 1474568 | tf_op jit(solution)/shard_map/ppermute | solution.py:170
  22.0 5.1 %collective-permute-start.8 = (f32[20,512]{1,0:T(8,128)S(1)}, f32[20,512]{1,0:T(8,128)S(1)}, u32[]{:S(2)}, u32[]{:S(2)}) collective-permute-start(f32[20,512]{1,0:T(8,128)S(1)} %get-tuple-element.33), channel_id=1, source_target_pairs={{0,1},{1,0},{2,3},{3,2},{4,5},{5,4},{6,7},{7,6},{8,9},{9,8},{10,11... | collective-permute-start | bytes 122888 | tf_op jit(solution)/shard_map/ppermute | solution.py:174
  24.5 1.3 %collective-permute-start.9 = (f32[16,512]{1,0:T(8,128)S(1)}, f32[16,512]{1,0:T(8,128)S(1)}, u32[]{:S(2)}, u32[]{:S(2)}) collective-permute-start(f32[16,512]{1,0:T(8,128)S(1)} %get-tuple-element.34), channel_id=1, source_target_pairs={{0,8},{8,0},{16,24},{24,16},{1,9},{9,1},{17,25},{25,17},{2,10},{10... | collective-permute-start | bytes 98312 | tf_op jit(solution)/shard_map/ppermute | solution.py:174
  27.1 4.2 %collective-permute-start.10 = (f32[20,512]{1,0:T(8,128)S(1)}, f32[20,512]{1,0:T(8,128)S(1)}, u32[]{:S(2)}, u32[]{:S(2)}) collective-permute-start(f32[20,512]{1,0:T(8,128)S(1)} %add.39), channel_id=1, source_target_pairs={{0,2},{1,3},{2,0},{3,1},{4,6},{5,7},{6,4},{7,5},{8,10},{9,11},{10,... | collective-permute-start | bytes 122888 | tf_op jit(solution)/shard_map/ppermute | solution.py:174
  31.2 5.1 %collective-permute-start.11 = (f32[20,512]{1,0:T(8,128)S(1)}, f32[20,512]{1,0:T(8,128)S(1)}, u32[]{:S(2)}, u32[]{:S(2)}) collective-permute-start(f32[20,512]{1,0:T(8,128)S(1)} %add.41), channel_id=1, source_target_pairs={{0,4},{1,5},{2,6},{3,7},{4,0},{5,1},{6,2},{7,3},{8,12},{9,13},{10,... | collective-permute-start | bytes 122888 | tf_op jit(solution)/shard_map/ppermute | solution.py:174
  33.6 3.9 %collective-permute-start.13 = (f32[16,512]{1,0:T(8,128)S(1)}, f32[16,512]{1,0:T(8,128)S(1)}, u32[]{:S(2)}, u32[]{:S(2)}) collective-permute-start(f32[16,512]{1,0:T(8,128)S(1)} %add.38), channel_id=1, source_target_pairs={{0,16},{8,24},{16,0},{24,8},{1,17},{9,25},{17,1},{25,9},{2,18},{10... | collective-permute-start | bytes 98312 | tf_op jit(solution)/shard_map/ppermute | solution.py:174
  34.6 8.0 %collective-permute-start.7 = (f32[10,8,512]{2,1,0:T(8,128)S(1)}, f32[10,8,512]{2,1,0:T(8,128)S(1)}, u32[]{:S(2)}, u32[]{:S(2)}) collective-permute-start(f32[10,8,512]{2,1,0:T(8,128)S(1)} %slice_add_fusion), channel_id=1, source_target_pairs={{0,1},{1,2},{2,3},{3,4},{4,5},{5,6},{6,7},{7,0},{8,9},{9,10},{10,1... | collective-permute-start | bytes 491528 | tf_op jit(solution)/shard_map/ppermute | solution.py:170
  36.3 6.3 %copy-start.6 = (f32[16,512]{1,0:T(8,128)S(1)}, f32[16,512]{1,0:T(8,128)}, u32[]{:S(2)}) copy-start(f32[16,512]{1,0:T(8,128)} %demand_ref.1) | copy-start | bytes 98308
  36.3 3.4 %collective-permute-start.12 = (f32[10,512]{1,0:T(8,128)S(1)}, f32[10,512]{1,0:T(8,128)S(1)}, u32[]{:S(2)}, u32[]{:S(2)}) collective-permute-start(f32[10,512]{1,0:T(8,128)S(1)} %get-tuple-element.40), channel_id=1, source_target_pairs={{0,8},{8,16},{16,24},{24,0},{1,9},{9,17},{17,25},{25,1},{2,10},{10... | collective-permute-start | bytes 61448 | tf_op jit(solution)/shard_map/ppermute | solution.py:170
  (4 other events, 8.4 us)

commit v3 on v2

--- a/solution.py
+++ b/solution.py
@@ -10,6 +10,7 @@
 
 DMAX = 6
 RIM = 8
+EDGE = DMAX - 1
 
 primal_step = 1.0
 dual_step = 0.1
@@ -86,62 +87,80 @@
         sink = sums_ref[sink_of(down_ref, j, count)]
         inside = place < RIM - lag
         tiles = turned([sink[k : k + RIM] for k in range(0, hours, RIM)], RIM - lag)
-        w_ref[j] = jnp.where(inside, 0.0, tiles[0] - sink[0:1])
+        w_ref[EDGE * j : EDGE * (j + 1)] = jnp.where(inside, 0.0, tiles[0] - sink[0:1])[RIM - EDGE :]
         tiles.append(jnp.zeros((RIM, lanes), jnp.float32))
         later = jnp.concatenate([jnp.where(inside, tiles[k], tiles[k + 1]) for k in range(hours // RIM)], 0)
         lead_ref[j] = later - sums_ref[j]
 
 
-def release_kernel(scale_time, scale_sum, down_ref, delay_ref, rows_ref, base_ref, lead_ref, w_ref, own_ref, next_ref, rel_ref, stock_ref, new_hbm, mine_ref, theirs_ref, tots_ref, power_ref, tot, new_ref, sems):
+def release_kernel(scale_time, scale_sum, down_ref, delay_ref, rows_ref, base_ref, lead_ref, w_ref, own_ref, next_ref, rel_ref, stock_ref, new_hbm, mine_ref, theirs_ref, tots_ref, power_ref, tot, new_ref, extra_ref, late_ref, sems):
     count, hours, lanes = base_ref.shape
     for i in range(count):
         tot[i] = own_ref[i : i + 1]
         tot[count + i] = next_ref[i : i + 1]
     tot[2 * count] = jnp.zeros((1, lanes), jnp.float32)
-    lags = [delay_ref[j] for j in range(count)]
     sinks = [sink_of(down_ref, j, count) for j in range(count)]
     shifts = [tot[sinks[j]] - tot[j] for j in range(count)]
     tot[...] = jnp.zeros_like(tot)
-    mine_ref[...] = jnp.zeros_like(mine_ref)
-    theirs_ref[...] = jnp.zeros_like(theirs_ref)
     power = jnp.zeros((hours, lanes), jnp.float32)
-    place = lax.broadcasted_iota(jnp.int32, (RIM, lanes), 0)
-    zeros = jnp.zeros((RIM, lanes), jnp.float32)
     more = lax.axis_index("hours") < lax.axis_size("hours") - 1
     copies = [pltpu.make_async_copy(new_ref.at[j], new_hbm.at[j], sems.at[j]) for j in range(count)]
-    for j in range(count):
-        rim = jnp.where(more, w_ref[j], 0.0)
-        later = lead_ref[j] + (jnp.concatenate([jnp.zeros((hours - RIM, lanes), jnp.float32), rim], 0) + shifts[j])
-        release = rel_ref[j]
+    totals = []
+    for j in range(count):
+        rim = jnp.where(more, w_ref[EDGE * j : EDGE * (j + 1)], 0.0)
+        later = lead_ref[j] + (jnp.concatenate([jnp.zeros((hours - EDGE, lanes), jnp.float32), rim], 0) + shifts[j])
         new = jnp.clip(base_ref[j] - (primal_step * scale_time) * later, 0.0, rows_ref[count + j : count + j + 1])
         new_ref[j] = new
         copies[j].start()
-        extra = 2.0 * new - release
+        extra = 2.0 * new - rel_ref[j]
+        extra_ref[j] = extra
         power = power + (scale_sum * rows_ref[j : j + 1]) * extra
-        sums, total = scan_rows(extra, False)
+        totals.append(jnp.sum(extra, 0, keepdims=True))
+    for j in range(count):
+        tot[sinks[j]] = tot[sinks[j]] + totals[j]
+    for i in range(2 * count):
+        change = tot[i]
+        if i < count:
+            change = change + (stock_ref[i, hours - 1 : hours] - totals[i])
+        tots_ref[i : i + 1] = change
+    power_ref[...] = power
+    windows(down_ref, delay_ref, extra_ref, stock_ref, mine_ref, theirs_ref, late_ref)
+    for copy in copies:
+        copy.wait()
+
+
+def windows(down_ref, delay_ref, extra_ref, stock_ref, mine_ref, theirs_ref, late_ref):
+    count, hours, lanes = extra_ref.shape
+    lags = [delay_ref[j] for j in range(count)]
+    sinks = [sink_of(down_ref, j, count) for j in range(count)]
+    mine_ref[...] = jnp.zeros_like(mine_ref)
+    theirs_ref[...] = jnp.zeros_like(theirs_ref)
+    late_ref[...] = jnp.zeros_like(late_ref)
+    place = lax.broadcasted_iota(jnp.int32, (RIM, lanes), 0)
+    zeros = jnp.zeros((RIM, lanes), jnp.float32)
+    for j in range(count):
+        sums, total = scan_rows(extra_ref[j], False)
         arrived = place >= lags[j]
         tiles = [zeros] + turned([sums[k : k + RIM] for k in range(0, hours, RIM)], lags[j])
-        window = [jnp.where(arrived, tiles[k + 1], tiles[k]) for k in range(hours // RIM)]
-        window.append(jnp.where(arrived, 0.0, tiles[-1] - total))
-        window = jnp.concatenate(window, 0)
+        window = jnp.concatenate([jnp.where(arrived, tiles[k + 1], tiles[k]) for k in range(hours // RIM)], 0)
+        late_ref[sinks[j]] = late_ref[sinks[j]] + jnp.where(arrived, 0.0, tiles[-1] - total)
 
         @pl.when(sinks[j] < count)
         def _():
-            mine_ref[sinks[j]] = mine_ref[sinks[j]] + window
+            at = pl.ds(pl.multiple_of(sinks[j] * hours, RIM), hours)
+            mine_ref[at] = mine_ref[at] + window
 
         @pl.when((sinks[j] >= count) & (sinks[j] < 2 * count))
         def _():
-            theirs_ref[sinks[j] - count] = theirs_ref[sinks[j] - count] + window
-
-        tot[sinks[j]] = tot[sinks[j]] + total
-        local = stock_ref[j] - sums
-        mine_ref[j, 0:hours] = mine_ref[j, 0:hours] + local
-        tot[j] = tot[j] + local[hours - 1 : hours]
-    for i in range(2 * count):
-        tots_ref[i : i + 1] = tot[i]
-    power_ref[...] = power
-    for copy in copies:
-        copy.wait()
+            at = pl.ds(pl.multiple_of((sinks[j] - count) * hours, RIM), hours)
+            theirs_ref[at] = theirs_ref[at] + window
+
+        at = slice(j * hours, (j + 1) * hours)
+        mine_ref[at] = mine_ref[at] + (stock_ref[j] - sums)
+    for i in range(count):
+        at = slice(count * hours + EDGE * i, count * hours + EDGE * (i + 1))
+        mine_ref[at] = late_ref[i, 0:EDGE]
+        theirs_ref[at] = late_ref[count + i, 0:EDGE]
 
 
 def storage_kernel(scale_time, rows_ref, mine_ref, came_ref, rim_ref, off_ref, offcame_ref, sd_ref, power_ref, dual_ref, demand_ref, sd_hbm, excess_hbm, dual_out, sd_out, excess_out, sems):
@@ -150,8 +169,9 @@
     copies = [[pltpu.make_async_copy(src.at[i], dst.at[i], sems.at[k, i]) for i in range(count)] for k, (src, dst) in enumerate(((sd_out, sd_hbm), (excess_out, excess_hbm)))]
     for i in range(count):
         row = [rows_ref[k * count + i : k * count + i + 1] for k in range(5)]
-        change = mine_ref[i, 0:hours] + came_ref[i, 0:hours] + (off_ref[i : i + 1] + offcame_ref[i : i + 1])
-        rim = jnp.concatenate([jnp.where(earlier, rim_ref[i], 0.0), jnp.zeros((hours - RIM, lanes), jnp.float32)], 0)
+        at = slice(i * hours, (i + 1) * hours)
+        change = mine_ref[at] + came_ref[at] + (off_ref[i : i + 1] + offcame_ref[i : i + 1])
+        rim = jnp.concatenate([jnp.where(earlier, rim_ref[EDGE * i : EDGE * (i + 1)], 0.0), jnp.zeros((hours - EDGE, lanes), jnp.float32)], 0)
         storage = row[2] + scale_time * (change + rim)
         low, high = row[3], row[4]
         dual = sd_ref[i]
@@ -168,6 +188,11 @@
 def passed_along(block, axis, distance):
     count = lax.axis_size(axis)
     return lax.ppermute(block, axis, [(i, (i + distance) % count) for i in range(count)])
+
+
+def handed_on(block, axis, distance):
+    devices = range(lax.axis_size(axis))
+    return lax.ppermute(block, axis, [(i, i + distance) for i in devices if i + distance in devices])
 
 
 def swapped(block, axis, bit):
@@ -230,12 +255,10 @@
     count, hours, lanes = release.shape
     scale_time = 1.0 / (hours * lax.axis_size("hours"))
     scale_sum = 1.0 / math.sqrt(count * lax.axis_size("river"))
-    slab, flat, rim = (count, hours, lanes), (count, lanes), (count, RIM, lanes)
-    wide = (count, hours + RIM, lanes)
+    slab, flat, wide = (count, hours, lanes), (count, lanes), (count * (hours + EDGE), lanes)
     dma = pltpu.SemaphoreType.DMA
 
     (total,) = call(totals_kernel, [(VMEM, storage_dual)], [(VMEM, flat)], [])
-    sd = storage_dual
     (sd_sent,) = call(copy_kernel, [(VMEM, lax.optimization_barrier((storage_dual, total))[0])], [(VMEM, slab)], [])
     sd_next = passed_along(sd_sent, "river", -1)
     base, rows = call(
@@ -247,8 +270,8 @@
     (stock,) = call(stock_kernel, [(VMEM, inflow)], [(VMEM, slab)], [])
     lead, w = call(
         route_kernel,
-        [(SMEM, downstream), (SMEM, travel_delay), (VMEM, sd), (VMEM, sd_next)],
-        [(VMEM, slab), (VMEM, rim)],
+        [(SMEM, downstream), (SMEM, travel_delay), (VMEM, storage_dual), (VMEM, sd_next)],
+        [(VMEM, slab), (VMEM, (EDGE * count, lanes))],
         [(2 * count + 1, hours, lanes)],
     )
     off_own = offsets(total, "hours", True, [(base, rows), (lead, w), (stock,)])
@@ -258,17 +281,17 @@
         functools.partial(release_kernel, scale_time, scale_sum),
         [(SMEM, downstream), (SMEM, travel_delay)] + [(VMEM, a) for a in (rows, base, lead, w, off_own, off_next, release, stock)],
         [(HBM, slab), (VMEM, wide), (VMEM, wide), (VMEM, (2 * count, lanes)), (VMEM, (hours, lanes))],
-        [(2 * count + 1, 1, lanes), slab, dma((count,))],
-    )
+        [(2 * count + 1, 1, lanes), slab, slab, (2 * count + 1, RIM, lanes), dma((count,))],
+    )
+    supplied, first = all_summed(power, "river")
     came = passed_along(theirs, "river", 1)
-    late = mine[:, hours:] + came[:, hours:]
-    supplied, first = all_summed(power, "river")
-    edge = passed_along(late, "hours", 1)
-    off = offsets(tots, "hours", False, [(first,), (late,)])
+    late = mine[count * hours :] + came[count * hours :]
+    edge = handed_on(late, "hours", 1)
+    off = offsets(tots, "hours", False, [(first,), (late, supplied)])
     off_came = passed_along(off[count:], "river", 1)
     storage_dual_new, storage_excess, demand_dual_new = call(
         functools.partial(storage_kernel, scale_time),
-        [(VMEM, a) for a in (rows, mine, came, edge, off[:count], off_came, sd, supplied, demand_dual, demand)],
+        [(VMEM, a) for a in (rows, mine, came, edge, off[:count], off_came, storage_dual, supplied, demand_dual, demand)],
         [(HBM, slab), (HBM, slab), (VMEM, (hours, lanes))],
         [slab, slab, dma((2, count))],
     )

time: 44.4 us -> 41.6 us (0.937)
  waiting for transfers between devices: 17.7 us -> 12 us
  starting transfers between devices: 19.6 us -> 22.6 us
    ppermute x0 -> x1, starting transfers between devices: none -> 3.38 us  [handed_on(): lax.ppermute(block, axis, [(i, i + distance) for i in devices if i + dist...]
    ppermute x6 -> x5, waiting for transfers between devices: 9.57 us -> 6.23 us  [passed_along(): lax.ppermute(block, axis, [(i, (i + distance) % count) for i in range(cou...]
    ppermute x8, waiting for transfers between devices: 8.1 us -> 5.75 us  [swapped(): lax.ppermute(block, axis, [(i, i ^ bit) for i in range(lax.axis_size(axis...]
    ppermute x6 -> x5, starting transfers between devices: 5.94 us -> 5.07 us  [passed_along(): lax.ppermute(block, axis, [(i, (i + distance) % count) for i in range(cou...]
    ppermute x8, starting transfers between devices: 13.7 us -> 14.2 us  [swapped(): lax.ppermute(block, axis, [(i, i ^ bit) for i in range(lax.axis_size(axis...]
  transfers between devices with their start and end apart: 14 -> 14, of which waited for: 12 -> 9; matrix products, arithmetic and copies ran while one was open for 0% -> 0% of each run, Pallas kernels for 4% -> 4%
where the time goes in v3:
time: 41.6 us; the launch traced here: 41.5 us
  starting transfers between devices  22.6 us (54%)
  waiting for transfers between devices  12 us (29%)
  Pallas kernels  4.83 us (12%)
  local copies, waits for them, and re-layouts  1.04 us (2%)
  between operations  0.87 us (2%)
    ppermute x8, starting transfers between devices, swapped(): lax.ppermute(block, axis, [(i, i ^ bit) for i in range(lax.axis_size(axis...  14.2 us
    ppermute x5, waiting for transfers between devices, passed_along(): lax.ppermute(block, axis, [(i, (i + distance) % count) for i in range(cou...  6.23 us
    ppermute x8, waiting for transfers between devices, swapped(): lax.ppermute(block, axis, [(i, i ^ bit) for i in range(lax.axis_size(axis...  5.75 us
    ppermute x5, starting transfers between devices, passed_along(): lax.ppermute(block, axis, [(i, (i + distance) % count) for i in range(cou...  5.07 us
    pallas_call x7, Pallas kernels, call(): pl.pallas_call(body, out_shape=[jax.ShapeDtypeStruct(shape, jnp.float32)...  4.83 us
    ppermute x1, starting transfers between devices, handed_on(): lax.ppermute(block, axis, [(i, i + distance) for i in devices if i + dist...  3.38 us
    unnamed x28, local copies, waits for them, and re-layouts  1.03 us
  transfers between devices with their start and end apart: 14, of which 9 were waited for; matrix products, arithmetic and copies ran while one was open for 0% of the time, Pallas kernels for 4%

profile of v3, /device:TPU:0, one launch (start us, length us, event | category | flops | bytes accessed | tf_op | source)
XLA Modules:
  0.0 41.5 jit_solution(11746436979589876974)
XLA Ops:
  0.6 1.0 %copy-done = f32[10,16,512]{2,1,0:T(8,128)S(1)} copy-done((f32[10,16,512]{2,1,0:T(8,128)S(1)}, f32[10,16,512]{2,1,0:T(8,128)}, u32[]{:S(2)}) %copy-start) | copy-done | bytes 327704
  1.8 2.4 %collective-permute-start = (f32[10,16,512]{2,1,0:T(8,128)S(1)}, f32[10,16,512]{2,1,0:T(8,128)S(1)}, u32[]{:S(2)}, u32[]{:S(2)}) collective-permute-start(f32[10,16,512]{2,1,0:T(8,128)S(1)} %shard_map.158), channel_id=1, source_target_pairs={{0,24},{8,0},{16,8},{24,16},{1,25},{9,1},{17,9},{25,17},{2,26},{10... | collective-permute-start | bytes 983048 | tf_op jit(solution)/shard_map/ppermute | solution.py:190
  4.2 1.5 %collective-permute-start.2 = (f32[10,512]{1,0:T(8,128)S(1)}, f32[10,512]{1,0:T(8,128)S(1)}, u32[]{:S(2)}, u32[]{:S(2)}) collective-permute-start(f32[10,512]{1,0:T(8,128)S(1)} %shard_map.157), channel_id=1, source_target_pairs={{0,1},{1,0},{2,3},{3,2},{4,5},{5,4},{6,7},{7,6},{8,9},{9,8},{10,11... | collective-permute-start | bytes 61448 | tf_op jit(solution)/shard_map/ppermute | solution.py:199
  5.8 0.7 %shard_map.156 = (f32[10,16,512]{2,1,0:T(8,128)S(1)}, f32[50,512]{1,0:T(8,128)S(1)}) custom-call(f32[10]{0:T(128)S(1)} %copy-done.9, f32[10]{0:T(128)S(1)} %copy-done.10, f32[10]{0:T(128)S(1)} %copy-done.11, f32[10]{0:T(128)S(1)} %copy-done.12, f32[10]{0:T(128)S(1)} %copy-done.13, f32[10,16,512]{2,1,0:T(8,128)S(1)} %copy-done.2, ...), custom_call_target="tpu_custom_call" | custom-call | tf_op jit(solution)/shard_map/pallas_call | solution.py:230
  6.5 1.7 %collective-permute-done.2 = f32[10,512]{1,0:T(8,128)S(1)} collective-permute-done((f32[10,512]{1,0:T(8,128)S(1)}, f32[10,512]{1,0:T(8,128)S(1)}, u32[]{:S(2)}, u32[]{:S(2)}) %collective-permute-start.2) | collective-permute-done | bytes 20512 | tf_op jit(solution)/shard_map/ppermute | solution.py:199
  8.1 1.6 %collective-permute-start.3 = (f32[10,512]{1,0:T(8,128)S(1)}, f32[10,512]{1,0:T(8,128)S(1)}, u32[]{:S(2)}, u32[]{:S(2)}) collective-permute-start(f32[10,512]{1,0:T(8,128)S(1)} %add.33), channel_id=1, source_target_pairs={{0,2},{1,3},{2,0},{3,1},{4,6},{5,7},{6,4},{7,5},{8,10},{9,11},{10,... | collective-permute-start | bytes 61448 | tf_op jit(solution)/shard_map/ppermute | solution.py:199
  9.8 0.8 %shard_map.159 = (f32[10,16,512]{2,1,0:T(8,128)S(1)}, f32[50,512]{1,0:T(8,128)S(1)}) custom-call(s32[10]{0:T(128)S(1)} %copy-done.7, s32[10]{0:T(128)S(1)} %copy-done.8, f32[10,16,512]{2,1,0:T(8,128)S(1)} %copy-done.1, f32[10,16,512]{2,1,0:T(8,128)S(1)} %collective-permute-done.next_ref), custom_call_target="tpu_custom_call" | custom-call | tf_op jit(solution)/shard_map/pallas_call | solution.py:230
  10.6 1.5 %collective-permute-done.3 = f32[10,512]{1,0:T(8,128)S(1)} collective-permute-done((f32[10,512]{1,0:T(8,128)S(1)}, f32[10,512]{1,0:T(8,128)S(1)}, u32[]{:S(2)}, u32[]{:S(2)}) %collective-permute-start.3) | collective-permute-done | bytes 20512 | tf_op jit(solution)/shard_map/ppermute | solution.py:199
  12.1 2.6 %collective-permute-start.4 = (f32[10,512]{1,0:T(8,128)S(1)}, f32[10,512]{1,0:T(8,128)S(1)}, u32[]{:S(2)}, u32[]{:S(2)}) collective-permute-start(f32[10,512]{1,0:T(8,128)S(1)} %add.35), channel_id=1, source_target_pairs={{0,4},{1,5},{2,6},{3,7},{4,0},{5,1},{6,2},{7,3},{8,12},{9,13},{10,... | collective-permute-start | bytes 61448 | tf_op jit(solution)/shard_map/ppermute | solution.py:199
  14.8 2.4 %collective-permute-start.1 = (f32[50,512]{1,0:T(8,128)S(1)}, f32[50,512]{1,0:T(8,128)S(1)}, u32[]{:S(2)}, u32[]{:S(2)}) collective-permute-start(f32[50,512]{1,0:T(8,128)S(1)} %get-tuple-element.26), channel_id=1, source_target_pairs={{0,7},{1,0},{2,1},{3,2},{4,3},{5,4},{6,5},{7,6},{8,15},{9,8},{10,9... | collective-permute-start | bytes 307208 | tf_op jit(solution)/shard_map/ppermute | solution.py:190
  17.3 1.6 %collective-permute-done.5.next_ref = f32[10,512]{1,0:T(8,128)S(1)} collective-permute-done((f32[10,512]{1,0:T(8,128)S(1)}, f32[10,512]{1,0:T(8,128)S(1)}, u32[]{:S(2)}, u32[]{:S(2)}) %collective-permute-start.5) | collective-permute-done | bytes 20512 | tf_op jit(solution)/shard_map/ppermute | solution.py:190
  18.9 0.8 %collective-permute-done.1.w_ref = f32[50,512]{1,0:T(8,128)S(1)} collective-permute-done((f32[50,512]{1,0:T(8,128)S(1)}, f32[50,512]{1,0:T(8,128)S(1)}, u32[]{:S(2)}, u32[]{:S(2)}) %collective-permute-start.1) | collective-permute-done | bytes 102432 | tf_op jit(solution)/shard_map/ppermute | solution.py:190
  19.7 1.5 %shard_map.161 = (f32[10,16,512]{2,1,0:T(8,128)}, f32[210,512]{1,0:T(8,128)S(1)}, f32[210,512]{1,0:T(8,128)S(1)}, f32[20,512]{1,0:T(8,128)S(1)}, f32[16,512]{1,0:T(8,128)S(1)}) custom-call(s32[10]{0:T(128)S(1)} %copy-done.7, s32[10]{0:T(128)S(1)} %copy-done.8, f32[50,512]{1,0:T(8,128)S(1)} %get-tuple-element.22.rows_ref, ...), custom_call_target="tpu_custom_call" | custom-call | tf_op jit(solution)/shard_map/pallas_call | solution.py:230
  21.4 0.6 %collective-permute-start.9 = (f32[16,512]{1,0:T(8,128)S(1)}, f32[16,512]{1,0:T(8,128)S(1)}, u32[]{:S(2)}, u32[]{:S(2)}) collective-permute-start(f32[16,512]{1,0:T(8,128)S(1)} %get-tuple-element.34), channel_id=1, source_target_pairs={{0,8},{8,0},{16,24},{24,16},{1,9},{9,1},{17,25},{25,17},{2,10},{10... | collective-permute-start | bytes 98312 | tf_op jit(solution)/shard_map/ppermute | solution.py:199
  22.0 2.4 %collective-permute-start.8 = (f32[20,512]{1,0:T(8,128)S(1)}, f32[20,512]{1,0:T(8,128)S(1)}, u32[]{:S(2)}, u32[]{:S(2)}) collective-permute-start(f32[20,512]{1,0:T(8,128)S(1)} %get-tuple-element.33), channel_id=1, source_target_pairs={{0,1},{1,0},{2,3},{3,2},{4,5},{5,4},{6,7},{7,6},{8,9},{9,8},{10,11... | collective-permute-start | bytes 122888 | tf_op jit(solution)/shard_map/ppermute | solution.py:199
  24.4 1.5 %collective-permute-start.11 = (f32[16,512]{1,0:T(8,128)S(1)}, f32[16,512]{1,0:T(8,128)S(1)}, u32[]{:S(2)}, u32[]{:S(2)}) collective-permute-start(f32[16,512]{1,0:T(8,128)S(1)} %add.38), channel_id=1, source_target_pairs={{0,16},{8,24},{16,0},{24,8},{1,17},{9,25},{17,1},{25,9},{2,18},{10... | collective-permute-start | bytes 98312 | tf_op jit(solution)/shard_map/ppermute | solution.py:199
  25.9 0.6 %collective-permute-done.8 = f32[20,512]{1,0:T(8,128)S(1)} collective-permute-done((f32[20,512]{1,0:T(8,128)S(1)}, f32[20,512]{1,0:T(8,128)S(1)}, u32[]{:S(2)}, u32[]{:S(2)}) %collective-permute-start.8) | collective-permute-done | bytes 40992 | tf_op jit(solution)/shard_map/ppermute | solution.py:199
  26.5 1.6 %collective-permute-start.10 = (f32[20,512]{1,0:T(8,128)S(1)}, f32[20,512]{1,0:T(8,128)S(1)}, u32[]{:S(2)}, u32[]{:S(2)}) collective-permute-start(f32[20,512]{1,0:T(8,128)S(1)} %add.39), channel_id=1, source_target_pairs={{0,2},{1,3},{2,0},{3,1},{4,6},{5,7},{6,4},{7,5},{8,10},{9,11},{10,... | collective-permute-start | bytes 122888 | tf_op jit(solution)/shard_map/ppermute | solution.py:199
  28.1 0.7 %collective-permute-done.11 = f32[16,512]{1,0:T(8,128)S(1)} collective-permute-done((f32[16,512]{1,0:T(8,128)S(1)}, f32[16,512]{1,0:T(8,128)S(1)}, u32[]{:S(2)}, u32[]{:S(2)}) %collective-permute-start.11) | collective-permute-done | bytes 32800 | tf_op jit(solution)/shard_map/ppermute | solution.py:199
  29.3 1.3 %collective-permute-done.10 = f32[20,512]{1,0:T(8,128)S(1)} collective-permute-done((f32[20,512]{1,0:T(8,128)S(1)}, f32[20,512]{1,0:T(8,128)S(1)}, u32[]{:S(2)}, u32[]{:S(2)}) %collective-permute-start.10) | collective-permute-done | bytes 40992 | tf_op jit(solution)/shard_map/ppermute | solution.py:199
  30.7 2.3 %collective-permute-start.12 = (f32[20,512]{1,0:T(8,128)S(1)}, f32[20,512]{1,0:T(8,128)S(1)}, u32[]{:S(2)}, u32[]{:S(2)}) collective-permute-start(f32[20,512]{1,0:T(8,128)S(1)} %add.42), channel_id=1, source_target_pairs={{0,4},{1,5},{2,6},{3,7},{4,0},{5,1},{6,2},{7,3},{8,12},{9,13},{10,... | collective-permute-start | bytes 122888 | tf_op jit(solution)/shard_map/ppermute | solution.py:199
  33.0 3.4 %collective-permute-start.7 = (f32[50,512]{1,0:T(8,128)S(1)}, f32[50,512]{1,0:T(8,128)S(1)}, u32[]{:S(2)}, u32[]{:S(2)}) collective-permute-start(f32[50,512]{1,0:T(8,128)S(1)} %slice_add_fusion), channel_id=1, source_target_pairs={{0,1},{1,2},{2,3},{3,4},{4,5},{5,6},{6,7},{8,9},{9,10},{10,11},{11... | collective-permute-start | bytes 307208 | tf_op jit(solution)/shard_map/ppermute | solution.py:195
  36.5 3.3 %collective-permute-done.13.offcame_ref = f32[10,512]{1,0:T(8,128)S(1)} collective-permute-done((f32[10,512]{1,0:T(8,128)S(1)}, f32[10,512]{1,0:T(8,128)S(1)}, u32[]{:S(2)}, u32[]{:S(2)}) %collective-permute-start.13) | collective-permute-done | bytes 20512 | tf_op jit(solution)/shard_map/ppermute | solution.py:190
  39.8 1.6 %shard_map.162 = (f32[10,16,512]{2,1,0:T(8,128)}, f32[10,16,512]{2,1,0:T(8,128)}, f32[16,512]{1,0:T(8,128)}) custom-call(f32[50,512]{1,0:T(8,128)S(1)} %get-tuple-element.22.rows_ref, f32[210,512]{1,0:T(8,128)S(1)} %get-tuple-element.31.mine_ref, f32[210,512]{1,0:T(8,128)S(1)} %collective-permute-done.6.came_ref, ...), custom_call_target="tpu_custom_call" | custom-call | tf_op jit(solution)/shard_map/pallas_call | solution.py:230
  (49 shorter events, 1.1 us)
Async XLA Ops:
  1.6 4.1 %copy-start.5 = (f32[16,512]{1,0:T(8,128)S(1)}, f32[16,512]{1,0:T(8,128)}, u32[]{:S(2)}) copy-start(f32[16,512]{1,0:T(8,128)} %dual_ref.3) | copy-start | bytes 98308
  1.6 4.1 %copy-start.9 = (f32[10]{0:T(128)S(1)}, f32[10]{0:T(128)}, u32[]{:S(2)}) copy-start(f32[10]{0:T(128)} %eff_hbm.1) | copy-start | bytes 124
  1.6 4.1 %copy-start.10 = (f32[10]{0:T(128)S(1)}, f32[10]{0:T(128)}, u32[]{:S(2)}) copy-start(f32[10]{0:T(128)} %cap_hbm.1) | copy-start | bytes 124
  1.6 4.1 %copy-start.11 = (f32[10]{0:T(128)S(1)}, f32[10]{0:T(128)}, u32[]{:S(2)}) copy-start(f32[10]{0:T(128)} %start_hbm.1) | copy-start | bytes 124
  1.6 4.1 %copy-start.12 = (f32[10]{0:T(128)S(1)}, f32[10]{0:T(128)}, u32[]{:S(2)}) copy-start(f32[10]{0:T(128)} %low_hbm.1) | copy-start | bytes 124
  1.6 4.1 %copy-start.13 = (f32[10]{0:T(128)S(1)}, f32[10]{0:T(128)}, u32[]{:S(2)}) copy-start(f32[10]{0:T(128)} %high_hbm.1) | copy-start | bytes 124
  1.7 4.1 %copy-start.2 = (f32[10,16,512]{2,1,0:T(8,128)S(1)}, f32[10,16,512]{2,1,0:T(8,128)}, u32[]{:S(2)}) copy-start(f32[10,16,512]{2,1,0:T(8,128)} %rel_ref.3) | copy-start | bytes 983044
  1.7 4.0 %copy-start.3 = (f32[10,16,512]{2,1,0:T(8,128)S(1)}, f32[10,16,512]{2,1,0:T(8,128)}, u32[]{:S(2)}) copy-start(f32[10,16,512]{2,1,0:T(8,128)} %cost_ref.1) | copy-start | bytes 983044
  1.8 8.0 %copy-start.1 = (f32[10,16,512]{2,1,0:T(8,128)S(1)}, f32[10,16,512]{2,1,0:T(8,128)}, u32[]{:S(2)}) copy-start(f32[10,16,512]{2,1,0:T(8,128)} %sd_ref.5) | copy-start | bytes 983044
  1.8 8.0 %collective-permute-start = (f32[10,16,512]{2,1,0:T(8,128)S(1)}, f32[10,16,512]{2,1,0:T(8,128)S(1)}, u32[]{:S(2)}, u32[]{:S(2)}) collective-permute-start(f32[10,16,512]{2,1,0:T(8,128)S(1)} %shard_map.158), channel_id=1, source_target_pairs={{0,24},{8,0},{16,8},{24,16},{1,25},{9,1},{17,9},{25,17},{2,26},{10... | collective-permute-start | bytes 983048 | tf_op jit(solution)/shard_map/ppermute | solution.py:190
  4.2 3.9 %collective-permute-start.2 = (f32[10,512]{1,0:T(8,128)S(1)}, f32[10,512]{1,0:T(8,128)S(1)}, u32[]{:S(2)}, u32[]{:S(2)}) collective-permute-start(f32[10,512]{1,0:T(8,128)S(1)} %shard_map.157), channel_id=1, source_target_pairs={{0,1},{1,0},{2,3},{3,2},{4,5},{5,4},{6,7},{7,6},{8,9},{9,8},{10,11... | collective-permute-start | bytes 61448 | tf_op jit(solution)/shard_map/ppermute | solution.py:199
  8.1 6.6 %copy-start.4 = (f32[10,16,512]{2,1,0:T(8,128)S(1)}, f32[10,16,512]{2,1,0:T(8,128)}, u32[]{:S(2)}) copy-start(f32[10,16,512]{2,1,0:T(8,128)} %inflow_ref.1) | copy-start | bytes 983044
  8.1 4.0 %collective-permute-start.3 = (f32[10,512]{1,0:T(8,128)S(1)}, f32[10,512]{1,0:T(8,128)S(1)}, u32[]{:S(2)}, u32[]{:S(2)}) collective-permute-start(f32[10,512]{1,0:T(8,128)S(1)} %add.33), channel_id=1, source_target_pairs={{0,2},{1,3},{2,0},{3,1},{4,6},{5,7},{6,4},{7,5},{8,10},{9,11},{10,... | collective-permute-start | bytes 61448 | tf_op jit(solution)/shard_map/ppermute | solution.py:199
  12.1 5.1 %collective-permute-start.4 = (f32[10,512]{1,0:T(8,128)S(1)}, f32[10,512]{1,0:T(8,128)S(1)}, u32[]{:S(2)}, u32[]{:S(2)}) collective-permute-start(f32[10,512]{1,0:T(8,128)S(1)} %add.35), channel_id=1, source_target_pairs={{0,4},{1,5},{2,6},{3,7},{4,0},{5,1},{6,2},{7,3},{8,12},{9,13},{10,... | collective-permute-start | bytes 61448 | tf_op jit(solution)/shard_map/ppermute | solution.py:199
  14.8 4.8 %collective-permute-start.1 = (f32[50,512]{1,0:T(8,128)S(1)}, f32[50,512]{1,0:T(8,128)S(1)}, u32[]{:S(2)}, u32[]{:S(2)}) collective-permute-start(f32[50,512]{1,0:T(8,128)S(1)} %get-tuple-element.26), channel_id=1, source_target_pairs={{0,7},{1,0},{2,1},{3,2},{4,3},{5,4},{6,5},{7,6},{8,15},{9,8},{10,9... | collective-permute-start | bytes 307208 | tf_op jit(solution)/shard_map/ppermute | solution.py:190
  17.2 1.7 %collective-permute-start.5 = (f32[10,512]{1,0:T(8,128)S(1)}, f32[10,512]{1,0:T(8,128)S(1)}, u32[]{:S(2)}, u32[]{:S(2)}) collective-permute-start(f32[10,512]{1,0:T(8,128)S(1)} %select_add_fusion.1.own_ref), channel_id=1, source_target_pairs={{0,24},{8,0},{16,8},{24,16},{1,25},{9,1},{17,9},{25,17},{2,26},{10... | collective-permute-start | bytes 61448 | tf_op jit(solution)/shard_map/ppermute | solution.py:190
  21.2 8.1 %collective-permute-start.6 = (f32[210,512]{1,0:T(8,128)S(1)}, f32[210,512]{1,0:T(8,128)S(1)}, u32[]{:S(2)}, u32[]{:S(2)}) collective-permute-start(f32[210,512]{1,0:T(8,128)S(1)} %get-tuple-element.32), channel_id=1, source_target_pairs={{0,8},{8,16},{16,24},{24,0},{1,9},{9,17},{17,25},{25,1},{2,10},{10... | collective-permute-start | bytes 1290248 | tf_op jit(solution)/shard_map/ppermute | solution.py:190
  21.4 3.1 %collective-permute-start.9 = (f32[16,512]{1,0:T(8,128)S(1)}, f32[16,512]{1,0:T(8,128)S(1)}, u32[]{:S(2)}, u32[]{:S(2)}) collective-permute-start(f32[16,512]{1,0:T(8,128)S(1)} %get-tuple-element.34), channel_id=1, source_target_pairs={{0,8},{8,0},{16,24},{24,16},{1,9},{9,1},{17,25},{25,17},{2,10},{10... | collective-permute-start | bytes 98312 | tf_op jit(solution)/shard_map/ppermute | solution.py:199
  22.0 4.5 %collective-permute-start.8 = (f32[20,512]{1,0:T(8,128)S(1)}, f32[20,512]{1,0:T(8,128)S(1)}, u32[]{:S(2)}, u32[]{:S(2)}) collective-permute-start(f32[20,512]{1,0:T(8,128)S(1)} %get-tuple-element.33), channel_id=1, source_target_pairs={{0,1},{1,0},{2,3},{3,2},{4,5},{5,4},{6,7},{7,6},{8,9},{9,8},{10,11... | collective-permute-start | bytes 122888 | tf_op jit(solution)/shard_map/ppermute | solution.py:199
  24.4 4.4 %collective-permute-start.11 = (f32[16,512]{1,0:T(8,128)S(1)}, f32[16,512]{1,0:T(8,128)S(1)}, u32[]{:S(2)}, u32[]{:S(2)}) collective-permute-start(f32[16,512]{1,0:T(8,128)S(1)} %add.38), channel_id=1, source_target_pairs={{0,16},{8,24},{16,0},{24,8},{1,17},{9,25},{17,1},{25,9},{2,18},{10... | collective-permute-start | bytes 98312 | tf_op jit(solution)/shard_map/ppermute | solution.py:199
  26.5 4.2 %collective-permute-start.10 = (f32[20,512]{1,0:T(8,128)S(1)}, f32[20,512]{1,0:T(8,128)S(1)}, u32[]{:S(2)}, u32[]{:S(2)}) collective-permute-start(f32[20,512]{1,0:T(8,128)S(1)} %add.39), channel_id=1, source_target_pairs={{0,2},{1,3},{2,0},{3,1},{4,6},{5,7},{6,4},{7,5},{8,10},{9,11},{10,... | collective-permute-start | bytes 122888 | tf_op jit(solution)/shard_map/ppermute | solution.py:199
  30.7 5.7 %collective-permute-start.12 = (f32[20,512]{1,0:T(8,128)S(1)}, f32[20,512]{1,0:T(8,128)S(1)}, u32[]{:S(2)}, u32[]{:S(2)}) collective-permute-start(f32[20,512]{1,0:T(8,128)S(1)} %add.42), channel_id=1, source_target_pairs={{0,4},{1,5},{2,6},{3,7},{4,0},{5,1},{6,2},{7,3},{8,12},{9,13},{10,... | collective-permute-start | bytes 122888 | tf_op jit(solution)/shard_map/ppermute | solution.py:199
  33.0 6.8 %collective-permute-start.7 = (f32[50,512]{1,0:T(8,128)S(1)}, f32[50,512]{1,0:T(8,128)S(1)}, u32[]{:S(2)}, u32[]{:S(2)}) collective-permute-start(f32[50,512]{1,0:T(8,128)S(1)} %slice_add_fusion), channel_id=1, source_target_pairs={{0,1},{1,2},{2,3},{3,4},{4,5},{5,6},{6,7},{8,9},{9,10},{10,11},{11... | collective-permute-start | bytes 307208 | tf_op jit(solution)/shard_map/ppermute | solution.py:195
  36.4 3.4 %collective-permute-start.13 = (f32[10,512]{1,0:T(8,128)S(1)}, f32[10,512]{1,0:T(8,128)S(1)}, u32[]{:S(2)}, u32[]{:S(2)}) collective-permute-start(f32[10,512]{1,0:T(8,128)S(1)} %get-tuple-element.40), channel_id=1, source_target_pairs={{0,8},{8,16},{16,24},{24,0},{1,9},{9,17},{17,25},{25,1},{2,10},{10... | collective-permute-start | bytes 61448 | tf_op jit(solution)/shard_map/ppermute | solution.py:190
  (4 other events, 7.8 us)

commit v4 on v3

--- a/solution.py
+++ b/solution.py
@@ -93,7 +93,7 @@
         lead_ref[j] = later - sums_ref[j]
 
 
-def release_kernel(scale_time, scale_sum, down_ref, delay_ref, rows_ref, base_ref, lead_ref, w_ref, own_ref, next_ref, rel_ref, stock_ref, new_hbm, mine_ref, theirs_ref, tots_ref, power_ref, tot, new_ref, extra_ref, late_ref, sems):
+def release_kernel(scale_time, scale_sum, down_ref, delay_ref, rows_ref, base_ref, lead_ref, w_ref, own_ref, next_ref, rel_ref, stock_ref, new_ref, extra_ref, minerim_ref, theirsrim_ref, tots_ref, power_ref, tot, late_ref):
     count, hours, lanes = base_ref.shape
     for i in range(count):
         tot[i] = own_ref[i : i + 1]
@@ -104,46 +104,52 @@
     tot[...] = jnp.zeros_like(tot)
     power = jnp.zeros((hours, lanes), jnp.float32)
     more = lax.axis_index("hours") < lax.axis_size("hours") - 1
-    copies = [pltpu.make_async_copy(new_ref.at[j], new_hbm.at[j], sems.at[j]) for j in range(count)]
     totals = []
     for j in range(count):
         rim = jnp.where(more, w_ref[EDGE * j : EDGE * (j + 1)], 0.0)
         later = lead_ref[j] + (jnp.concatenate([jnp.zeros((hours - EDGE, lanes), jnp.float32), rim], 0) + shifts[j])
         new = jnp.clip(base_ref[j] - (primal_step * scale_time) * later, 0.0, rows_ref[count + j : count + j + 1])
         new_ref[j] = new
-        copies[j].start()
         extra = 2.0 * new - rel_ref[j]
         extra_ref[j] = extra
         power = power + (scale_sum * rows_ref[j : j + 1]) * extra
         totals.append(jnp.sum(extra, 0, keepdims=True))
     for j in range(count):
         tot[sinks[j]] = tot[sinks[j]] + totals[j]
+    late_ref[...] = jnp.zeros_like(late_ref)
+    place = lax.broadcasted_iota(jnp.int32, (RIM, lanes), 0)
+    for j in range(count):
+        lag = delay_ref[j]
+        last = extra_ref[j, hours - RIM :]
+        after = pltpu.roll(scan_rows(last, True)[0] - last, lag, 0)
+        late_ref[sinks[j]] = late_ref[sinks[j]] - jnp.where(place < lag, after, 0.0)
+    for i in range(count):
+        at = slice(EDGE * i, EDGE * (i + 1))
+        minerim_ref[at] = late_ref[i, 0:EDGE]
+        theirsrim_ref[at] = late_ref[count + i, 0:EDGE]
     for i in range(2 * count):
         change = tot[i]
         if i < count:
             change = change + (stock_ref[i, hours - 1 : hours] - totals[i])
         tots_ref[i : i + 1] = change
     power_ref[...] = power
-    windows(down_ref, delay_ref, extra_ref, stock_ref, mine_ref, theirs_ref, late_ref)
-    for copy in copies:
-        copy.wait()
-
-
-def windows(down_ref, delay_ref, extra_ref, stock_ref, mine_ref, theirs_ref, late_ref):
+
+
+def windows_kernel(down_ref, delay_ref, extra_ref, stock_ref, new_ref, new_hbm, mine_ref, theirs_ref, sem):
+    copy = pltpu.make_async_copy(new_ref, new_hbm, sem)
+    copy.start()
     count, hours, lanes = extra_ref.shape
     lags = [delay_ref[j] for j in range(count)]
     sinks = [sink_of(down_ref, j, count) for j in range(count)]
     mine_ref[...] = jnp.zeros_like(mine_ref)
     theirs_ref[...] = jnp.zeros_like(theirs_ref)
-    late_ref[...] = jnp.zeros_like(late_ref)
     place = lax.broadcasted_iota(jnp.int32, (RIM, lanes), 0)
     zeros = jnp.zeros((RIM, lanes), jnp.float32)
     for j in range(count):
-        sums, total = scan_rows(extra_ref[j], False)
+        sums, _ = scan_rows(extra_ref[j], False)
         arrived = place >= lags[j]
         tiles = [zeros] + turned([sums[k : k + RIM] for k in range(0, hours, RIM)], lags[j])
         window = jnp.concatenate([jnp.where(arrived, tiles[k + 1], tiles[k]) for k in range(hours // RIM)], 0)
-        late_ref[sinks[j]] = late_ref[sinks[j]] + jnp.where(arrived, 0.0, tiles[-1] - total)
 
         @pl.when(sinks[j] < count)
         def _():
@@ -157,32 +163,36 @@
 
         at = slice(j * hours, (j + 1) * hours)
         mine_ref[at] = mine_ref[at] + (stock_ref[j] - sums)
-    for i in range(count):
-        at = slice(count * hours + EDGE * i, count * hours + EDGE * (i + 1))
-        mine_ref[at] = late_ref[i, 0:EDGE]
-        theirs_ref[at] = late_ref[count + i, 0:EDGE]
-
-
-def storage_kernel(scale_time, rows_ref, mine_ref, came_ref, rim_ref, off_ref, offcame_ref, sd_ref, power_ref, dual_ref, demand_ref, sd_hbm, excess_hbm, dual_out, sd_out, excess_out, sems):
+    copy.wait()
+
+
+def storage_kernel(scale_time, rows_ref, mine_ref, came_ref, rim_ref, off_ref, sd_ref, power_ref, dual_ref, demand_ref, sd_hbm, excess_hbm, dual_hbm, sd_out, excess_out, dual_out, sems, dual_sem):
     count, hours, lanes = sd_ref.shape
     earlier = lax.axis_index("hours") > 0
     copies = [[pltpu.make_async_copy(src.at[i], dst.at[i], sems.at[k, i]) for i in range(count)] for k, (src, dst) in enumerate(((sd_out, sd_hbm), (excess_out, excess_hbm)))]
+    dual_out[...] = jnp.minimum(dual_ref[...] + dual_step * (power_ref[...] - demand_ref[...]), 0.0)
+    dual_copy = pltpu.make_async_copy(dual_out, dual_hbm, dual_sem)
+    dual_copy.start()
     for i in range(count):
         row = [rows_ref[k * count + i : k * count + i + 1] for k in range(5)]
-        at = slice(i * hours, (i + 1) * hours)
-        change = mine_ref[at] + came_ref[at] + (off_ref[i : i + 1] + offcame_ref[i : i + 1])
-        rim = jnp.concatenate([jnp.where(earlier, rim_ref[EDGE * i : EDGE * (i + 1)], 0.0), jnp.zeros((hours - EDGE, lanes), jnp.float32)], 0)
-        storage = row[2] + scale_time * (change + rim)
-        low, high = row[3], row[4]
-        dual = sd_ref[i]
-        sd_out[i] = dual + dual_step * storage - dual_step * jnp.clip(dual / dual_step + storage, low, high)
+        level, low, high = row[2] + scale_time * off_ref[i : i + 1], row[3], row[4]
+        low_dual, high_dual = dual_step * low, dual_step * high
+        for k in range(0, hours, RIM):
+            at = slice(i * hours + k, i * hours + k + RIM)
+            change = mine_ref[at] + came_ref[at]
+            if k == 0:
+                rim = jnp.where(earlier, rim_ref[EDGE * i : EDGE * (i + 1)], 0.0)
+                change = change + jnp.concatenate([rim, jnp.zeros((RIM - EDGE, lanes), jnp.float32)], 0)
+            storage = level + scale_time * change
+            ahead = sd_ref[i, k : k + RIM] + dual_step * storage
+            sd_out[i, k : k + RIM] = ahead - jnp.clip(ahead, low_dual, high_dual)
+            excess_out[i, k : k + RIM] = storage - jnp.clip(storage, low, high)
         copies[0][i].start()
-        excess_out[i] = storage - jnp.clip(storage, low, high)
         copies[1][i].start()
-    dual_out[...] = jnp.minimum(dual_ref[...] + dual_step * (power_ref[...] - demand_ref[...]), 0.0)
     for i in range(count):
         for k in range(2):
             copies[k][i].wait()
+    dual_copy.wait()
 
 
 def passed_along(block, axis, distance):
@@ -190,13 +200,14 @@
     return lax.ppermute(block, axis, [(i, (i + distance) % count) for i in range(count)])
 
 
-def handed_on(block, axis, distance):
-    devices = range(lax.axis_size(axis))
-    return lax.ppermute(block, axis, [(i, i + distance) for i in devices if i + distance in devices])
-
-
 def swapped(block, axis, bit):
     return lax.ppermute(block, axis, [(i, i ^ bit) for i in range(lax.axis_size(axis))])
+
+
+def all_summed(part, axis, done):
+    for step in range(done, (lax.axis_size(axis) - 1).bit_length()):
+        part = part + swapped(part, axis, 1 << step)
+    return part
 
 
 def offsets(total, axis, reverse, beside):
@@ -211,14 +222,6 @@
         result = result + jnp.where(low if reverse else ~low, other, 0.0)
         total = total + other
     return result
-
-
-def all_summed(part, axis):
-    count, first = lax.axis_size(axis), None
-    for step in range((count - 1).bit_length()):
-        part = part + swapped(part, axis, 1 << step)
-        first = part if first is None else first
-    return part, first
 
 
 SMEM = pl.BlockSpec(memory_space=pltpu.SMEM)
@@ -255,7 +258,8 @@
     count, hours, lanes = release.shape
     scale_time = 1.0 / (hours * lax.axis_size("hours"))
     scale_sum = 1.0 / math.sqrt(count * lax.axis_size("river"))
-    slab, flat, wide = (count, hours, lanes), (count, lanes), (count * (hours + EDGE), lanes)
+    slab, flat = (count, hours, lanes), (count, lanes)
+    wide, edges = (count * hours, lanes), (count * EDGE, lanes)
     dma = pltpu.SemaphoreType.DMA
 
     (total,) = call(totals_kernel, [(VMEM, storage_dual)], [(VMEM, flat)], [])
@@ -268,32 +272,63 @@
         [pltpu.SMEM((5, count), jnp.float32), dma((5,))],
     )
     (stock,) = call(stock_kernel, [(VMEM, inflow)], [(VMEM, slab)], [])
-    lead, w = call(
+    lead, w_sent = call(
         route_kernel,
         [(SMEM, downstream), (SMEM, travel_delay), (VMEM, storage_dual), (VMEM, sd_next)],
-        [(VMEM, slab), (VMEM, (EDGE * count, lanes))],
+        [(VMEM, slab), (VMEM, edges)],
         [(2 * count + 1, hours, lanes)],
     )
-    off_own = offsets(total, "hours", True, [(base, rows), (lead, w), (stock,)])
+    w = passed_along(w_sent, "hours", -1)
+    off_own = offsets(total, "hours", True, [(base, rows), (lead, w_sent), (stock,)])
     off_next = passed_along(off_own, "river", -1)
-    w = passed_along(w, "hours", -1)
-    release_new, mine, theirs, tots, power = call(
+
+    new, extra, rim_mine, rim_theirs, tots, power = call(
         functools.partial(release_kernel, scale_time, scale_sum),
         [(SMEM, downstream), (SMEM, travel_delay)] + [(VMEM, a) for a in (rows, base, lead, w, off_own, off_next, release, stock)],
-        [(HBM, slab), (VMEM, wide), (VMEM, wide), (VMEM, (2 * count, lanes)), (VMEM, (hours, lanes))],
-        [(2 * count + 1, 1, lanes), slab, slab, (2 * count + 1, RIM, lanes), dma((count,))],
-    )
-    supplied, first = all_summed(power, "river")
+        [(VMEM, slab), (VMEM, slab), (VMEM, edges), (VMEM, edges), (VMEM, (2 * count, lanes)), (VMEM, (hours, lanes))],
+        [(2 * count + 1, 1, lanes), (2 * count + 1, RIM, lanes)],
+    )
+    release_new, mine, theirs = call(
+        windows_kernel,
+        [(SMEM, downstream), (SMEM, travel_delay)] + [(VMEM, a) for a in (extra, stock, new)],
+        [(HBM, slab), (VMEM, wide), (VMEM, wide)],
+        [dma],
+    )
+
+    power = power + swapped(power, "river", 1)
+    pairs = lax.axis_size("river") == 4
+    if pairs:
+        moved = passed_along(jnp.concatenate([rim_theirs, power], 0), "river", 1)
+        late = rim_mine + moved[: count * EDGE]
+        whole = power + moved[count * EDGE :]
+    else:
+        late = rim_mine + passed_along(rim_theirs, "river", 1)
+    tot_came = passed_along(tots[count:], "river", 1)
+    tot_came, theirs, mine, power = lax.optimization_barrier((tot_came, theirs, mine, power))
     came = passed_along(theirs, "river", 1)
-    late = mine[count * hours :] + came[count * hours :]
-    edge = handed_on(late, "hours", 1)
-    off = offsets(tots, "hours", False, [(first,), (late, supplied)])
-    off_came = passed_along(off[count:], "river", 1)
+    edge = passed_along(late, "hours", 1)
+    place, steps = lax.axis_index("hours"), (lax.axis_size("hours") - 1).bit_length()
+    tot = tots[:count] + tot_came
+    off = jnp.zeros_like(tot)
+    for step in range(steps):
+        other = swapped(tot, "hours", 1 << step)
+        if step == 0:
+            other, late = lax.optimization_barrier((other, late))
+            if pairs:
+                supplied = jnp.where(lax.axis_index("river") % 2 == 0, whole, swapped(whole, "river", 1))
+            else:
+                supplied = all_summed(power, "river", 1)
+        if step == 1:
+            other, came = lax.optimization_barrier((other, came))
+        if step == steps - 1:
+            other, edge = lax.optimization_barrier((other, edge))
+        off = off + jnp.where((place & (1 << step)) != 0, other, 0.0)
+        tot = tot + other
     storage_dual_new, storage_excess, demand_dual_new = call(
         functools.partial(storage_kernel, scale_time),
-        [(VMEM, a) for a in (rows, mine, came, edge, off[:count], off_came, storage_dual, supplied, demand_dual, demand)],
-        [(HBM, slab), (HBM, slab), (VMEM, (hours, lanes))],
-        [slab, slab, dma((2, count))],
+        [(VMEM, a) for a in (rows, mine, came, edge, off, storage_dual, supplied, demand_dual, demand)],
+        [(HBM, slab), (HBM, slab), (HBM, (hours, lanes))],
+        [slab, slab, (hours, lanes), dma((2, count)), dma],
     )
     return (release_new, storage_dual_new, demand_dual_new, storage_excess)
 

time: 41.6 us -> 39.1 us (0.940)
  starting transfers between devices: 22.6 us -> 20.5 us
  waiting for transfers between devices: 12 us -> 11.5 us
    ppermute x1 -> x0, starting transfers between devices: 3.38 us -> none  [handed_on(): lax.ppermute(block, axis, [(i, i + distance) for i in devices if i + dist...]
    ppermute x5 -> x7, starting transfers between devices: 5.07 us -> 8.24 us  [passed_along(): lax.ppermute(block, axis, [(i, (i + distance) % count) for i in range(cou...]
    ppermute x8, starting transfers between devices: 14.2 us -> 12.3 us  [swapped(): lax.ppermute(block, axis, [(i, i ^ bit) for i in range(lax.axis_size(axis...]
    ppermute x8, waiting for transfers between devices: 5.75 us -> 4.52 us  [swapped(): lax.ppermute(block, axis, [(i, i ^ bit) for i in range(lax.axis_size(axis...]
    ppermute x5 -> x7, waiting for transfers between devices: 6.23 us -> 6.96 us  [passed_along(): lax.ppermute(block, axis, [(i, (i + distance) % count) for i in range(cou...]
    pallas_call x7 -> x8, Pallas kernels: 4.83 us -> 4.89 us  [call(): pl.pallas_call(body, out_shape=[jax.ShapeDtypeStruct(shape, jnp.float32)...]
  transfers between devices with their start and end apart: 14 -> 15, of which waited for: 9 -> 10; matrix products, arithmetic and copies ran while one was open for 0% -> 0% of each run, Pallas kernels for 4% -> 7%
where the time goes in v4:
time: 39.1 us; the launch traced here: 38.9 us
  starting transfers between devices  20.5 us (52%)
  waiting for transfers between devices  11.5 us (29%)
  Pallas kernels  4.89 us (13%)
  local copies, waits for them, and re-layouts  1.04 us (3%)
  between operations  0.88 us (2%)
    ppermute x8, starting transfers between devices, swapped(): lax.ppermute(block, axis, [(i, i ^ bit) for i in range(lax.axis_size(axis...  12.3 us
    ppermute x7, starting transfers between devices, passed_along(): lax.ppermute(block, axis, [(i, (i + distance) % count) for i in range(cou...  8.24 us
    ppermute x7, waiting for transfers between devices, passed_along(): lax.ppermute(block, axis, [(i, (i + distance) % count) for i in range(cou...  6.96 us
    pallas_call x8, Pallas kernels, call(): pl.pallas_call(body, out_shape=[jax.ShapeDtypeStruct(shape, jnp.float32)...  4.89 us
    ppermute x8, waiting for transfers between devices, swapped(): lax.ppermute(block, axis, [(i, i ^ bit) for i in range(lax.axis_size(axis...  4.52 us
    unnamed x28, local copies, waits for them, and re-layouts  1.03 us
  transfers between devices with their start and end apart: 15, of which 10 were waited for; matrix products, arithmetic and copies ran while one was open for 0% of the time, Pallas kernels for 7%

profile of v4, /device:TPU:0, one launch (start us, length us, event | category | flops | bytes accessed | tf_op | source)
XLA Modules:
  0.0 38.9 jit_solution(1799191359922728262)
XLA Ops:
  0.6 1.0 %copy-done = f32[10,16,512]{2,1,0:T(8,128)S(1)} copy-done((f32[10,16,512]{2,1,0:T(8,128)S(1)}, f32[10,16,512]{2,1,0:T(8,128)}, u32[]{:S(2)}) %copy-start) | copy-done | bytes 327704
  1.8 2.4 %collective-permute-start = (f32[10,16,512]{2,1,0:T(8,128)S(1)}, f32[10,16,512]{2,1,0:T(8,128)S(1)}, u32[]{:S(2)}, u32[]{:S(2)}) collective-permute-start(f32[10,16,512]{2,1,0:T(8,128)S(1)} %shard_map.158), channel_id=1, source_target_pairs={{0,24},{8,0},{16,8},{24,16},{1,25},{9,1},{17,9},{25,17},{2,26},{10... | collective-permute-start | bytes 983048 | tf_op jit(solution)/shard_map/ppermute | solution.py:200
  4.2 1.5 %collective-permute-start.2 = (f32[10,512]{1,0:T(8,128)S(1)}, f32[10,512]{1,0:T(8,128)S(1)}, u32[]{:S(2)}, u32[]{:S(2)}) collective-permute-start(f32[10,512]{1,0:T(8,128)S(1)} %shard_map.157), channel_id=1, source_target_pairs={{0,1},{1,0},{2,3},{3,2},{4,5},{5,4},{6,7},{7,6},{8,9},{9,8},{10,11... | collective-permute-start | bytes 61448 | tf_op jit(solution)/shard_map/ppermute | solution.py:204
  5.8 0.7 %shard_map.156 = (f32[10,16,512]{2,1,0:T(8,128)S(1)}, f32[50,512]{1,0:T(8,128)S(1)}) custom-call(f32[10]{0:T(128)S(1)} %copy-done.9, f32[10]{0:T(128)S(1)} %copy-done.10, f32[10]{0:T(128)S(1)} %copy-done.11, f32[10]{0:T(128)S(1)} %copy-done.12, f32[10]{0:T(128)S(1)} %copy-done.13, f32[10,16,512]{2,1,0:T(8,128)S(1)} %copy-done.2, ...), custom_call_target="tpu_custom_call" | custom-call | tf_op jit(solution)/shard_map/pallas_call | solution.py:233
  6.5 1.7 %collective-permute-done.2 = f32[10,512]{1,0:T(8,128)S(1)} collective-permute-done((f32[10,512]{1,0:T(8,128)S(1)}, f32[10,512]{1,0:T(8,128)S(1)}, u32[]{:S(2)}, u32[]{:S(2)}) %collective-permute-start.2) | collective-permute-done | bytes 20512 | tf_op jit(solution)/shard_map/ppermute | solution.py:204
  8.1 1.6 %collective-permute-start.3 = (f32[10,512]{1,0:T(8,128)S(1)}, f32[10,512]{1,0:T(8,128)S(1)}, u32[]{:S(2)}, u32[]{:S(2)}) collective-permute-start(f32[10,512]{1,0:T(8,128)S(1)} %add.40), channel_id=1, source_target_pairs={{0,2},{1,3},{2,0},{3,1},{4,6},{5,7},{6,4},{7,5},{8,10},{9,11},{10,... | collective-permute-start | bytes 61448 | tf_op jit(solution)/shard_map/ppermute | solution.py:204
  9.8 0.8 %shard_map.159 = (f32[10,16,512]{2,1,0:T(8,128)S(1)}, f32[50,512]{1,0:T(8,128)S(1)}) custom-call(s32[10]{0:T(128)S(1)} %copy-done.7, s32[10]{0:T(128)S(1)} %copy-done.8, f32[10,16,512]{2,1,0:T(8,128)S(1)} %copy-done.1, f32[10,16,512]{2,1,0:T(8,128)S(1)} %collective-permute-done.next_ref), custom_call_target="tpu_custom_call" | custom-call | tf_op jit(solution)/shard_map/pallas_call | solution.py:233
  10.6 1.5 %collective-permute-done.3 = f32[10,512]{1,0:T(8,128)S(1)} collective-permute-done((f32[10,512]{1,0:T(8,128)S(1)}, f32[10,512]{1,0:T(8,128)S(1)}, u32[]{:S(2)}, u32[]{:S(2)}) %collective-permute-start.3) | collective-permute-done | bytes 20512 | tf_op jit(solution)/shard_map/ppermute | solution.py:204
  12.1 2.6 %collective-permute-start.4 = (f32[10,512]{1,0:T(8,128)S(1)}, f32[10,512]{1,0:T(8,128)S(1)}, u32[]{:S(2)}, u32[]{:S(2)}) collective-permute-start(f32[10,512]{1,0:T(8,128)S(1)} %add.42), channel_id=1, source_target_pairs={{0,4},{1,5},{2,6},{3,7},{4,0},{5,1},{6,2},{7,3},{8,12},{9,13},{10,... | collective-permute-start | bytes 61448 | tf_op jit(solution)/shard_map/ppermute | solution.py:204
  14.8 2.4 %collective-permute-start.1 = (f32[50,512]{1,0:T(8,128)S(1)}, f32[50,512]{1,0:T(8,128)S(1)}, u32[]{:S(2)}, u32[]{:S(2)}) collective-permute-start(f32[50,512]{1,0:T(8,128)S(1)} %get-tuple-element.36), channel_id=1, source_target_pairs={{0,7},{1,0},{2,1},{3,2},{4,3},{5,4},{6,5},{7,6},{8,15},{9,8},{10,9... | collective-permute-start | bytes 307208 | tf_op jit(solution)/shard_map/ppermute | solution.py:200
  17.3 1.6 %collective-permute-done.5.next_ref = f32[10,512]{1,0:T(8,128)S(1)} collective-permute-done((f32[10,512]{1,0:T(8,128)S(1)}, f32[10,512]{1,0:T(8,128)S(1)}, u32[]{:S(2)}, u32[]{:S(2)}) %collective-permute-start.5) | collective-permute-done | bytes 20512 | tf_op jit(solution)/shard_map/ppermute | solution.py:200
  18.9 0.8 %collective-permute-done.1.w_ref = f32[50,512]{1,0:T(8,128)S(1)} collective-permute-done((f32[50,512]{1,0:T(8,128)S(1)}, f32[50,512]{1,0:T(8,128)S(1)}, u32[]{:S(2)}, u32[]{:S(2)}) %collective-permute-start.1) | collective-permute-done | bytes 102432 | tf_op jit(solution)/shard_map/ppermute | solution.py:200
  19.7 0.9 %shard_map.161 = (f32[10,16,512]{2,1,0:T(8,128)S(1)}, f32[10,16,512]{2,1,0:T(8,128)S(1)}, f32[50,512]{1,0:T(8,128)S(1)}, f32[50,512]{1,0:T(8,128)S(1)}, f32[20,512]{1,0:T(8,128)S(1)}, /*index=5*/f32[16,512]{1,0:T(8,128)S(1)}) custom-call(s32[10]{0:T(128)S(1)} %copy-done.7, s32[10]{0:T(128)S(1)} %copy-done.8, f32[50,512]{1,0:T(8,128)S(1)} %get-tuple-element.32.rows_ref, ...), custom_call_target="tpu_custom_call" | custom-call | tf_op jit(solution)/shard_map/pallas_call | solution.py:233
  21.2 1.3 %shard_map.162 = (f32[10,16,512]{2,1,0:T(8,128)}, f32[160,512]{1,0:T(8,128)S(1)}, f32[160,512]{1,0:T(8,128)S(1)}) custom-call(s32[10]{0:T(128)S(1)} %copy-done.7, s32[10]{0:T(128)S(1)} %copy-done.8, f32[10,16,512]{2,1,0:T(8,128)S(1)} %get-tuple-element.40.extra_ref, f32[10,16,512]{2,1,0:T(8,128)S(1)} %shard_map.160.stock_ref, ...), custom_call_target="tpu_custom_call" | custom-call | tf_op jit(solution)/shard_map/pallas_call | solution.py:233
  22.5 1.0 %collective-permute-start.9 = (f32[66,512]{1,0:T(8,128)S(1)}, f32[66,512]{1,0:T(8,128)S(1)}, u32[]{:S(2)}, u32[]{:S(2)}) collective-permute-start(f32[66,512]{1,0:T(8,128)S(1)} %pad_maximum_fusion), channel_id=1, source_target_pairs={{0,8},{8,16},{16,24},{24,0},{1,9},{9,17},{17,25},{25,1},{2,10},{10... | collective-permute-start | bytes 405512 | tf_op jit(solution)/shard_map/ppermute | solution.py:200
  23.5 0.6 %collective-permute-done.6 = f32[10,512]{1,0:T(8,128)S(1)} collective-permute-done((f32[10,512]{1,0:T(8,128)S(1)}, f32[10,512]{1,0:T(8,128)S(1)}, u32[]{:S(2)}, u32[]{:S(2)}) %collective-permute-start.6) | collective-permute-done | bytes 20512 | tf_op jit(solution)/shard_map/ppermute | solution.py:200
  24.1 2.4 %collective-permute-start.8 = (f32[10,512]{1,0:T(8,128)S(1)}, f32[10,512]{1,0:T(8,128)S(1)}, u32[]{:S(2)}, u32[]{:S(2)}) collective-permute-start(f32[10,512]{1,0:T(8,128)S(1)} %slice_add_fusion.2), channel_id=1, source_target_pairs={{0,1},{1,0},{2,3},{3,2},{4,5},{5,4},{6,7},{7,6},{8,9},{9,8},{10,11... | collective-permute-start | bytes 61448 | tf_op jit(solution)/shard_map/ppermute | solution.py:204
  27.4 1.0 %collective-permute-done.8 = f32[10,512]{1,0:T(8,128)S(1)} collective-permute-done((f32[10,512]{1,0:T(8,128)S(1)}, f32[10,512]{1,0:T(8,128)S(1)}, u32[]{:S(2)}, u32[]{:S(2)}) %collective-permute-start.8) | collective-permute-done | bytes 20512 | tf_op jit(solution)/shard_map/ppermute | solution.py:204
  28.4 1.6 %collective-permute-start.10 = (f32[10,512]{1,0:T(8,128)S(1)}, f32[10,512]{1,0:T(8,128)S(1)}, u32[]{:S(2)}, u32[]{:S(2)}) collective-permute-start(f32[10,512]{1,0:T(8,128)S(1)} %add.47), channel_id=1, source_target_pairs={{0,2},{1,3},{2,0},{3,1},{4,6},{5,7},{6,4},{7,5},{8,10},{9,11},{10,... | collective-permute-start | bytes 61448 | tf_op jit(solution)/shard_map/ppermute | solution.py:204
  30.0 2.0 %collective-permute-start.13 = (f32[50,512]{1,0:T(8,128)S(1)}, f32[50,512]{1,0:T(8,128)S(1)}, u32[]{:S(2)}, u32[]{:S(2)}) collective-permute-start(f32[50,512]{1,0:T(8,128)S(1)} %slice_add_fusion), channel_id=1, source_target_pairs={{0,1},{1,2},{2,3},{3,4},{4,5},{5,6},{6,7},{7,0},{8,9},{9,10},{10,1... | collective-permute-start | bytes 307208 | tf_op jit(solution)/shard_map/ppermute | solution.py:200
  32.3 0.7 %collective-permute-done.11.came_ref = f32[160,512]{1,0:T(8,128)S(1)} collective-permute-done((f32[160,512]{1,0:T(8,128)S(1)}, f32[160,512]{1,0:T(8,128)S(1)}, u32[]{:S(2)}, u32[]{:S(2)}) %collective-permute-start.11) | collective-permute-done | bytes 327712 | tf_op jit(solution)/shard_map/ppermute | solution.py:200
  33.0 2.2 %collective-permute-start.12 = (f32[10,512]{1,0:T(8,128)S(1)}, f32[10,512]{1,0:T(8,128)S(1)}, u32[]{:S(2)}, u32[]{:S(2)}) collective-permute-start(f32[10,512]{1,0:T(8,128)S(1)} %add.48), channel_id=1, source_target_pairs={{0,4},{1,5},{2,6},{3,7},{4,0},{5,1},{6,2},{7,3},{8,12},{9,13},{10,... | collective-permute-start | bytes 61448 | tf_op jit(solution)/shard_map/ppermute | solution.py:204
  35.2 2.6 %collective-permute-done.13.rim_ref = f32[50,512]{1,0:T(8,128)S(1)} collective-permute-done((f32[50,512]{1,0:T(8,128)S(1)}, f32[50,512]{1,0:T(8,128)S(1)}, u32[]{:S(2)}, u32[]{:S(2)}) %collective-permute-start.13) | collective-permute-done | bytes 102432 | tf_op jit(solution)/shard_map/ppermute | solution.py:200
  37.9 1.0 %shard_map.163 = (f32[10,16,512]{2,1,0:T(8,128)}, f32[10,16,512]{2,1,0:T(8,128)}, f32[16,512]{1,0:T(8,128)}) custom-call(f32[50,512]{1,0:T(8,128)S(1)} %get-tuple-element.32.rows_ref, f32[160,512]{1,0:T(8,128)S(1)} %get-tuple-element.47.mine_ref, f32[160,512]{1,0:T(8,128)S(1)} %collective-permute-done.11.came_ref, ...), custom_call_target="tpu_custom_call" | custom-call | tf_op jit(solution)/shard_map/pallas_call | solution.py:233
  (55 shorter events, 2.1 us)
Async XLA Ops:
  1.6 4.1 %copy-start.5 = (f32[16,512]{1,0:T(8,128)S(1)}, f32[16,512]{1,0:T(8,128)}, u32[]{:S(2)}) copy-start(f32[16,512]{1,0:T(8,128)} %dual_ref.3) | copy-start | bytes 98308
  1.6 4.1 %copy-start.9 = (f32[10]{0:T(128)S(1)}, f32[10]{0:T(128)}, u32[]{:S(2)}) copy-start(f32[10]{0:T(128)} %eff_hbm.1) | copy-start | bytes 124
  1.6 4.1 %copy-start.10 = (f32[10]{0:T(128)S(1)}, f32[10]{0:T(128)}, u32[]{:S(2)}) copy-start(f32[10]{0:T(128)} %cap_hbm.1) | copy-start | bytes 124
  1.6 4.1 %copy-start.11 = (f32[10]{0:T(128)S(1)}, f32[10]{0:T(128)}, u32[]{:S(2)}) copy-start(f32[10]{0:T(128)} %start_hbm.1) | copy-start | bytes 124
  1.6 4.1 %copy-start.12 = (f32[10]{0:T(128)S(1)}, f32[10]{0:T(128)}, u32[]{:S(2)}) copy-start(f32[10]{0:T(128)} %low_hbm.1) | copy-start | bytes 124
  1.6 4.1 %copy-start.13 = (f32[10]{0:T(128)S(1)}, f32[10]{0:T(128)}, u32[]{:S(2)}) copy-start(f32[10]{0:T(128)} %high_hbm.1) | copy-start | bytes 124
  1.7 4.1 %copy-start.2 = (f32[10,16,512]{2,1,0:T(8,128)S(1)}, f32[10,16,512]{2,1,0:T(8,128)}, u32[]{:S(2)}) copy-start(f32[10,16,512]{2,1,0:T(8,128)} %rel_ref.3) | copy-start | bytes 983044
  1.8 8.0 %copy-start.1 = (f32[10,16,512]{2,1,0:T(8,128)S(1)}, f32[10,16,512]{2,1,0:T(8,128)}, u32[]{:S(2)}) copy-start(f32[10,16,512]{2,1,0:T(8,128)} %sd_ref.5) | copy-start | bytes 983044
  1.8 8.0 %collective-permute-start = (f32[10,16,512]{2,1,0:T(8,128)S(1)}, f32[10,16,512]{2,1,0:T(8,128)S(1)}, u32[]{:S(2)}, u32[]{:S(2)}) collective-permute-start(f32[10,16,512]{2,1,0:T(8,128)S(1)} %shard_map.158), channel_id=1, source_target_pairs={{0,24},{8,0},{16,8},{24,16},{1,25},{9,1},{17,9},{25,17},{2,26},{10... | collective-permute-start | bytes 983048 | tf_op jit(solution)/shard_map/ppermute | solution.py:200
  4.2 3.9 %collective-permute-start.2 = (f32[10,512]{1,0:T(8,128)S(1)}, f32[10,512]{1,0:T(8,128)S(1)}, u32[]{:S(2)}, u32[]{:S(2)}) collective-permute-start(f32[10,512]{1,0:T(8,128)S(1)} %shard_map.157), channel_id=1, source_target_pairs={{0,1},{1,0},{2,3},{3,2},{4,5},{5,4},{6,7},{7,6},{8,9},{9,8},{10,11... | collective-permute-start | bytes 61448 | tf_op jit(solution)/shard_map/ppermute | solution.py:204
  8.1 6.6 %copy-start.4 = (f32[10,16,512]{2,1,0:T(8,128)S(1)}, f32[10,16,512]{2,1,0:T(8,128)}, u32[]{:S(2)}) copy-start(f32[10,16,512]{2,1,0:T(8,128)} %inflow_ref.1) | copy-start | bytes 983044
  8.1 4.0 %collective-permute-start.3 = (f32[10,512]{1,0:T(8,128)S(1)}, f32[10,512]{1,0:T(8,128)S(1)}, u32[]{:S(2)}, u32[]{:S(2)}) collective-permute-start(f32[10,512]{1,0:T(8,128)S(1)} %add.40), channel_id=1, source_target_pairs={{0,2},{1,3},{2,0},{3,1},{4,6},{5,7},{6,4},{7,5},{8,10},{9,11},{10,... | collective-permute-start | bytes 61448 | tf_op jit(solution)/shard_map/ppermute | solution.py:204
  12.1 5.1 %collective-permute-start.4 = (f32[10,512]{1,0:T(8,128)S(1)}, f32[10,512]{1,0:T(8,128)S(1)}, u32[]{:S(2)}, u32[]{:S(2)}) collective-permute-start(f32[10,512]{1,0:T(8,128)S(1)} %add.42), channel_id=1, source_target_pairs={{0,4},{1,5},{2,6},{3,7},{4,0},{5,1},{6,2},{7,3},{8,12},{9,13},{10,... | collective-permute-start | bytes 61448 | tf_op jit(solution)/shard_map/ppermute | solution.py:204
  14.8 4.8 %collective-permute-start.1 = (f32[50,512]{1,0:T(8,128)S(1)}, f32[50,512]{1,0:T(8,128)S(1)}, u32[]{:S(2)}, u32[]{:S(2)}) collective-permute-start(f32[50,512]{1,0:T(8,128)S(1)} %get-tuple-element.36), channel_id=1, source_target_pairs={{0,7},{1,0},{2,1},{3,2},{4,3},{5,4},{6,5},{7,6},{8,15},{9,8},{10,9... | collective-permute-start | bytes 307208 | tf_op jit(solution)/shard_map/ppermute | solution.py:200
  17.2 1.7 %collective-permute-start.5 = (f32[10,512]{1,0:T(8,128)S(1)}, f32[10,512]{1,0:T(8,128)S(1)}, u32[]{:S(2)}, u32[]{:S(2)}) collective-permute-start(f32[10,512]{1,0:T(8,128)S(1)} %select_add_fusion.1.own_ref), channel_id=1, source_target_pairs={{0,24},{8,0},{16,8},{24,16},{1,25},{9,1},{17,9},{25,17},{2,26},{10... | collective-permute-start | bytes 61448 | tf_op jit(solution)/shard_map/ppermute | solution.py:200
  20.6 1.9 %collective-permute-start.7 = (f32[16,512]{1,0:T(8,128)S(1)}, f32[16,512]{1,0:T(8,128)S(1)}, u32[]{:S(2)}, u32[]{:S(2)}) collective-permute-start(f32[16,512]{1,0:T(8,128)S(1)} %get-tuple-element.46), channel_id=1, source_target_pairs={{0,8},{8,0},{16,24},{24,16},{1,9},{9,1},{17,25},{25,17},{2,10},{10... | collective-permute-start | bytes 98312 | tf_op jit(solution)/shard_map/ppermute | solution.py:204
  20.8 3.3 %collective-permute-start.6 = (f32[10,512]{1,0:T(8,128)S(1)}, f32[10,512]{1,0:T(8,128)S(1)}, u32[]{:S(2)}, u32[]{:S(2)}) collective-permute-start(f32[10,512]{1,0:T(8,128)S(1)} %slice.12), channel_id=1, source_target_pairs={{0,8},{8,16},{16,24},{24,0},{1,9},{9,17},{17,25},{25,1},{2,10},{10... | collective-permute-start | bytes 61448 | tf_op jit(solution)/shard_map/ppermute | solution.py:200
  22.5 4.6 %collective-permute-start.9 = (f32[66,512]{1,0:T(8,128)S(1)}, f32[66,512]{1,0:T(8,128)S(1)}, u32[]{:S(2)}, u32[]{:S(2)}) collective-permute-start(f32[66,512]{1,0:T(8,128)S(1)} %pad_maximum_fusion), channel_id=1, source_target_pairs={{0,8},{8,16},{16,24},{24,0},{1,9},{9,17},{17,25},{25,1},{2,10},{10... | collective-permute-start | bytes 405512 | tf_op jit(solution)/shard_map/ppermute | solution.py:200
  24.1 4.3 %collective-permute-start.8 = (f32[10,512]{1,0:T(8,128)S(1)}, f32[10,512]{1,0:T(8,128)S(1)}, u32[]{:S(2)}, u32[]{:S(2)}) collective-permute-start(f32[10,512]{1,0:T(8,128)S(1)} %slice_add_fusion.2), channel_id=1, source_target_pairs={{0,1},{1,0},{2,3},{3,2},{4,5},{5,4},{6,7},{7,6},{8,9},{9,8},{10,11... | collective-permute-start | bytes 61448 | tf_op jit(solution)/shard_map/ppermute | solution.py:204
  26.5 6.5 %collective-permute-start.11 = (f32[160,512]{1,0:T(8,128)S(1)}, f32[160,512]{1,0:T(8,128)S(1)}, u32[]{:S(2)}, u32[]{:S(2)}) collective-permute-start(f32[160,512]{1,0:T(8,128)S(1)} %get-tuple-element.52), channel_id=1, source_target_pairs={{0,8},{8,16},{16,24},{24,0},{1,9},{9,17},{17,25},{25,1},{2,10},{10... | collective-permute-start | bytes 983048 | tf_op jit(solution)/shard_map/ppermute | solution.py:200
  27.1 8.1 %collective-permute-start.14 = (f32[16,512]{1,0:T(8,128)S(1)}, f32[16,512]{1,0:T(8,128)S(1)}, u32[]{:S(2)}, u32[]{:S(2)}) collective-permute-start(f32[16,512]{1,0:T(8,128)S(1)} %slice_add_fusion.1), channel_id=1, source_target_pairs={{0,8},{8,0},{16,24},{24,16},{1,9},{9,1},{17,25},{25,17},{2,10},{10... | collective-permute-start | bytes 98312 | tf_op jit(solution)/shard_map/ppermute | solution.py:204
  28.4 3.9 %collective-permute-start.10 = (f32[10,512]{1,0:T(8,128)S(1)}, f32[10,512]{1,0:T(8,128)S(1)}, u32[]{:S(2)}, u32[]{:S(2)}) collective-permute-start(f32[10,512]{1,0:T(8,128)S(1)} %add.47), channel_id=1, source_target_pairs={{0,2},{1,3},{2,0},{3,1},{4,6},{5,7},{6,4},{7,5},{8,10},{9,11},{10,... | collective-permute-start | bytes 61448 | tf_op jit(solution)/shard_map/ppermute | solution.py:204
  30.0 7.9 %collective-permute-start.13 = (f32[50,512]{1,0:T(8,128)S(1)}, f32[50,512]{1,0:T(8,128)S(1)}, u32[]{:S(2)}, u32[]{:S(2)}) collective-permute-start(f32[50,512]{1,0:T(8,128)S(1)} %slice_add_fusion), channel_id=1, source_target_pairs={{0,1},{1,2},{2,3},{3,4},{4,5},{5,6},{6,7},{7,0},{8,9},{9,10},{10,1... | collective-permute-start | bytes 307208 | tf_op jit(solution)/shard_map/ppermute | solution.py:200
  33.0 4.8 %collective-permute-start.12 = (f32[10,512]{1,0:T(8,128)S(1)}, f32[10,512]{1,0:T(8,128)S(1)}, u32[]{:S(2)}, u32[]{:S(2)}) collective-permute-start(f32[10,512]{1,0:T(8,128)S(1)} %add.48), channel_id=1, source_target_pairs={{0,4},{1,5},{2,6},{3,7},{4,0},{5,1},{6,2},{7,3},{8,12},{9,13},{10,... | collective-permute-start | bytes 61448 | tf_op jit(solution)/shard_map/ppermute | solution.py:204
  (5 other events, 11.0 us)

commit v5 on v4

--- a/solution.py
+++ b/solution.py
@@ -35,10 +35,11 @@
     return jnp.concatenate(tiles, 0), carry
 
 
-def sink_of(down_ref, j, count):
-    down = down_ref[j]
+def routes(down_ref, delay_ref):
+    down, delay = down_ref[...], delay_ref[...]
+    (count,) = down.shape
     base = lax.axis_index("river") * count
-    return jnp.where(down < 0, 2 * count, down - base)
+    return [jnp.where(down[j] < 0, 2 * count, down[j] - base) for j in range(count)], [delay[j] for j in range(count)]
 
 
 def turned(tiles, amount):
@@ -50,20 +51,15 @@
         total_ref[i : i + 1] = jnp.sum(sd_ref[i], 0, keepdims=True)
 
 
-def price_kernel(scale_sum, eff_hbm, cap_hbm, start_hbm, low_hbm, high_hbm, rel_ref, cost_ref, dual_ref, base_ref, rows_ref, scalars, sems):
+def price_kernel(scale_sum, eff_ref, cap_ref, start_ref, low_ref, high_ref, rel_ref, cost_ref, dual_ref, base_ref, rows_ref):
     count, hours, lanes = base_ref.shape
-    small = (eff_hbm, cap_hbm, start_hbm, low_hbm, high_hbm)
-    copies = [pltpu.make_async_copy(ref, scalars.at[k], sems.at[k]) for k, ref in enumerate(small)]
-    for copy in copies:
-        copy.start()
-    for copy in copies:
-        copy.wait()
     dual = dual_ref[...]
+    scalars = [ref[...] for ref in (eff_ref, cap_ref, start_ref, low_ref, high_ref)]
     for j in range(count):
         for k in range(5):
             at = k * count + j
-            rows_ref[at : at + 1] = jnp.full((1, lanes), scalars[k, j], jnp.float32)
-        base_ref[j] = rel_ref[j] - primal_step * (cost_ref[j] + (scale_sum * scalars[0, j]) * dual)
+            rows_ref[at : at + 1] = jnp.full((1, lanes), scalars[k][j], jnp.float32)
+        base_ref[j] = rel_ref[j] - primal_step * (cost_ref[j] + (scale_sum * scalars[0][j]) * dual)
 
 
 def stock_kernel(inflow_ref, stock_ref):
@@ -82,9 +78,10 @@
         sums_ref[i] = scan_rows(ref[k], True)[0]
     sums_ref[2 * count] = jnp.zeros((hours, lanes), jnp.float32)
     place = lax.broadcasted_iota(jnp.int32, (RIM, lanes), 0)
-    for j in range(count):
-        lag = delay_ref[j]
-        sink = sums_ref[sink_of(down_ref, j, count)]
+    sinks, lags = routes(down_ref, delay_ref)
+    for j in range(count):
+        lag = lags[j]
+        sink = sums_ref[sinks[j]]
         inside = place < RIM - lag
         tiles = turned([sink[k : k + RIM] for k in range(0, hours, RIM)], RIM - lag)
         w_ref[EDGE * j : EDGE * (j + 1)] = jnp.where(inside, 0.0, tiles[0] - sink[0:1])[RIM - EDGE :]
@@ -99,7 +96,7 @@
         tot[i] = own_ref[i : i + 1]
         tot[count + i] = next_ref[i : i + 1]
     tot[2 * count] = jnp.zeros((1, lanes), jnp.float32)
-    sinks = [sink_of(down_ref, j, count) for j in range(count)]
+    sinks, lags = routes(down_ref, delay_ref)
     shifts = [tot[sinks[j]] - tot[j] for j in range(count)]
     tot[...] = jnp.zeros_like(tot)
     power = jnp.zeros((hours, lanes), jnp.float32)
@@ -119,7 +116,7 @@
     late_ref[...] = jnp.zeros_like(late_ref)
     place = lax.broadcasted_iota(jnp.int32, (RIM, lanes), 0)
     for j in range(count):
-        lag = delay_ref[j]
+        lag = lags[j]
         last = extra_ref[j, hours - RIM :]
         after = pltpu.roll(scan_rows(last, True)[0] - last, lag, 0)
         late_ref[sinks[j]] = late_ref[sinks[j]] - jnp.where(place < lag, after, 0.0)
@@ -139,8 +136,7 @@
     copy = pltpu.make_async_copy(new_ref, new_hbm, sem)
     copy.start()
     count, hours, lanes = extra_ref.shape
-    lags = [delay_ref[j] for j in range(count)]
-    sinks = [sink_of(down_ref, j, count) for j in range(count)]
+    sinks, lags = routes(down_ref, delay_ref)
     mine_ref[...] = jnp.zeros_like(mine_ref)
     theirs_ref[...] = jnp.zeros_like(theirs_ref)
     place = lax.broadcasted_iota(jnp.int32, (RIM, lanes), 0)
@@ -224,7 +220,6 @@
     return result
 
 
-SMEM = pl.BlockSpec(memory_space=pltpu.SMEM)
 VMEM = pl.BlockSpec(memory_space=pltpu.VMEM)
 HBM = pl.BlockSpec(memory_space=pltpu.HBM)
 
@@ -267,14 +262,14 @@
     sd_next = passed_along(sd_sent, "river", -1)
     base, rows = call(
         functools.partial(price_kernel, scale_sum),
-        [(HBM, a) for a in (efficiency, release_cap, storage_start, storage_low, storage_high)] + [(VMEM, a) for a in (release, cost, demand_dual)],
+        [(VMEM, a) for a in (efficiency, release_cap, storage_start, storage_low, storage_high, release, cost, demand_dual)],
         [(VMEM, slab), (VMEM, (5 * count, lanes))],
-        [pltpu.SMEM((5, count), jnp.float32), dma((5,))],
+        [],
     )
     (stock,) = call(stock_kernel, [(VMEM, inflow)], [(VMEM, slab)], [])
     lead, w_sent = call(
         route_kernel,
-        [(SMEM, downstream), (SMEM, travel_delay), (VMEM, storage_dual), (VMEM, sd_next)],
+        [(VMEM, a) for a in (downstream, travel_delay, storage_dual, sd_next)],
         [(VMEM, slab), (VMEM, edges)],
         [(2 * count + 1, hours, lanes)],
     )
@@ -284,17 +279,18 @@
 
     new, extra, rim_mine, rim_theirs, tots, power = call(
         functools.partial(release_kernel, scale_time, scale_sum),
-        [(SMEM, downstream), (SMEM, travel_delay)] + [(VMEM, a) for a in (rows, base, lead, w, off_own, off_next, release, stock)],
+        [(VMEM, a) for a in (downstream, travel_delay, rows, base, lead, w, off_own, off_next, release, stock)],
         [(VMEM, slab), (VMEM, slab), (VMEM, edges), (VMEM, edges), (VMEM, (2 * count, lanes)), (VMEM, (hours, lanes))],
         [(2 * count + 1, 1, lanes), (2 * count + 1, RIM, lanes)],
     )
     release_new, mine, theirs = call(
         windows_kernel,
-        [(SMEM, downstream), (SMEM, travel_delay)] + [(VMEM, a) for a in (extra, stock, new)],
+        [(VMEM, a) for a in (downstream, travel_delay, extra, stock, new)],
         [(HBM, slab), (VMEM, wide), (VMEM, wide)],
         [dma],
     )
 
+    tot_came = passed_along(tots[count:], "river", 1)
     power = power + swapped(power, "river", 1)
     pairs = lax.axis_size("river") == 4
     if pairs:
@@ -303,7 +299,6 @@
         whole = power + moved[count * EDGE :]
     else:
         late = rim_mine + passed_along(rim_theirs, "river", 1)
-    tot_came = passed_along(tots[count:], "river", 1)
     tot_came, theirs, mine, power = lax.optimization_barrier((tot_came, theirs, mine, power))
     came = passed_along(theirs, "river", 1)
     edge = passed_along(late, "hours", 1)

time: 39.1 us -> 38.5 us (0.985)
  Pallas kernels: 4.89 us -> 2.84 us
  waiting for transfers between devices: 11.5 us -> 12.5 us
  starting transfers between devices: 20.5 us -> 21 us
    pallas_call x8, Pallas kernels: 4.89 us -> 2.84 us  [call(): pl.pallas_call(body, out_shape=[jax.ShapeDtypeStruct(shape, jnp.float32)...]
    ppermute x8, waiting for transfers between devices: 4.52 us -> 5.54 us  [swapped(): lax.ppermute(block, axis, [(i, i ^ bit) for i in range(lax.axis_size(axis...]
    ppermute x8, starting transfers between devices: 12.3 us -> 12.8 us  [swapped(): lax.ppermute(block, axis, [(i, i ^ bit) for i in range(lax.axis_size(axis...]
  transfers between devices with their start and end apart: 15 -> 15, of which waited for: 10 -> 10; matrix products, arithmetic and copies ran while one was open for 0% -> 0% of each run, Pallas kernels for 7% -> 3%
where the time goes in v5:
time: 38.5 us; the launch traced here: 38.4 us
  starting transfers between devices  21 us (55%)
  waiting for transfers between devices  12.5 us (32%)
  Pallas kernels  2.84 us (7%)
  local copies, waits for them, and re-layouts  1.04 us (3%)
  between operations  0.88 us (2%)
    ppermute x8, starting transfers between devices, swapped(): lax.ppermute(block, axis, [(i, i ^ bit) for i in range(lax.axis_size(axis...  12.8 us
    ppermute x7, starting transfers between devices, passed_along(): lax.ppermute(block, axis, [(i, (i + distance) % count) for i in range(cou...  8.24 us
    ppermute x7, waiting for transfers between devices, passed_along(): lax.ppermute(block, axis, [(i, (i + distance) % count) for i in range(cou...  6.96 us
    ppermute x8, waiting for transfers between devices, swapped(): lax.ppermute(block, axis, [(i, i ^ bit) for i in range(lax.axis_size(axis...  5.54 us
    pallas_call x8, Pallas kernels, call(): pl.pallas_call(body, out_shape=[jax.ShapeDtypeStruct(shape, jnp.float32)...  2.84 us
    unnamed x28, local copies, waits for them, and re-layouts  1.03 us
  transfers between devices with their start and end apart: 15, of which 10 were waited for; matrix products, arithmetic and copies ran while one was open for 0% of the time, Pallas kernels for 3%

profile of v5, /device:TPU:0, one launch (start us, length us, event | category | flops | bytes accessed | tf_op | source)
XLA Modules:
  0.0 38.4 jit_solution(15029908730164080069)
XLA Ops:
  0.6 1.0 %copy-done = f32[10,16,512]{2,1,0:T(8,128)S(1)} copy-done((f32[10,16,512]{2,1,0:T(8,128)S(1)}, f32[10,16,512]{2,1,0:T(8,128)}, u32[]{:S(2)}) %copy-start) | copy-done | bytes 327704
  1.8 2.4 %collective-permute-start = (f32[10,16,512]{2,1,0:T(8,128)S(1)}, f32[10,16,512]{2,1,0:T(8,128)S(1)}, u32[]{:S(2)}, u32[]{:S(2)}) collective-permute-start(f32[10,16,512]{2,1,0:T(8,128)S(1)} %shard_map.158), channel_id=1, source_target_pairs={{0,24},{8,0},{16,8},{24,16},{1,25},{9,1},{17,9},{25,17},{2,26},{10... | collective-permute-start | bytes 983048 | tf_op jit(solution)/shard_map/ppermute | solution.py:196
  4.2 1.5 %collective-permute-start.2 = (f32[10,512]{1,0:T(8,128)S(1)}, f32[10,512]{1,0:T(8,128)S(1)}, u32[]{:S(2)}, u32[]{:S(2)}) collective-permute-start(f32[10,512]{1,0:T(8,128)S(1)} %shard_map.157), channel_id=1, source_target_pairs={{0,1},{1,0},{2,3},{3,2},{4,5},{5,4},{6,7},{7,6},{8,9},{9,8},{10,11... | collective-permute-start | bytes 61448 | tf_op jit(solution)/shard_map/ppermute | solution.py:200
  5.9 2.2 %collective-permute-done.2 = f32[10,512]{1,0:T(8,128)S(1)} collective-permute-done((f32[10,512]{1,0:T(8,128)S(1)}, f32[10,512]{1,0:T(8,128)S(1)}, u32[]{:S(2)}, u32[]{:S(2)}) %collective-permute-start.2) | collective-permute-done | bytes 20512 | tf_op jit(solution)/shard_map/ppermute | solution.py:200
  8.1 1.6 %collective-permute-start.3 = (f32[10,512]{1,0:T(8,128)S(1)}, f32[10,512]{1,0:T(8,128)S(1)}, u32[]{:S(2)}, u32[]{:S(2)}) collective-permute-start(f32[10,512]{1,0:T(8,128)S(1)} %add.40), channel_id=1, source_target_pairs={{0,2},{1,3},{2,0},{3,1},{4,6},{5,7},{6,4},{7,5},{8,10},{9,11},{10,... | collective-permute-start | bytes 61448 | tf_op jit(solution)/shard_map/ppermute | solution.py:200
  10.1 2.0 %collective-permute-done.3 = f32[10,512]{1,0:T(8,128)S(1)} collective-permute-done((f32[10,512]{1,0:T(8,128)S(1)}, f32[10,512]{1,0:T(8,128)S(1)}, u32[]{:S(2)}, u32[]{:S(2)}) %collective-permute-start.3) | collective-permute-done | bytes 20512 | tf_op jit(solution)/shard_map/ppermute | solution.py:200
  12.1 2.6 %collective-permute-start.4 = (f32[10,512]{1,0:T(8,128)S(1)}, f32[10,512]{1,0:T(8,128)S(1)}, u32[]{:S(2)}, u32[]{:S(2)}) collective-permute-start(f32[10,512]{1,0:T(8,128)S(1)} %add.42), channel_id=1, source_target_pairs={{0,4},{1,5},{2,6},{3,7},{4,0},{5,1},{6,2},{7,3},{8,12},{9,13},{10,... | collective-permute-start | bytes 61448 | tf_op jit(solution)/shard_map/ppermute | solution.py:200
  14.8 2.4 %collective-permute-start.1 = (f32[50,512]{1,0:T(8,128)S(1)}, f32[50,512]{1,0:T(8,128)S(1)}, u32[]{:S(2)}, u32[]{:S(2)}) collective-permute-start(f32[50,512]{1,0:T(8,128)S(1)} %get-tuple-element.36), channel_id=1, source_target_pairs={{0,7},{1,0},{2,1},{3,2},{4,3},{5,4},{6,5},{7,6},{8,15},{9,8},{10,9... | collective-permute-start | bytes 307208 | tf_op jit(solution)/shard_map/ppermute | solution.py:196
  17.3 1.6 %collective-permute-done.5.next_ref = f32[10,512]{1,0:T(8,128)S(1)} collective-permute-done((f32[10,512]{1,0:T(8,128)S(1)}, f32[10,512]{1,0:T(8,128)S(1)}, u32[]{:S(2)}, u32[]{:S(2)}) %collective-permute-start.5) | collective-permute-done | bytes 20512 | tf_op jit(solution)/shard_map/ppermute | solution.py:196
  18.9 0.8 %collective-permute-done.1.w_ref = f32[50,512]{1,0:T(8,128)S(1)} collective-permute-done((f32[50,512]{1,0:T(8,128)S(1)}, f32[50,512]{1,0:T(8,128)S(1)}, u32[]{:S(2)}, u32[]{:S(2)}) %collective-permute-start.1) | collective-permute-done | bytes 102432 | tf_op jit(solution)/shard_map/ppermute | solution.py:196
  19.7 0.4 %shard_map.161 = (f32[10,16,512]{2,1,0:T(8,128)S(1)}, f32[10,16,512]{2,1,0:T(8,128)S(1)}, f32[50,512]{1,0:T(8,128)S(1)}, f32[50,512]{1,0:T(8,128)S(1)}, f32[20,512]{1,0:T(8,128)S(1)}, /*index=5*/f32[16,512]{1,0:T(8,128)S(1)}) custom-call(s32[10]{0:T(128)S(1)} %copy-done.7, s32[10]{0:T(128)S(1)} %copy-done.8, f32[50,512]{1,0:T(8,128)S(1)} %get-tuple-element.32.rows_ref, ...), custom_call_target="tpu_custom_call" | custom-call | tf_op jit(solution)/shard_map/pallas_call | solution.py:228
  20.3 0.4 %collective-permute-start.6 = (f32[10,512]{1,0:T(8,128)S(1)}, f32[10,512]{1,0:T(8,128)S(1)}, u32[]{:S(2)}, u32[]{:S(2)}) collective-permute-start(f32[10,512]{1,0:T(8,128)S(1)} %slice.12), channel_id=1, source_target_pairs={{0,8},{8,16},{16,24},{24,0},{1,9},{9,17},{17,25},{25,1},{2,10},{10... | collective-permute-start | bytes 61448 | tf_op jit(solution)/shard_map/ppermute | solution.py:196
  20.7 0.7 %shard_map.162 = (f32[10,16,512]{2,1,0:T(8,128)}, f32[160,512]{1,0:T(8,128)S(1)}, f32[160,512]{1,0:T(8,128)S(1)}) custom-call(s32[10]{0:T(128)S(1)} %copy-done.7, s32[10]{0:T(128)S(1)} %copy-done.8, f32[10,16,512]{2,1,0:T(8,128)S(1)} %get-tuple-element.40.extra_ref, f32[10,16,512]{2,1,0:T(8,128)S(1)} %shard_map.160.stock_ref, ...), custom_call_target="tpu_custom_call" | custom-call | tf_op jit(solution)/shard_map/pallas_call | solution.py:228
  21.5 1.0 %collective-permute-start.9 = (f32[66,512]{1,0:T(8,128)S(1)}, f32[66,512]{1,0:T(8,128)S(1)}, u32[]{:S(2)}, u32[]{:S(2)}) collective-permute-start(f32[66,512]{1,0:T(8,128)S(1)} %pad_maximum_fusion), channel_id=1, source_target_pairs={{0,8},{8,16},{16,24},{24,0},{1,9},{9,17},{17,25},{25,1},{2,10},{10... | collective-permute-start | bytes 405512 | tf_op jit(solution)/shard_map/ppermute | solution.py:196
  22.5 1.2 %collective-permute-done.6 = f32[10,512]{1,0:T(8,128)S(1)} collective-permute-done((f32[10,512]{1,0:T(8,128)S(1)}, f32[10,512]{1,0:T(8,128)S(1)}, u32[]{:S(2)}, u32[]{:S(2)}) %collective-permute-start.6) | collective-permute-done | bytes 20512 | tf_op jit(solution)/shard_map/ppermute | solution.py:196
  23.6 2.4 %collective-permute-start.8 = (f32[10,512]{1,0:T(8,128)S(1)}, f32[10,512]{1,0:T(8,128)S(1)}, u32[]{:S(2)}, u32[]{:S(2)}) collective-permute-start(f32[10,512]{1,0:T(8,128)S(1)} %slice_add_fusion.2), channel_id=1, source_target_pairs={{0,1},{1,0},{2,3},{3,2},{4,5},{5,4},{6,7},{7,6},{8,9},{9,8},{10,11... | collective-permute-start | bytes 61448 | tf_op jit(solution)/shard_map/ppermute | solution.py:200
  26.1 0.7 %collective-permute-start.14 = (f32[16,512]{1,0:T(8,128)S(1)}, f32[16,512]{1,0:T(8,128)S(1)}, u32[]{:S(2)}, u32[]{:S(2)}) collective-permute-start(f32[16,512]{1,0:T(8,128)S(1)} %slice_add_fusion.1), channel_id=1, source_target_pairs={{0,8},{8,0},{16,24},{24,16},{1,9},{9,1},{17,25},{25,17},{2,10},{10... | collective-permute-start | bytes 98312 | tf_op jit(solution)/shard_map/ppermute | solution.py:200
  26.9 1.0 %collective-permute-done.8 = f32[10,512]{1,0:T(8,128)S(1)} collective-permute-done((f32[10,512]{1,0:T(8,128)S(1)}, f32[10,512]{1,0:T(8,128)S(1)}, u32[]{:S(2)}, u32[]{:S(2)}) %collective-permute-start.8) | collective-permute-done | bytes 20512 | tf_op jit(solution)/shard_map/ppermute | solution.py:200
  27.9 1.6 %collective-permute-start.10 = (f32[10,512]{1,0:T(8,128)S(1)}, f32[10,512]{1,0:T(8,128)S(1)}, u32[]{:S(2)}, u32[]{:S(2)}) collective-permute-start(f32[10,512]{1,0:T(8,128)S(1)} %add.47), channel_id=1, source_target_pairs={{0,2},{1,3},{2,0},{3,1},{4,6},{5,7},{6,4},{7,5},{8,10},{9,11},{10,... | collective-permute-start | bytes 61448 | tf_op jit(solution)/shard_map/ppermute | solution.py:200
  29.5 2.0 %collective-permute-start.13 = (f32[50,512]{1,0:T(8,128)S(1)}, f32[50,512]{1,0:T(8,128)S(1)}, u32[]{:S(2)}, u32[]{:S(2)}) collective-permute-start(f32[50,512]{1,0:T(8,128)S(1)} %slice_add_fusion), channel_id=1, source_target_pairs={{0,1},{1,2},{2,3},{3,4},{4,5},{5,6},{6,7},{7,0},{8,9},{9,10},{10,1... | collective-permute-start | bytes 307208 | tf_op jit(solution)/shard_map/ppermute | solution.py:196
  31.8 0.7 %collective-permute-done.11.came_ref = f32[160,512]{1,0:T(8,128)S(1)} collective-permute-done((f32[160,512]{1,0:T(8,128)S(1)}, f32[160,512]{1,0:T(8,128)S(1)}, u32[]{:S(2)}, u32[]{:S(2)}) %collective-permute-start.11) | collective-permute-done | bytes 327712 | tf_op jit(solution)/shard_map/ppermute | solution.py:196
  32.5 2.2 %collective-permute-start.12 = (f32[10,512]{1,0:T(8,128)S(1)}, f32[10,512]{1,0:T(8,128)S(1)}, u32[]{:S(2)}, u32[]{:S(2)}) collective-permute-start(f32[10,512]{1,0:T(8,128)S(1)} %add.48), channel_id=1, source_target_pairs={{0,4},{1,5},{2,6},{3,7},{4,0},{5,1},{6,2},{7,3},{8,12},{9,13},{10,... | collective-permute-start | bytes 61448 | tf_op jit(solution)/shard_map/ppermute | solution.py:200
  34.7 2.6 %collective-permute-done.13.rim_ref = f32[50,512]{1,0:T(8,128)S(1)} collective-permute-done((f32[50,512]{1,0:T(8,128)S(1)}, f32[50,512]{1,0:T(8,128)S(1)}, u32[]{:S(2)}, u32[]{:S(2)}) %collective-permute-start.13) | collective-permute-done | bytes 102432 | tf_op jit(solution)/shard_map/ppermute | solution.py:196
  37.3 1.0 %shard_map.163 = (f32[10,16,512]{2,1,0:T(8,128)}, f32[10,16,512]{2,1,0:T(8,128)}, f32[16,512]{1,0:T(8,128)}) custom-call(f32[50,512]{1,0:T(8,128)S(1)} %get-tuple-element.32.rows_ref, f32[160,512]{1,0:T(8,128)S(1)} %get-tuple-element.47.mine_ref, f32[160,512]{1,0:T(8,128)S(1)} %collective-permute-done.11.came_ref, ...), custom_call_target="tpu_custom_call" | custom-call | tf_op jit(solution)/shard_map/pallas_call | solution.py:228
  (55 shorter events, 1.5 us)
Async XLA Ops:
  1.6 4.1 %copy-start.5 = (f32[16,512]{1,0:T(8,128)S(1)}, f32[16,512]{1,0:T(8,128)}, u32[]{:S(2)}) copy-start(f32[16,512]{1,0:T(8,128)} %dual_ref.3) | copy-start | bytes 98308
  1.6 4.1 %copy-start.9 = (f32[10]{0:T(128)S(1)}, f32[10]{0:T(128)}, u32[]{:S(2)}) copy-start(f32[10]{0:T(128)} %eff_ref.1) | copy-start | bytes 124
  1.6 4.1 %copy-start.10 = (f32[10]{0:T(128)S(1)}, f32[10]{0:T(128)}, u32[]{:S(2)}) copy-start(f32[10]{0:T(128)} %cap_ref.1) | copy-start | bytes 124
  1.6 4.1 %copy-start.11 = (f32[10]{0:T(128)S(1)}, f32[10]{0:T(128)}, u32[]{:S(2)}) copy-start(f32[10]{0:T(128)} %start_ref.1) | copy-start | bytes 124
  1.6 4.1 %copy-start.12 = (f32[10]{0:T(128)S(1)}, f32[10]{0:T(128)}, u32[]{:S(2)}) copy-start(f32[10]{0:T(128)} %low_ref.1) | copy-start | bytes 124
  1.6 4.1 %copy-start.13 = (f32[10]{0:T(128)S(1)}, f32[10]{0:T(128)}, u32[]{:S(2)}) copy-start(f32[10]{0:T(128)} %high_ref.1) | copy-start | bytes 124
  1.7 4.1 %copy-start.2 = (f32[10,16,512]{2,1,0:T(8,128)S(1)}, f32[10,16,512]{2,1,0:T(8,128)}, u32[]{:S(2)}) copy-start(f32[10,16,512]{2,1,0:T(8,128)} %rel_ref.3) | copy-start | bytes 983044
  1.8 8.0 %copy-start.1 = (f32[10,16,512]{2,1,0:T(8,128)S(1)}, f32[10,16,512]{2,1,0:T(8,128)}, u32[]{:S(2)}) copy-start(f32[10,16,512]{2,1,0:T(8,128)} %sd_ref.5) | copy-start | bytes 983044
  1.8 8.0 %collective-permute-start = (f32[10,16,512]{2,1,0:T(8,128)S(1)}, f32[10,16,512]{2,1,0:T(8,128)S(1)}, u32[]{:S(2)}, u32[]{:S(2)}) collective-permute-start(f32[10,16,512]{2,1,0:T(8,128)S(1)} %shard_map.158), channel_id=1, source_target_pairs={{0,24},{8,0},{16,8},{24,16},{1,25},{9,1},{17,9},{25,17},{2,26},{10... | collective-permute-start | bytes 983048 | tf_op jit(solution)/shard_map/ppermute | solution.py:196
  4.2 3.9 %collective-permute-start.2 = (f32[10,512]{1,0:T(8,128)S(1)}, f32[10,512]{1,0:T(8,128)S(1)}, u32[]{:S(2)}, u32[]{:S(2)}) collective-permute-start(f32[10,512]{1,0:T(8,128)S(1)} %shard_map.157), channel_id=1, source_target_pairs={{0,1},{1,0},{2,3},{3,2},{4,5},{5,4},{6,7},{7,6},{8,9},{9,8},{10,11... | collective-permute-start | bytes 61448 | tf_op jit(solution)/shard_map/ppermute | solution.py:200
  8.1 6.6 %copy-start.4 = (f32[10,16,512]{2,1,0:T(8,128)S(1)}, f32[10,16,512]{2,1,0:T(8,128)}, u32[]{:S(2)}) copy-start(f32[10,16,512]{2,1,0:T(8,128)} %inflow_ref.1) | copy-start | bytes 983044
  8.1 4.0 %collective-permute-start.3 = (f32[10,512]{1,0:T(8,128)S(1)}, f32[10,512]{1,0:T(8,128)S(1)}, u32[]{:S(2)}, u32[]{:S(2)}) collective-permute-start(f32[10,512]{1,0:T(8,128)S(1)} %add.40), channel_id=1, source_target_pairs={{0,2},{1,3},{2,0},{3,1},{4,6},{5,7},{6,4},{7,5},{8,10},{9,11},{10,... | collective-permute-start | bytes 61448 | tf_op jit(solution)/shard_map/ppermute | solution.py:200
  12.1 5.1 %collective-permute-start.4 = (f32[10,512]{1,0:T(8,128)S(1)}, f32[10,512]{1,0:T(8,128)S(1)}, u32[]{:S(2)}, u32[]{:S(2)}) collective-permute-start(f32[10,512]{1,0:T(8,128)S(1)} %add.42), channel_id=1, source_target_pairs={{0,4},{1,5},{2,6},{3,7},{4,0},{5,1},{6,2},{7,3},{8,12},{9,13},{10,... | collective-permute-start | bytes 61448 | tf_op jit(solution)/shard_map/ppermute | solution.py:200
  14.8 4.8 %collective-permute-start.1 = (f32[50,512]{1,0:T(8,128)S(1)}, f32[50,512]{1,0:T(8,128)S(1)}, u32[]{:S(2)}, u32[]{:S(2)}) collective-permute-start(f32[50,512]{1,0:T(8,128)S(1)} %get-tuple-element.36), channel_id=1, source_target_pairs={{0,7},{1,0},{2,1},{3,2},{4,3},{5,4},{6,5},{7,6},{8,15},{9,8},{10,9... | collective-permute-start | bytes 307208 | tf_op jit(solution)/shard_map/ppermute | solution.py:196
  17.2 1.7 %collective-permute-start.5 = (f32[10,512]{1,0:T(8,128)S(1)}, f32[10,512]{1,0:T(8,128)S(1)}, u32[]{:S(2)}, u32[]{:S(2)}) collective-permute-start(f32[10,512]{1,0:T(8,128)S(1)} %select_add_fusion.1.own_ref), channel_id=1, source_target_pairs={{0,24},{8,0},{16,8},{24,16},{1,25},{9,1},{17,9},{25,17},{2,26},{10... | collective-permute-start | bytes 61448 | tf_op jit(solution)/shard_map/ppermute | solution.py:196
  20.1 1.3 %collective-permute-start.7 = (f32[16,512]{1,0:T(8,128)S(1)}, f32[16,512]{1,0:T(8,128)S(1)}, u32[]{:S(2)}, u32[]{:S(2)}) collective-permute-start(f32[16,512]{1,0:T(8,128)S(1)} %get-tuple-element.46), channel_id=1, source_target_pairs={{0,8},{8,0},{16,24},{24,16},{1,9},{9,1},{17,25},{25,17},{2,10},{10... | collective-permute-start | bytes 98312 | tf_op jit(solution)/shard_map/ppermute | solution.py:200
  20.3 3.3 %collective-permute-start.6 = (f32[10,512]{1,0:T(8,128)S(1)}, f32[10,512]{1,0:T(8,128)S(1)}, u32[]{:S(2)}, u32[]{:S(2)}) collective-permute-start(f32[10,512]{1,0:T(8,128)S(1)} %slice.12), channel_id=1, source_target_pairs={{0,8},{8,16},{16,24},{24,0},{1,9},{9,17},{17,25},{25,1},{2,10},{10... | collective-permute-start | bytes 61448 | tf_op jit(solution)/shard_map/ppermute | solution.py:196
  21.5 4.6 %collective-permute-start.9 = (f32[66,512]{1,0:T(8,128)S(1)}, f32[66,512]{1,0:T(8,128)S(1)}, u32[]{:S(2)}, u32[]{:S(2)}) collective-permute-start(f32[66,512]{1,0:T(8,128)S(1)} %pad_maximum_fusion), channel_id=1, source_target_pairs={{0,8},{8,16},{16,24},{24,0},{1,9},{9,17},{17,25},{25,1},{2,10},{10... | collective-permute-start | bytes 405512 | tf_op jit(solution)/shard_map/ppermute | solution.py:196
  23.6 4.3 %collective-permute-start.8 = (f32[10,512]{1,0:T(8,128)S(1)}, f32[10,512]{1,0:T(8,128)S(1)}, u32[]{:S(2)}, u32[]{:S(2)}) collective-permute-start(f32[10,512]{1,0:T(8,128)S(1)} %slice_add_fusion.2), channel_id=1, source_target_pairs={{0,1},{1,0},{2,3},{3,2},{4,5},{5,4},{6,7},{7,6},{8,9},{9,8},{10,11... | collective-permute-start | bytes 61448 | tf_op jit(solution)/shard_map/ppermute | solution.py:200
  26.0 6.5 %collective-permute-start.11 = (f32[160,512]{1,0:T(8,128)S(1)}, f32[160,512]{1,0:T(8,128)S(1)}, u32[]{:S(2)}, u32[]{:S(2)}) collective-permute-start(f32[160,512]{1,0:T(8,128)S(1)} %get-tuple-element.52), channel_id=1, source_target_pairs={{0,8},{8,16},{16,24},{24,0},{1,9},{9,17},{17,25},{25,1},{2,10},{10... | collective-permute-start | bytes 983048 | tf_op jit(solution)/shard_map/ppermute | solution.py:196
  26.1 8.6 %collective-permute-start.14 = (f32[16,512]{1,0:T(8,128)S(1)}, f32[16,512]{1,0:T(8,128)S(1)}, u32[]{:S(2)}, u32[]{:S(2)}) collective-permute-start(f32[16,512]{1,0:T(8,128)S(1)} %slice_add_fusion.1), channel_id=1, source_target_pairs={{0,8},{8,0},{16,24},{24,16},{1,9},{9,1},{17,25},{25,17},{2,10},{10... | collective-permute-start | bytes 98312 | tf_op jit(solution)/shard_map/ppermute | solution.py:200
  27.9 3.9 %collective-permute-start.10 = (f32[10,512]{1,0:T(8,128)S(1)}, f32[10,512]{1,0:T(8,128)S(1)}, u32[]{:S(2)}, u32[]{:S(2)}) collective-permute-start(f32[10,512]{1,0:T(8,128)S(1)} %add.47), channel_id=1, source_target_pairs={{0,2},{1,3},{2,0},{3,1},{4,6},{5,7},{6,4},{7,5},{8,10},{9,11},{10,... | collective-permute-start | bytes 61448 | tf_op jit(solution)/shard_map/ppermute | solution.py:200
  29.5 7.8 %collective-permute-start.13 = (f32[50,512]{1,0:T(8,128)S(1)}, f32[50,512]{1,0:T(8,128)S(1)}, u32[]{:S(2)}, u32[]{:S(2)}) collective-permute-start(f32[50,512]{1,0:T(8,128)S(1)} %slice_add_fusion), channel_id=1, source_target_pairs={{0,1},{1,2},{2,3},{3,4},{4,5},{5,6},{6,7},{7,0},{8,9},{9,10},{10,1... | collective-permute-start | bytes 307208 | tf_op jit(solution)/shard_map/ppermute | solution.py:196
  32.5 4.8 %collective-permute-start.12 = (f32[10,512]{1,0:T(8,128)S(1)}, f32[10,512]{1,0:T(8,128)S(1)}, u32[]{:S(2)}, u32[]{:S(2)}) collective-permute-start(f32[10,512]{1,0:T(8,128)S(1)} %add.48), channel_id=1, source_target_pairs={{0,4},{1,5},{2,6},{3,7},{4,0},{5,1},{6,2},{7,3},{8,12},{9,13},{10,... | collective-permute-start | bytes 61448 | tf_op jit(solution)/shard_map/ppermute | solution.py:200
  (5 other events, 11.0 us)

commit v6 on v5

--- a/solution.py
+++ b/solution.py
@@ -274,7 +274,7 @@
         [(2 * count + 1, hours, lanes)],
     )
     w = passed_along(w_sent, "hours", -1)
-    off_own = offsets(total, "hours", True, [(base, rows), (lead, w_sent), (stock,)])
+    off_own = offsets(total, "hours", True, [(base, rows), (lead, w_sent, stock), (stock,)])
     off_next = passed_along(off_own, "river", -1)
 
     new, extra, rim_mine, rim_theirs, tots, power = call(
@@ -299,7 +299,7 @@
         whole = power + moved[count * EDGE :]
     else:
         late = rim_mine + passed_along(rim_theirs, "river", 1)
-    tot_came, theirs, mine, power = lax.optimization_barrier((tot_came, theirs, mine, power))
+    tot_came, theirs, power = lax.optimization_barrier((tot_came, theirs, power))
     came = passed_along(theirs, "river", 1)
     edge = passed_along(late, "hours", 1)
     place, steps = lax.axis_index("hours"), (lax.axis_size("hours") - 1).bit_length()

time: 38.5 us -> 38.4 us (level)
  no operation moved by 1% of the time
where the time goes in v6:
time: 38.4 us; the launch traced here: 38.2 us
  starting transfers between devices  21 us (55%)
  waiting for transfers between devices  12.3 us (32%)
  Pallas kernels  2.84 us (7%)
  local copies, waits for them, and re-layouts  1.04 us (3%)
  between operations  0.89 us (2%)
    ppermute x8, starting transfers between devices, swapped(): lax.ppermute(block, axis, [(i, i ^ bit) for i in range(lax.axis_size(axis...  12.8 us
    ppermute x7, starting transfers between devices, passed_along(): lax.ppermute(block, axis, [(i, (i + distance) % count) for i in range(cou...  8.21 us
    ppermute x7, waiting for transfers between devices, passed_along(): lax.ppermute(block, axis, [(i, (i + distance) % count) for i in range(cou...  6.91 us
    ppermute x8, waiting for transfers between devices, swapped(): lax.ppermute(block, axis, [(i, i ^ bit) for i in range(lax.axis_size(axis...  5.42 us
    pallas_call x8, Pallas kernels, call(): pl.pallas_call(body, out_shape=[jax.ShapeDtypeStruct(shape, jnp.float32)...  2.84 us
    unnamed x28, local copies, waits for them, and re-layouts  1.03 us
  transfers between devices with their start and end apart: 15, of which 10 were waited for; matrix products, arithmetic and copies ran while one was open for 0% of the time, Pallas kernels for 3%

profile of v6, /device:TPU:0, one launch (start us, length us, event | category | flops | bytes accessed | tf_op | source)
XLA Modules:
  0.0 38.2 jit_solution(13656186446834121451)
XLA Ops:
  0.6 1.0 %copy-done = f32[10,16,512]{2,1,0:T(8,128)S(1)} copy-done((f32[10,16,512]{2,1,0:T(8,128)S(1)}, f32[10,16,512]{2,1,0:T(8,128)}, u32[]{:S(2)}) %copy-start) | copy-done | bytes 327704
  1.8 2.4 %collective-permute-start = (f32[10,16,512]{2,1,0:T(8,128)S(1)}, f32[10,16,512]{2,1,0:T(8,128)S(1)}, u32[]{:S(2)}, u32[]{:S(2)}) collective-permute-start(f32[10,16,512]{2,1,0:T(8,128)S(1)} %shard_map.158), channel_id=1, source_target_pairs={{0,24},{8,0},{16,8},{24,16},{1,25},{9,1},{17,9},{25,17},{2,26},{10... | collective-permute-start | bytes 983048 | tf_op jit(solution)/shard_map/ppermute | solution.py:196
  4.2 1.5 %collective-permute-start.2 = (f32[10,512]{1,0:T(8,128)S(1)}, f32[10,512]{1,0:T(8,128)S(1)}, u32[]{:S(2)}, u32[]{:S(2)}) collective-permute-start(f32[10,512]{1,0:T(8,128)S(1)} %shard_map.157), channel_id=1, source_target_pairs={{0,1},{1,0},{2,3},{3,2},{4,5},{5,4},{6,7},{7,6},{8,9},{9,8},{10,11... | collective-permute-start | bytes 61448 | tf_op jit(solution)/shard_map/ppermute | solution.py:200
  5.9 2.2 %collective-permute-done.2 = f32[10,512]{1,0:T(8,128)S(1)} collective-permute-done((f32[10,512]{1,0:T(8,128)S(1)}, f32[10,512]{1,0:T(8,128)S(1)}, u32[]{:S(2)}, u32[]{:S(2)}) %collective-permute-start.2) | collective-permute-done | bytes 20512 | tf_op jit(solution)/shard_map/ppermute | solution.py:200
  8.1 1.6 %collective-permute-start.3 = (f32[10,512]{1,0:T(8,128)S(1)}, f32[10,512]{1,0:T(8,128)S(1)}, u32[]{:S(2)}, u32[]{:S(2)}) collective-permute-start(f32[10,512]{1,0:T(8,128)S(1)} %add.40), channel_id=1, source_target_pairs={{0,2},{1,3},{2,0},{3,1},{4,6},{5,7},{6,4},{7,5},{8,10},{9,11},{10,... | collective-permute-start | bytes 61448 | tf_op jit(solution)/shard_map/ppermute | solution.py:200
  10.3 1.9 %collective-permute-done.3 = f32[10,512]{1,0:T(8,128)S(1)} collective-permute-done((f32[10,512]{1,0:T(8,128)S(1)}, f32[10,512]{1,0:T(8,128)S(1)}, u32[]{:S(2)}, u32[]{:S(2)}) %collective-permute-start.3) | collective-permute-done | bytes 20512 | tf_op jit(solution)/shard_map/ppermute | solution.py:200
  12.1 2.6 %collective-permute-start.4 = (f32[10,512]{1,0:T(8,128)S(1)}, f32[10,512]{1,0:T(8,128)S(1)}, u32[]{:S(2)}, u32[]{:S(2)}) collective-permute-start(f32[10,512]{1,0:T(8,128)S(1)} %add.42), channel_id=1, source_target_pairs={{0,4},{1,5},{2,6},{3,7},{4,0},{5,1},{6,2},{7,3},{8,12},{9,13},{10,... | collective-permute-start | bytes 61448 | tf_op jit(solution)/shard_map/ppermute | solution.py:200
  14.7 2.3 %collective-permute-start.1 = (f32[50,512]{1,0:T(8,128)S(1)}, f32[50,512]{1,0:T(8,128)S(1)}, u32[]{:S(2)}, u32[]{:S(2)}) collective-permute-start(f32[50,512]{1,0:T(8,128)S(1)} %get-tuple-element.35), channel_id=1, source_target_pairs={{0,7},{1,0},{2,1},{3,2},{4,3},{5,4},{6,5},{7,6},{8,15},{9,8},{10,9... | collective-permute-start | bytes 307208 | tf_op jit(solution)/shard_map/ppermute | solution.py:196
  17.1 1.6 %collective-permute-done.5.next_ref = f32[10,512]{1,0:T(8,128)S(1)} collective-permute-done((f32[10,512]{1,0:T(8,128)S(1)}, f32[10,512]{1,0:T(8,128)S(1)}, u32[]{:S(2)}, u32[]{:S(2)}) %collective-permute-start.5) | collective-permute-done | bytes 20512 | tf_op jit(solution)/shard_map/ppermute | solution.py:196
  18.7 0.8 %collective-permute-done.1.w_ref = f32[50,512]{1,0:T(8,128)S(1)} collective-permute-done((f32[50,512]{1,0:T(8,128)S(1)}, f32[50,512]{1,0:T(8,128)S(1)}, u32[]{:S(2)}, u32[]{:S(2)}) %collective-permute-start.1) | collective-permute-done | bytes 102432 | tf_op jit(solution)/shard_map/ppermute | solution.py:196
  19.5 0.4 %shard_map.161 = (f32[10,16,512]{2,1,0:T(8,128)S(1)}, f32[10,16,512]{2,1,0:T(8,128)S(1)}, f32[50,512]{1,0:T(8,128)S(1)}, f32[50,512]{1,0:T(8,128)S(1)}, f32[20,512]{1,0:T(8,128)S(1)}, /*index=5*/f32[16,512]{1,0:T(8,128)S(1)}) custom-call(s32[10]{0:T(128)S(1)} %copy-done.7, s32[10]{0:T(128)S(1)} %copy-done.8, f32[50,512]{1,0:T(8,128)S(1)} %get-tuple-element.31.rows_ref, ...), custom_call_target="tpu_custom_call" | custom-call | tf_op jit(solution)/shard_map/pallas_call | solution.py:228
  20.1 0.4 %collective-permute-start.6 = (f32[10,512]{1,0:T(8,128)S(1)}, f32[10,512]{1,0:T(8,128)S(1)}, u32[]{:S(2)}, u32[]{:S(2)}) collective-permute-start(f32[10,512]{1,0:T(8,128)S(1)} %slice.13), channel_id=1, source_target_pairs={{0,8},{8,16},{16,24},{24,0},{1,9},{9,17},{17,25},{25,1},{2,10},{10... | collective-permute-start | bytes 61448 | tf_op jit(solution)/shard_map/ppermute | solution.py:196
  20.5 0.7 %shard_map.162 = (f32[10,16,512]{2,1,0:T(8,128)}, f32[160,512]{1,0:T(8,128)S(1)}, f32[160,512]{1,0:T(8,128)S(1)}) custom-call(s32[10]{0:T(128)S(1)} %copy-done.7, s32[10]{0:T(128)S(1)} %copy-done.8, f32[10,16,512]{2,1,0:T(8,128)S(1)} %get-tuple-element.39.extra_ref, f32[10,16,512]{2,1,0:T(8,128)S(1)} %shard_map.160.stock_ref, ...), custom_call_target="tpu_custom_call" | custom-call | tf_op jit(solution)/shard_map/pallas_call | solution.py:228
  21.3 1.0 %collective-permute-start.9 = (f32[66,512]{1,0:T(8,128)S(1)}, f32[66,512]{1,0:T(8,128)S(1)}, u32[]{:S(2)}, u32[]{:S(2)}) collective-permute-start(f32[66,512]{1,0:T(8,128)S(1)} %pad_maximum_fusion), channel_id=1, source_target_pairs={{0,8},{8,16},{16,24},{24,0},{1,9},{9,17},{17,25},{25,1},{2,10},{10... | collective-permute-start | bytes 405512 | tf_op jit(solution)/shard_map/ppermute | solution.py:196
  22.3 1.1 %collective-permute-done.6 = f32[10,512]{1,0:T(8,128)S(1)} collective-permute-done((f32[10,512]{1,0:T(8,128)S(1)}, f32[10,512]{1,0:T(8,128)S(1)}, u32[]{:S(2)}, u32[]{:S(2)}) %collective-permute-start.6) | collective-permute-done | bytes 20512 | tf_op jit(solution)/shard_map/ppermute | solution.py:196
  23.5 2.4 %collective-permute-start.8 = (f32[10,512]{1,0:T(8,128)S(1)}, f32[10,512]{1,0:T(8,128)S(1)}, u32[]{:S(2)}, u32[]{:S(2)}) collective-permute-start(f32[10,512]{1,0:T(8,128)S(1)} %slice_add_fusion.2), channel_id=1, source_target_pairs={{0,1},{1,0},{2,3},{3,2},{4,5},{5,4},{6,7},{7,6},{8,9},{9,8},{10,11... | collective-permute-start | bytes 61448 | tf_op jit(solution)/shard_map/ppermute | solution.py:200
  25.9 0.7 %collective-permute-start.14 = (f32[16,512]{1,0:T(8,128)S(1)}, f32[16,512]{1,0:T(8,128)S(1)}, u32[]{:S(2)}, u32[]{:S(2)}) collective-permute-start(f32[16,512]{1,0:T(8,128)S(1)} %slice_add_fusion.1), channel_id=1, source_target_pairs={{0,8},{8,0},{16,24},{24,16},{1,9},{9,1},{17,25},{25,17},{2,10},{10... | collective-permute-start | bytes 98312 | tf_op jit(solution)/shard_map/ppermute | solution.py:200
  26.7 1.0 %collective-permute-done.8 = f32[10,512]{1,0:T(8,128)S(1)} collective-permute-done((f32[10,512]{1,0:T(8,128)S(1)}, f32[10,512]{1,0:T(8,128)S(1)}, u32[]{:S(2)}, u32[]{:S(2)}) %collective-permute-start.8) | collective-permute-done | bytes 20512 | tf_op jit(solution)/shard_map/ppermute | solution.py:200
  27.7 1.6 %collective-permute-start.10 = (f32[10,512]{1,0:T(8,128)S(1)}, f32[10,512]{1,0:T(8,128)S(1)}, u32[]{:S(2)}, u32[]{:S(2)}) collective-permute-start(f32[10,512]{1,0:T(8,128)S(1)} %add.47), channel_id=1, source_target_pairs={{0,2},{1,3},{2,0},{3,1},{4,6},{5,7},{6,4},{7,5},{8,10},{9,11},{10,... | collective-permute-start | bytes 61448 | tf_op jit(solution)/shard_map/ppermute | solution.py:200
  29.3 2.0 %collective-permute-start.13 = (f32[50,512]{1,0:T(8,128)S(1)}, f32[50,512]{1,0:T(8,128)S(1)}, u32[]{:S(2)}, u32[]{:S(2)}) collective-permute-start(f32[50,512]{1,0:T(8,128)S(1)} %slice_add_fusion), channel_id=1, source_target_pairs={{0,1},{1,2},{2,3},{3,4},{4,5},{5,6},{6,7},{7,0},{8,9},{9,10},{10,1... | collective-permute-start | bytes 307208 | tf_op jit(solution)/shard_map/ppermute | solution.py:196
  31.6 0.7 %collective-permute-done.11.came_ref = f32[160,512]{1,0:T(8,128)S(1)} collective-permute-done((f32[160,512]{1,0:T(8,128)S(1)}, f32[160,512]{1,0:T(8,128)S(1)}, u32[]{:S(2)}, u32[]{:S(2)}) %collective-permute-start.11) | collective-permute-done | bytes 327712 | tf_op jit(solution)/shard_map/ppermute | solution.py:196
  32.3 2.2 %collective-permute-start.12 = (f32[10,512]{1,0:T(8,128)S(1)}, f32[10,512]{1,0:T(8,128)S(1)}, u32[]{:S(2)}, u32[]{:S(2)}) collective-permute-start(f32[10,512]{1,0:T(8,128)S(1)} %add.48), channel_id=1, source_target_pairs={{0,4},{1,5},{2,6},{3,7},{4,0},{5,1},{6,2},{7,3},{8,12},{9,13},{10,... | collective-permute-start | bytes 61448 | tf_op jit(solution)/shard_map/ppermute | solution.py:200
  34.5 2.6 %collective-permute-done.13.rim_ref = f32[50,512]{1,0:T(8,128)S(1)} collective-permute-done((f32[50,512]{1,0:T(8,128)S(1)}, f32[50,512]{1,0:T(8,128)S(1)}, u32[]{:S(2)}, u32[]{:S(2)}) %collective-permute-start.13) | collective-permute-done | bytes 102432 | tf_op jit(solution)/shard_map/ppermute | solution.py:196
  37.2 1.0 %shard_map.163 = (f32[10,16,512]{2,1,0:T(8,128)}, f32[10,16,512]{2,1,0:T(8,128)}, f32[16,512]{1,0:T(8,128)}) custom-call(f32[50,512]{1,0:T(8,128)S(1)} %get-tuple-element.31.rows_ref, f32[160,512]{1,0:T(8,128)S(1)} %get-tuple-element.42.mine_ref, f32[160,512]{1,0:T(8,128)S(1)} %collective-permute-done.11.came_ref, ...), custom_call_target="tpu_custom_call" | custom-call | tf_op jit(solution)/shard_map/pallas_call | solution.py:228
  (55 shorter events, 1.5 us)
Async XLA Ops:
  1.6 4.1 %copy-start.5 = (f32[16,512]{1,0:T(8,128)S(1)}, f32[16,512]{1,0:T(8,128)}, u32[]{:S(2)}) copy-start(f32[16,512]{1,0:T(8,128)} %dual_ref.3) | copy-start | bytes 98308
  1.6 4.1 %copy-start.9 = (f32[10]{0:T(128)S(1)}, f32[10]{0:T(128)}, u32[]{:S(2)}) copy-start(f32[10]{0:T(128)} %eff_ref.1) | copy-start | bytes 124
  1.6 4.1 %copy-start.10 = (f32[10]{0:T(128)S(1)}, f32[10]{0:T(128)}, u32[]{:S(2)}) copy-start(f32[10]{0:T(128)} %cap_ref.1) | copy-start | bytes 124
  1.6 4.1 %copy-start.11 = (f32[10]{0:T(128)S(1)}, f32[10]{0:T(128)}, u32[]{:S(2)}) copy-start(f32[10]{0:T(128)} %start_ref.1) | copy-start | bytes 124
  1.6 4.1 %copy-start.12 = (f32[10]{0:T(128)S(1)}, f32[10]{0:T(128)}, u32[]{:S(2)}) copy-start(f32[10]{0:T(128)} %low_ref.1) | copy-start | bytes 124
  1.6 4.1 %copy-start.13 = (f32[10]{0:T(128)S(1)}, f32[10]{0:T(128)}, u32[]{:S(2)}) copy-start(f32[10]{0:T(128)} %high_ref.1) | copy-start | bytes 124
  1.7 4.1 %copy-start.2 = (f32[10,16,512]{2,1,0:T(8,128)S(1)}, f32[10,16,512]{2,1,0:T(8,128)}, u32[]{:S(2)}) copy-start(f32[10,16,512]{2,1,0:T(8,128)} %rel_ref.3) | copy-start | bytes 983044
  1.7 4.0 %copy-start.3 = (f32[10,16,512]{2,1,0:T(8,128)S(1)}, f32[10,16,512]{2,1,0:T(8,128)}, u32[]{:S(2)}) copy-start(f32[10,16,512]{2,1,0:T(8,128)} %cost_ref.1) | copy-start | bytes 983044
  1.8 8.0 %copy-start.4 = (f32[10,16,512]{2,1,0:T(8,128)S(1)}, f32[10,16,512]{2,1,0:T(8,128)}, u32[]{:S(2)}) copy-start(f32[10,16,512]{2,1,0:T(8,128)} %inflow_ref.1) | copy-start | bytes 983044
  1.8 8.1 %collective-permute-start = (f32[10,16,512]{2,1,0:T(8,128)S(1)}, f32[10,16,512]{2,1,0:T(8,128)S(1)}, u32[]{:S(2)}, u32[]{:S(2)}) collective-permute-start(f32[10,16,512]{2,1,0:T(8,128)S(1)} %shard_map.158), channel_id=1, source_target_pairs={{0,24},{8,0},{16,8},{24,16},{1,25},{9,1},{17,9},{25,17},{2,26},{10... | collective-permute-start | bytes 983048 | tf_op jit(solution)/shard_map/ppermute | solution.py:196
  4.2 3.9 %collective-permute-start.2 = (f32[10,512]{1,0:T(8,128)S(1)}, f32[10,512]{1,0:T(8,128)S(1)}, u32[]{:S(2)}, u32[]{:S(2)}) collective-permute-start(f32[10,512]{1,0:T(8,128)S(1)} %shard_map.157), channel_id=1, source_target_pairs={{0,1},{1,0},{2,3},{3,2},{4,5},{5,4},{6,7},{7,6},{8,9},{9,8},{10,11... | collective-permute-start | bytes 61448 | tf_op jit(solution)/shard_map/ppermute | solution.py:200
  8.1 4.0 %collective-permute-start.3 = (f32[10,512]{1,0:T(8,128)S(1)}, f32[10,512]{1,0:T(8,128)S(1)}, u32[]{:S(2)}, u32[]{:S(2)}) collective-permute-start(f32[10,512]{1,0:T(8,128)S(1)} %add.40), channel_id=1, source_target_pairs={{0,2},{1,3},{2,0},{3,1},{4,6},{5,7},{6,4},{7,5},{8,10},{9,11},{10,... | collective-permute-start | bytes 61448 | tf_op jit(solution)/shard_map/ppermute | solution.py:200
  12.1 4.9 %collective-permute-start.4 = (f32[10,512]{1,0:T(8,128)S(1)}, f32[10,512]{1,0:T(8,128)S(1)}, u32[]{:S(2)}, u32[]{:S(2)}) collective-permute-start(f32[10,512]{1,0:T(8,128)S(1)} %add.42), channel_id=1, source_target_pairs={{0,4},{1,5},{2,6},{3,7},{4,0},{5,1},{6,2},{7,3},{8,12},{9,13},{10,... | collective-permute-start | bytes 61448 | tf_op jit(solution)/shard_map/ppermute | solution.py:200
  14.7 4.8 %collective-permute-start.1 = (f32[50,512]{1,0:T(8,128)S(1)}, f32[50,512]{1,0:T(8,128)S(1)}, u32[]{:S(2)}, u32[]{:S(2)}) collective-permute-start(f32[50,512]{1,0:T(8,128)S(1)} %get-tuple-element.35), channel_id=1, source_target_pairs={{0,7},{1,0},{2,1},{3,2},{4,3},{5,4},{6,5},{7,6},{8,15},{9,8},{10,9... | collective-permute-start | bytes 307208 | tf_op jit(solution)/shard_map/ppermute | solution.py:196
  17.1 1.7 %collective-permute-start.5 = (f32[10,512]{1,0:T(8,128)S(1)}, f32[10,512]{1,0:T(8,128)S(1)}, u32[]{:S(2)}, u32[]{:S(2)}) collective-permute-start(f32[10,512]{1,0:T(8,128)S(1)} %select_add_fusion.1.own_ref), channel_id=1, source_target_pairs={{0,24},{8,0},{16,8},{24,16},{1,25},{9,1},{17,9},{25,17},{2,26},{10... | collective-permute-start | bytes 61448 | tf_op jit(solution)/shard_map/ppermute | solution.py:196
  19.9 1.3 %collective-permute-start.7 = (f32[16,512]{1,0:T(8,128)S(1)}, f32[16,512]{1,0:T(8,128)S(1)}, u32[]{:S(2)}, u32[]{:S(2)}) collective-permute-start(f32[16,512]{1,0:T(8,128)S(1)} %get-tuple-element.45), channel_id=1, source_target_pairs={{0,8},{8,0},{16,24},{24,16},{1,9},{9,1},{17,25},{25,17},{2,10},{10... | collective-permute-start | bytes 98312 | tf_op jit(solution)/shard_map/ppermute | solution.py:200
  20.1 3.3 %collective-permute-start.6 = (f32[10,512]{1,0:T(8,128)S(1)}, f32[10,512]{1,0:T(8,128)S(1)}, u32[]{:S(2)}, u32[]{:S(2)}) collective-permute-start(f32[10,512]{1,0:T(8,128)S(1)} %slice.13), channel_id=1, source_target_pairs={{0,8},{8,16},{16,24},{24,0},{1,9},{9,17},{17,25},{25,1},{2,10},{10... | collective-permute-start | bytes 61448 | tf_op jit(solution)/shard_map/ppermute | solution.py:196
  21.3 4.6 %collective-permute-start.9 = (f32[66,512]{1,0:T(8,128)S(1)}, f32[66,512]{1,0:T(8,128)S(1)}, u32[]{:S(2)}, u32[]{:S(2)}) collective-permute-start(f32[66,512]{1,0:T(8,128)S(1)} %pad_maximum_fusion), channel_id=1, source_target_pairs={{0,8},{8,16},{16,24},{24,0},{1,9},{9,17},{17,25},{25,1},{2,10},{10... | collective-permute-start | bytes 405512 | tf_op jit(solution)/shard_map/ppermute | solution.py:196
  23.5 4.3 %collective-permute-start.8 = (f32[10,512]{1,0:T(8,128)S(1)}, f32[10,512]{1,0:T(8,128)S(1)}, u32[]{:S(2)}, u32[]{:S(2)}) collective-permute-start(f32[10,512]{1,0:T(8,128)S(1)} %slice_add_fusion.2), channel_id=1, source_target_pairs={{0,1},{1,0},{2,3},{3,2},{4,5},{5,4},{6,7},{7,6},{8,9},{9,8},{10,11... | collective-permute-start | bytes 61448 | tf_op jit(solution)/shard_map/ppermute | solution.py:200
  25.8 6.5 %collective-permute-start.11 = (f32[160,512]{1,0:T(8,128)S(1)}, f32[160,512]{1,0:T(8,128)S(1)}, u32[]{:S(2)}, u32[]{:S(2)}) collective-permute-start(f32[160,512]{1,0:T(8,128)S(1)} %get-tuple-element.50), channel_id=1, source_target_pairs={{0,8},{8,16},{16,24},{24,0},{1,9},{9,17},{17,25},{25,1},{2,10},{10... | collective-permute-start | bytes 983048 | tf_op jit(solution)/shard_map/ppermute | solution.py:196
  25.9 8.6 %collective-permute-start.14 = (f32[16,512]{1,0:T(8,128)S(1)}, f32[16,512]{1,0:T(8,128)S(1)}, u32[]{:S(2)}, u32[]{:S(2)}) collective-permute-start(f32[16,512]{1,0:T(8,128)S(1)} %slice_add_fusion.1), channel_id=1, source_target_pairs={{0,8},{8,0},{16,24},{24,16},{1,9},{9,1},{17,25},{25,17},{2,10},{10... | collective-permute-start | bytes 98312 | tf_op jit(solution)/shard_map/ppermute | solution.py:200
  27.7 3.9 %collective-permute-start.10 = (f32[10,512]{1,0:T(8,128)S(1)}, f32[10,512]{1,0:T(8,128)S(1)}, u32[]{:S(2)}, u32[]{:S(2)}) collective-permute-start(f32[10,512]{1,0:T(8,128)S(1)} %add.47), channel_id=1, source_target_pairs={{0,2},{1,3},{2,0},{3,1},{4,6},{5,7},{6,4},{7,5},{8,10},{9,11},{10,... | collective-permute-start | bytes 61448 | tf_op jit(solution)/shard_map/ppermute | solution.py:200
  29.3 7.8 %collective-permute-start.13 = (f32[50,512]{1,0:T(8,128)S(1)}, f32[50,512]{1,0:T(8,128)S(1)}, u32[]{:S(2)}, u32[]{:S(2)}) collective-permute-start(f32[50,512]{1,0:T(8,128)S(1)} %slice_add_fusion), channel_id=1, source_target_pairs={{0,1},{1,2},{2,3},{3,4},{4,5},{5,6},{6,7},{7,0},{8,9},{9,10},{10,1... | collective-permute-start | bytes 307208 | tf_op jit(solution)/shard_map/ppermute | solution.py:196
  32.3 4.8 %collective-permute-start.12 = (f32[10,512]{1,0:T(8,128)S(1)}, f32[10,512]{1,0:T(8,128)S(1)}, u32[]{:S(2)}, u32[]{:S(2)}) collective-permute-start(f32[10,512]{1,0:T(8,128)S(1)} %add.48), channel_id=1, source_target_pairs={{0,4},{1,5},{2,6},{3,7},{4,0},{5,1},{6,2},{7,3},{8,12},{9,13},{10,... | collective-permute-start | bytes 61448 | tf_op jit(solution)/shard_map/ppermute | solution.py:200
  (5 other events, 9.0 us)
